TPU v7x, 32 devices: a whole 2x2x4 slice. The times are simulated.
32 devices in a mesh: grp: 4 (over x, core), row: 2 (over y), col: 4 (over z).
Axes of the slice: x: 2, y: 2, z: 4, core: 2. Of those that a mesh axis runs over, the one named last changes fastest.
Arguments:
- tokens: bfloat16 [9216, 2048], P(('grp', 'col'), 'row'), may hold values from -6 to 6
- gain: bfloat16 [2048], P(('row', 'grp')), may hold values from 0.5 to 1.5
- in_proj: bfloat16 [2048, 2, 4096], P('row', None, ('col', 'grp')), may hold values from -0.125 to 0.125
- conv_weight: bfloat16 [4, 4096], P(None, ('col', 'row', 'grp')), may hold values from -3 to 3
- conv_bias: bfloat16 [4096], P(('col', 'row', 'grp')), may hold values from -1.5 to 1.5
- x_proj: bfloat16 [4096, 160], P(('col', 'row', 'grp')), may hold values from -0.09375 to 0.09375
- dt_proj: bfloat16 [128, 4096], P(None, ('col', 'row', 'grp')), may hold values from -0.5 to 0.5
- dt_bias: bfloat16 [4096], P(('col', 'row', 'grp')), may hold values from -6 to -2.5
- a_log: bfloat16 [16, 4096], P(None, ('col', 'row', 'grp')), may hold values from 0 to 2.6875
- d_skip: bfloat16 [4096], P(('col', 'row', 'grp')), may hold values from 0.25 to 1.75
- out_proj: bfloat16 [4096, 2048], P('col', ('row', 'grp')), may hold values from -0.1875 to 0.1875
- table: int32 [8], P('grp'), may hold values from 0 to 1
- cotangent: bfloat16 [9216, 2048], P(('grp', 'col'), 'row'), may hold values from -6 to 6
Outputs:
- output: bfloat16 [9216, 2048], P(('grp', 'col'), 'row')
- input_grad: bfloat16 [9216, 2048], P(('grp', 'col'), 'row')
- gain_grad: float32 [2048], P(('row', 'grp'))
- in_proj_grad: float32 [2048, 2, 4096], P('row', None, ('col', 'grp'))
- conv_weight_grad: float32 [4, 4096], P(None, ('col', 'row', 'grp'))
- conv_bias_grad: float32 [4096], P(('col', 'row', 'grp'))
- x_proj_grad: float32 [4096, 160], P(('col', 'row', 'grp'))
- dt_proj_grad: float32 [128, 4096], P(None, ('col', 'row', 'grp'))
- dt_bias_grad: float32 [4096], P(('col', 'row', 'grp'))
- a_log_grad: float32 [16, 4096], P(None, ('col', 'row', 'grp'))
- d_skip_grad: float32 [4096], P(('col', 'row', 'grp'))
- out_proj_grad: float32 [4096, 2048], P('col', ('row', 'grp'))
Inputs may be any that keep to these rules, and one draw needn't show every extreme that they name: `table`: entry k * 2 + j names which of group k's prompts its j-th continuation resumes.
All inputs are finite; a program needn't handle non-finite values.
Results may differ from a plain program's by a relative error of at most 0.011.
Values may be sent and summed in bfloat16 or wider, within the bound.
A program may use at most 320 MiB of HBM per device.

v0:
```python
import jax
import jax.numpy as jnp
from jax import lax
from jax.sharding import PartitionSpec as P

D = 2048
NSTATE = 16
KCONV = 4
RANK = 128
NPROMPT = 2
LP = 1024
LC = 128
NCONT = 2


eps = 1e-05
span_len = 16
highest = lax.Precision.HIGHEST


def time_major(source, blocks):
    shaped = source.reshape((blocks, span_len) + source.shape[1:])
    return jnp.swapaxes(shaped, 0, 1)


def token_major(source):
    swapped = jnp.swapaxes(source, 0, 1)
    return swapped.reshape((-1,) + swapped.shape[2:])


def step_terms(step_size, values, input_map, decay_rate):
    factor = jnp.exp(step_size[:, None, :] * decay_rate[None])
    injected = (step_size * values)[:, None, :] * input_map[:, :, None]
    return (factor, injected)


def block_products(step_steps, decay_rate):
    return jnp.exp(jnp.sum(step_steps, axis=0)[:, None, :] * decay_rate[None])


def forward_chain(products, ends, anchor):

    def forward_link(state, pair):
        return (pair[0] * state + pair[1], state)

    final, starts = lax.scan(
        forward_link, anchor, (jnp.swapaxes(products, 0, 1), jnp.swapaxes(ends, 0, 1))
    )
    return (final, jnp.swapaxes(starts, 0, 1))


def backward_chain(products, local, terminal):

    def backward_link(carried, pair):
        return (pair[1] + pair[0] * carried, carried)

    first, incoming = lax.scan(
        backward_link,
        terminal,
        (jnp.swapaxes(products, 0, 1), jnp.swapaxes(local, 0, 1)),
        reverse=True,
    )
    return (first, jnp.swapaxes(incoming, 0, 1))


def block_entry(step_size, values, input_map, decay_rate, choose):
    blocks = step_size.shape[0] // span_len
    inputs = (
        time_major(step_size, blocks),
        time_major(values, blocks),
        time_major(input_map, blocks),
    )
    shape_tail = (decay_rate.shape[0], step_size.shape[1])

    def block_advance(hidden, step_in):
        factor, injected = step_terms(step_in[0], step_in[1], step_in[2], decay_rate)
        return (factor * hidden + injected, None)

    empty_state = jnp.zeros((blocks,) + shape_tail, jnp.float32)
    ends, ignored = lax.scan(block_advance, empty_state, inputs)
    products = block_products(inputs[0], decay_rate)
    prompt_blocks = NPROMPT * LP // span_len
    finals, prompt_start = forward_chain(
        products[:prompt_blocks].reshape((NPROMPT, -1) + shape_tail),
        ends[:prompt_blocks].reshape((NPROMPT, -1) + shape_tail),
        jnp.zeros((NPROMPT,) + shape_tail, jnp.float32),
    )
    anchor = jnp.einsum("cp,pnw->cnw", choose, finals, precision=highest)
    unused, cont_start = forward_chain(
        products[prompt_blocks:].reshape((NCONT, -1) + shape_tail),
        ends[prompt_blocks:].reshape((NCONT, -1) + shape_tail),
        anchor,
    )
    starts = jnp.concatenate(
        [prompt_start.reshape((-1,) + shape_tail), cont_start.reshape((-1,) + shape_tail)], axis=0
    )
    return (starts, inputs)


def sweep_forward(starts, inputs, read_steps, decay_rate):

    def sweep_advance(hidden, step_in):
        factor, injected = step_terms(step_in[0], step_in[1], step_in[2], decay_rate)
        hidden = factor * hidden + injected
        return (hidden, jnp.sum(hidden * step_in[3][:, :, None], axis=1))

    ignored, results = lax.scan(sweep_advance, starts, inputs + (read_steps,))
    return token_major(results)


def group_grads(starts, step_size, values, input_map, read_map, decay_rate, choose, d_out):
    blocks = starts.shape[0]
    shape_tail = starts.shape[1:]
    inputs = (
        time_major(step_size, blocks),
        time_major(values, blocks),
        time_major(input_map, blocks),
    )
    read_steps = time_major(read_map, blocks)
    grad_steps = time_major(d_out, blocks)

    def group_advance(hidden, step_in):
        factor, injected = step_terms(step_in[0], step_in[1], step_in[2], decay_rate)
        return (factor * hidden + injected, hidden)

    ignored, previous = lax.scan(group_advance, starts, inputs)

    def retreat(carried, step_in):
        step_t, read_t, grad_t = step_in
        factor = jnp.exp(step_t[:, None, :] * decay_rate[None])
        grad_sum = read_t[:, :, None] * grad_t[:, None, :] + carried
        return (factor * grad_sum, None)

    empty_state = jnp.zeros_like(starts)
    local_back, ignored = lax.scan(
        retreat, empty_state, (inputs[0], read_steps, grad_steps), reverse=True
    )
    products = block_products(inputs[0], decay_rate)
    prompt_blocks = NPROMPT * LP // span_len
    cont_first, cont_in = backward_chain(
        products[prompt_blocks:].reshape((NCONT, -1) + shape_tail),
        local_back[prompt_blocks:].reshape((NCONT, -1) + shape_tail),
        jnp.zeros((NCONT,) + shape_tail, jnp.float32),
    )
    into_prompt = jnp.einsum("cp,cnw->pnw", choose, cont_first, precision=highest)
    unused, prompt_in = backward_chain(
        products[:prompt_blocks].reshape((NPROMPT, -1) + shape_tail),
        local_back[:prompt_blocks].reshape((NPROMPT, -1) + shape_tail),
        into_prompt,
    )
    incoming = jnp.concatenate(
        [prompt_in.reshape((-1,) + shape_tail), cont_in.reshape((-1,) + shape_tail)], axis=0
    )

    def descend(carried, step_in):
        step_t, value_t, input_t, read_t, grad_t, prior = step_in
        factor, injected = step_terms(step_t, value_t, input_t, decay_rate)
        grad_sum = read_t[:, :, None] * grad_t[:, None, :] + carried
        weighted = grad_sum * prior * factor
        through_input = jnp.sum(grad_sum * input_t[:, :, None], axis=1)
        d_step = jnp.sum(weighted * decay_rate[None], axis=1) + value_t * through_input
        d_values = step_t * through_input
        d_input = jnp.sum(grad_sum * (step_t * value_t)[:, None, :], axis=2)
        d_read = jnp.sum((factor * prior + injected) * grad_t[:, None, :], axis=2)
        rate_term = jnp.sum(weighted * step_t[:, None, :], axis=0)
        return (factor * grad_sum, (d_step, d_values, d_input, d_read, rate_term))

    ignored, grads = lax.scan(
        descend, incoming, inputs + (read_steps, grad_steps, previous), reverse=True
    )
    return (
        token_major(grads[0]),
        token_major(grads[1]),
        token_major(grads[2]),
        token_major(grads[3]),
        jnp.sum(grads[4], axis=0) * decay_rate,
    )


def scan_grads(starts, step_size, values, input_map, read_map, decay_rate, choose, d_out):
    channels = step_size.shape[1]
    group_width = min(128, channels)
    group_count = channels // group_width

    def by_groups(source):
        return jnp.moveaxis(source.reshape(source.shape[:-1] + (group_count, group_width)), -2, 0)

    def join_groups(source):
        return jnp.moveaxis(source, 0, 1).reshape(source.shape[1], channels)

    def per_group(pieces):
        return group_grads(
            pieces[4], pieces[0], pieces[1], input_map, read_map, pieces[3], choose, pieces[2]
        )

    results = lax.map(
        per_group,
        (
            by_groups(step_size),
            by_groups(values),
            by_groups(d_out),
            by_groups(decay_rate),
            by_groups(starts),
        ),
    )
    return (
        join_groups(results[0]),
        join_groups(results[1]),
        jnp.sum(results[2], axis=0),
        jnp.sum(results[3], axis=0),
        join_groups(results[4]),
    )


def pad_inputs(inner_part, choose, kernel):
    channels = inner_part.shape[1]
    prompts = inner_part[: NPROMPT * LP].reshape(NPROMPT, LP, channels)
    conts = inner_part[NPROMPT * LP :].reshape(NCONT, LC, channels)
    tails = jnp.einsum("cp,pke->cke", choose, prompts[:, LP - kernel + 1 :], precision=highest)
    prompt_pad = jnp.concatenate(
        [jnp.zeros((NPROMPT, kernel - 1, channels), jnp.float32), prompts], axis=1
    )
    return (prompt_pad, jnp.concatenate([tails, conts], axis=1))


def convolve(padded, kernel, shift_bias, length):
    summed = shift_bias
    for offset in range(kernel.shape[0]):
        summed = summed + kernel[offset] * padded[:, offset : offset + length]
    return summed


def convolve_grads(padded, kernel, grad_in, length):
    taps = kernel.shape[0]
    d_padded = jnp.zeros(padded.shape, jnp.float32)
    kernel_rows = []
    for offset in range(taps):
        d_padded = d_padded + jnp.pad(
            kernel[offset] * grad_in, ((0, 0), (offset, taps - 1 - offset), (0, 0))
        )
        kernel_rows.append(jnp.sum(padded[:, offset : offset + length] * grad_in, axis=(0, 1)))
    return (d_padded, jnp.stack(kernel_rows, axis=0))


def per_device(
    tokens,
    gain,
    in_proj,
    conv_weight,
    conv_bias,
    x_proj,
    dt_proj,
    dt_bias,
    a_log,
    d_skip,
    out_proj,
    table,
    cotangent,
):
    (
        gain_block,
        in_block,
        conv_block,
        conv_shift,
        xproj_block,
        dtproj_block,
        bias_block,
        alog_block,
        skip_block,
        out_block,
    ) = (
        lax.all_gather(gain, "grp", axis=0, tiled=True),
        lax.all_gather(in_proj, "grp", axis=2, tiled=True),
        lax.all_gather(conv_weight, "grp", axis=1, tiled=True),
        lax.all_gather(conv_bias, "grp", axis=0, tiled=True),
        lax.all_gather(x_proj, "grp", axis=0, tiled=True),
        lax.all_gather(dt_proj, "grp", axis=1, tiled=True),
        lax.all_gather(dt_bias, "grp", axis=0, tiled=True),
        lax.all_gather(a_log, "grp", axis=1, tiled=True),
        lax.all_gather(d_skip, "grp", axis=0, tiled=True),
        lax.all_gather(out_proj, "grp", axis=1, tiled=True),
    )
    row_count = lax.axis_size("row")
    local_rows = tokens.shape[0]
    whole_rows, whole_cot = (
        lax.all_gather(tokens, "col", axis=0, tiled=True),
        lax.all_gather(cotangent, "col", axis=0, tiled=True),
    )
    total_rows = whole_rows.shape[0]
    gain_wide = gain_block.astype(jnp.float32)
    wide_rows = whole_rows.astype(jnp.float32)
    squares = jnp.sum(wide_rows * wide_rows, axis=1)
    normed = (wide_rows * gain_wide).astype(jnp.bfloat16)
    partial_value = jnp.einsum("td,dke->tke", normed, in_block, preferred_element_type=jnp.float32)
    projected, square_sum = (
        lax.psum_scatter(partial_value, "row", scatter_dimension=2, tiled=True),
        lax.psum_scatter(
            jnp.broadcast_to(squares[:, None], (total_rows, row_count)),
            "row",
            scatter_dimension=1,
            tiled=True,
        ),
    )
    square_total = square_sum[:, 0]
    inv_rms = lax.rsqrt(square_total / D + eps)
    mixed = inv_rms[:, None, None] * projected
    inner_part = mixed[:, 0]
    gate_part = mixed[:, 1]
    channels = inner_part.shape[1]
    choose = (table[:, None] == jnp.arange(NPROMPT)[None, :]).astype(jnp.float32)
    kernel = conv_block.astype(jnp.float32)
    shift_bias = conv_shift.astype(jnp.float32)
    prompt_pad, cont_pad = pad_inputs(inner_part, choose, KCONV)
    conv_out = jnp.concatenate(
        [
            convolve(prompt_pad, kernel, shift_bias, LP).reshape(-1, channels),
            convolve(cont_pad, kernel, shift_bias, LC).reshape(-1, channels),
        ],
        axis=0,
    )
    xconv_low = jax.nn.silu(conv_out).astype(jnp.bfloat16)
    xconv = xconv_low.astype(jnp.float32)
    xdbl = lax.psum(
        jnp.dot(xconv_low, xproj_block, preferred_element_type=jnp.float32), ("row", "col")
    )
    dtlow = xdbl[:, :RANK].astype(jnp.bfloat16)
    input_map = xdbl[:, RANK : RANK + NSTATE]
    read_map = xdbl[:, RANK + NSTATE :]
    step_inner = jnp.dot(
        dtlow, dtproj_block, preferred_element_type=jnp.float32
    ) + bias_block.astype(jnp.float32)
    step_size = jax.nn.softplus(step_inner)
    decay_rate = -jnp.exp(alog_block.astype(jnp.float32))
    starts, inputs = block_entry(step_size, xconv, input_map, decay_rate, choose)
    yscan = sweep_forward(starts, inputs, time_major(read_map, starts.shape[0]), decay_rate)
    skip_wide = skip_block.astype(jnp.float32)
    yfull = yscan + skip_wide * xconv
    gate_sig = jax.nn.sigmoid(gate_part)
    gate_silu = gate_part * gate_sig
    gated = (yfull * gate_silu).astype(jnp.bfloat16)
    gated_full = lax.all_gather(gated, "row", axis=1, tiled=True)
    branch = lax.psum_scatter(
        jnp.dot(gated_full, out_block, preferred_element_type=jnp.float32).astype(jnp.bfloat16),
        "col",
        scatter_dimension=0,
        tiled=True,
    ).astype(jnp.float32)
    local_tokens = tokens.astype(jnp.float32)
    output = (local_tokens + branch).astype(jnp.bfloat16)
    out_grad = jnp.einsum("te,td->ed", gated_full, whole_cot, preferred_element_type=jnp.float32)
    d_gated = lax.psum_scatter(
        jnp.einsum("td,ed->te", whole_cot, out_block, preferred_element_type=jnp.float32),
        "row",
        scatter_dimension=1,
        tiled=True,
    )
    d_yfull = d_gated * gate_silu
    d_gate = d_gated * yfull * gate_sig * (1.0 + gate_part * (1.0 - gate_sig))
    skip_grad = jnp.sum(d_yfull * xconv, axis=0)
    d_step, d_xscan, d_input, d_read, alog_grad = scan_grads(
        starts, step_size, xconv, input_map, read_map, decay_rate, choose, d_yfull
    )
    d_step_inner = d_step * jax.nn.sigmoid(step_inner)
    bias_grad = jnp.sum(d_step_inner, axis=0)
    d_dtin = d_step_inner.astype(jnp.bfloat16)
    dtproj_grad = jnp.einsum("tr,te->re", dtlow, d_dtin, preferred_element_type=jnp.float32)
    d_rank = jnp.einsum("te,re->tr", d_dtin, dtproj_block, preferred_element_type=jnp.float32)
    d_xdbl = lax.psum(jnp.concatenate([d_rank, d_input, d_read], axis=1), ("row", "col")).astype(
        jnp.bfloat16
    )
    xproj_grad = jnp.einsum("te,tk->ek", xconv_low, d_xdbl, preferred_element_type=jnp.float32)
    d_xconv = (
        d_xscan
        + skip_wide * d_yfull
        + jnp.einsum("tk,ek->te", d_xdbl, xproj_block, preferred_element_type=jnp.float32)
    )
    conv_sig = jax.nn.sigmoid(conv_out)
    d_conv = d_xconv * conv_sig * (1.0 + conv_out * (1.0 - conv_sig))
    split_at = NPROMPT * LP
    d_prompt_pad, prompt_kernel = convolve_grads(
        prompt_pad, kernel, d_conv[:split_at].reshape(NPROMPT, LP, channels), LP
    )
    d_cont_pad, cont_kernel = convolve_grads(
        cont_pad, kernel, d_conv[split_at:].reshape(NCONT, LC, channels), LC
    )
    conv_grad = prompt_kernel + cont_kernel
    shift_grad = jnp.sum(d_conv, axis=0)
    d_tail = jnp.einsum("cp,cke->pke", choose, d_cont_pad[:, : KCONV - 1], precision=highest)
    d_prompt = d_prompt_pad[:, KCONV - 1 :] + jnp.pad(d_tail, ((0, 0), (LP - KCONV + 1, 0), (0, 0)))
    d_inner = jnp.concatenate(
        [d_prompt.reshape(-1, channels), d_cont_pad[:, KCONV - 1 :].reshape(-1, channels)], axis=0
    )
    d_mixed = jnp.stack([d_inner, d_gate], axis=1)
    d_scale = jnp.sum(d_mixed * projected, axis=(1, 2))
    d_proj = (inv_rms[:, None, None] * d_mixed).astype(jnp.bfloat16)
    d_proj_full = lax.all_gather(d_proj, "row", axis=2, tiled=True)
    in_grad = jnp.einsum("td,tke->dke", normed, d_proj_full, preferred_element_type=jnp.float32)
    d_normed = lax.psum_scatter(
        jnp.einsum("tke,dke->td", d_proj_full, in_block, preferred_element_type=jnp.float32),
        "col",
        scatter_dimension=0,
        tiled=True,
    )
    gain_part = jnp.sum(d_normed * local_tokens, axis=0)
    row_width = gain_part.shape[0]
    row_start = lax.axis_index("row") * row_width
    spread = lax.dynamic_update_slice(
        jnp.zeros((row_width * row_count,), jnp.float32), gain_part, (row_start,)
    )
    scale_sum, gain_sum = lax.psum((d_scale, spread), ("row", "col"))
    col_start = lax.axis_index("col") * local_rows
    local_scale = lax.dynamic_slice_in_dim(scale_sum, col_start, local_rows)
    local_inv = lax.dynamic_slice_in_dim(inv_rms, col_start, local_rows)
    gain_grad = lax.dynamic_slice_in_dim(gain_sum, row_start, row_width)
    input_grad = (
        cotangent.astype(jnp.float32)
        + d_normed * gain_wide
        - (local_scale * local_inv * local_inv * local_inv / D)[:, None] * local_tokens
    ).astype(jnp.bfloat16)
    summed = (
        lax.psum_scatter(gain_grad, "grp", scatter_dimension=0, tiled=True),
        lax.psum_scatter(in_grad, "grp", scatter_dimension=2, tiled=True),
        lax.psum_scatter(conv_grad, "grp", scatter_dimension=1, tiled=True),
        lax.psum_scatter(shift_grad, "grp", scatter_dimension=0, tiled=True),
        lax.psum_scatter(xproj_grad, "grp", scatter_dimension=0, tiled=True),
        lax.psum_scatter(dtproj_grad, "grp", scatter_dimension=1, tiled=True),
        lax.psum_scatter(bias_grad, "grp", scatter_dimension=0, tiled=True),
        lax.psum_scatter(alog_grad, "grp", scatter_dimension=1, tiled=True),
        lax.psum_scatter(skip_grad, "grp", scatter_dimension=0, tiled=True),
        lax.psum_scatter(out_grad, "grp", scatter_dimension=1, tiled=True),
    )
    return (
        output,
        input_grad,
        summed[0],
        summed[1],
        summed[2],
        summed[3],
        summed[4],
        summed[5],
        summed[6],
        summed[7],
        summed[8],
        summed[9],
    )


def solution(mesh):
    placed = (
        P(("grp", "col"), "row"),
        P(("row", "grp")),
        P("row", None, ("col", "grp")),
        P(None, ("col", "row", "grp")),
        P(("col", "row", "grp")),
        P(("col", "row", "grp"), None),
        P(None, ("col", "row", "grp")),
        P(("col", "row", "grp")),
        P(None, ("col", "row", "grp")),
        P(("col", "row", "grp")),
        P("col", ("row", "grp")),
        P("grp"),
        P(("grp", "col"), "row"),
    )
    return jax.shard_map(
        per_device,
        mesh=mesh,
        in_specs=placed,
        out_specs=(
            P(("grp", "col"), "row"),
            P(("grp", "col"), "row"),
            P(("row", "grp")),
            P("row", None, ("col", "grp")),
            P(None, ("col", "row", "grp")),
            P(("col", "row", "grp")),
            P(("col", "row", "grp"), None),
            P(None, ("col", "row", "grp")),
            P(("col", "row", "grp")),
            P(None, ("col", "row", "grp")),
            P(("col", "row", "grp")),
            P("col", ("row", "grp")),
        ),
        check_vma=False,
    )
```

profile of v0, /device:TPU:14, one launch (start us, length us, event | category | flops | bytes accessed | tf_op | source)
XLA Modules:
  0.0 3489.3 jit_solution(973523209398337264)
XLA Ops:
  16.8 28.6 all-gather.13.cloned.1.call-done
  45.4 89.4 %all-gather.11.cloned.1.call-done = bf16[2304,1024]{1,0:T(8,128)(2,1)} async-done(((bf16[576,1024]{1,0:T(8,128)(2,1)}), bf16[2304,1024]{1,0:T(8,128)(2,1)}) %all-gather.11.cloned.1.call-update) | async-done | bytes 4718608 | tf_op jit(solution)/shard_map/all_gather | solution.py:286
  134.8 16.6 fusion.33
  159.3 89.3 %all-gather.19.cloned.1.call-done = bf16[2304,1024]{1,0:T(8,128)(2,1)} async-done(((bf16[576,1024]{1,0:T(8,128)(2,1)}), bf16[2304,1024]{1,0:T(8,128)(2,1)}) %all-gather.19.cloned.1.call-update) | async-done | bytes 4718608 | tf_op jit(solution)/shard_map/all_gather | solution.py:287
  248.6 10.3 fusion.76
  301.3 19.5 all-reduce.10
  322.1 140.9 %reduce-scatter.13.cloned.1.call-done = f32[2304,2,512]{2,0,1:T(8,128)} async-done(((f32[2304,2,1024]{2,0,1:T(8,128)}), f32[2304,2,512]{2,0,1:T(8,128)}) %reduce-scatter.13.cloned.1.call-update) | async-done | bytes 9437200 | tf_op jit(solution)/shard_map/reduce_scatter | solution.py:296
  482.6 93.2 %reduce-scatter.17.cloned.1.call-done = f32[2304,512]{1,0:T(8,128)} async-done(((f32[2304,1024]{1,0:T(8,128)}), f32[2304,512]{1,0:T(8,128)}) %reduce-scatter.17.cloned.1.call-update) | async-done | bytes 4718608 | tf_op jit(solution)/shard_map/reduce_scatter | solution.py:351
  602.4 73.4 %all-reduce.20.cloned.1.call-done = f32[2304,160]{0,1:T(8,128)} async-done(((f32[2304,160]{0,1:T(8,128)}), f32[2304,160]{0,1:T(8,128)}) %all-reduce.20.cloned.1.call-update) | async-done | bytes 1474576 | tf_op jit(solution)/shard_map/psum | solution.py:323
  689.3 9.7 copy_bitcast_fusion.1
  701.9 104.3 %while.271 = (s32[]{:T(128)}, f32[144,16,512]{2,1,0:T(8,128)}, f32[16,144,512]{2,1,0:T(8,128)}, f32[16,512]{1,0:T(8,128)S(1)}, f32[16,144,512]{2,1,0:T(8,128)}, ...) while((s32[]{:T(128)}, f32[144,16,512]{2,1,0:T(8,128)}, f32[16,144,512]{2,1,0:T(8,128)}, ...), condition=%wide.region_6.7_spmd.clone, body=%wide.region_5.6_spmd.clone.sunk | while | flops 5971971 | bytes 11562099 | solution.py:80
  812.9 99.4 %while.272 = (s32[]{:T(128)}, f32[2,16,512]{2,1,0:T(8,128)S(1)}, f32[64,2,16,512]{3,2,0,1:T(8,128)}, f32[64,2,16,512]{3,2,0,1:T(8,128)}, f32[64,2,16,512]{3,2,0,1:T(8,128)}, /*index=5*/s32[]{:T(128)}, s32[]{:T(128)}) while((s32[]{:T(128)}, f32[2,16,512]{2,1,0:T(8,128)S(1)}, f32[64,2,16,512]{3,2,0,1:T(8,128)}, ...), condition=%wide.region_8.9_spmd.clone, body=%wide.region_7.8_spmd.clone.sunk | while | flops 65539 | bytes 393320 | solution.py:46
  938.4 1600.7 %while.270 = (s32[]{:T(128)}, f32[4,2304,128]{2,1,0:T(8,128)}, f32[4,2304,128]{2,1,0:T(8,128)}, f32[4,2304,16]{1,2,0:T(8,128)}, f32[4,2304,16]{1,2,0:T(8,128)}, ...) while((s32[]{:T(128)}, f32[4,2304,128]{2,1,0:T(8,128)}, ...), condition=%wide.region_34.35_spmd.clone, body=%wide.region_16.34_spmd.clone.sunk | while | flops 9328154 | bytes 62113280 | solution.py:196
  949.1 74.9 %while.273 = (s32[]{:T(128)}, f32[144,16,128]{2,1,0:T(8,128)S(1)}, f32[16,144,128]{2,1,0:T(8,128)S(1)}, f32[16,128]{1,0:T(8,128)S(1)}, f32[16,144,16]{2,1,0:T(8,...) while((s32[]{:T(128)}, f32[144,16,128]{2,1,0:T(8,128)S(1)}, ...), condition=%wide.region_19.19_spmd.clone, body=%wide.region_18.18_spmd.clone.sunk | while | flops 1474564 | bytes 2837635 | solution.py:135
  1027.8 20.7 while.274
  1052.5 48.6 %while.275 = (s32[]{:T(128)}, f32[2,16,128]{2,1,0:T(8,128)S(1)}, f32[64,2,16,128]{3,2,1,0:T(8,128)S(1)}, f32[64,2,16,128]{3,2,1,0:T(8,128)}, f32[64,2,16,128]{3,2,0,1:T(8,128)}, /*index=5*/s32[]{:T(128)}, s32[]{:T(128)}) while((s32[]{:T(128)}, f32[2,16,128]{2,1,0:T(8,128)S(1)}, f32[64,2,16,128]{3,2,1,0:T(8,128)S(1)}, ...), condition=%wide.region_23.23_spmd, body=%wide.region_22.22_spmd.sunk | while | flops 8195 | bytes 98409 | solution.py:57
  1113.8 56.7 %while.276 = (s32[]{:T(128)}, f32[144,16,128]{2,1,0:T(8,128)S(1)}, f32[16,144,16,128]{3,2,1,0:T(8,128)}, f32[16,144,128]{2,1,0:T(8,128)S(1)}, f32[16,128]{1,0:T(...) while((s32[]{:T(128)}, f32[144,16,128]{2,1,0:T(8,128)S(1)}, ...), condition=%wide.region_25.25_spmd, body=%wide.region_24.24_spmd.sunk | while | flops 1198082 | bytes 5270637 | solution.py:126
  1174.6 154.3 %while.277 = (s32[]{:T(128)}, f32[144,16,128]{2,1,0:T(8,128)S(1)}, f32[16,144,128]{2,1,0:T(8,128)S(1)}, f32[16,144,128]{2,1,0:T(8,128)}, f32[16,144,16]{2,1,0:T(...) while((s32[]{:T(128)}, f32[144,16,128]{2,1,0:T(8,128)S(1)}, ...), condition=%wide.region_32.32_spmd, body=%wide.region_26.31_spmd.sunk | while | flops 5633539 | bytes 5138637 | solution.py:168
  1349.2 74.9 %while.273 = (s32[]{:T(128)}, f32[144,16,128]{2,1,0:T(8,128)S(1)}, f32[16,144,128]{2,1,0:T(8,128)S(1)}, f32[16,128]{1,0:T(8,128)S(1)}, f32[16,144,16]{2,1,0:T(8,...) while((s32[]{:T(128)}, f32[144,16,128]{2,1,0:T(8,128)S(1)}, ...), condition=%wide.region_19.19_spmd.clone, body=%wide.region_18.18_spmd.clone.sunk | while | flops 1474564 | bytes 2837635 | solution.py:135
  1427.9 20.7 while.274
  1452.5 48.6 %while.275 = (s32[]{:T(128)}, f32[2,16,128]{2,1,0:T(8,128)S(1)}, f32[64,2,16,128]{3,2,1,0:T(8,128)S(1)}, f32[64,2,16,128]{3,2,1,0:T(8,128)}, f32[64,2,16,128]{3,2,0,1:T(8,128)}, /*index=5*/s32[]{:T(128)}, s32[]{:T(128)}) while((s32[]{:T(128)}, f32[2,16,128]{2,1,0:T(8,128)S(1)}, f32[64,2,16,128]{3,2,1,0:T(8,128)S(1)}, ...), condition=%wide.region_23.23_spmd, body=%wide.region_22.22_spmd.sunk | while | flops 8195 | bytes 98409 | solution.py:57
  1513.9 56.7 %while.276 = (s32[]{:T(128)}, f32[144,16,128]{2,1,0:T(8,128)S(1)}, f32[16,144,16,128]{3,2,1,0:T(8,128)}, f32[16,144,128]{2,1,0:T(8,128)S(1)}, f32[16,128]{1,0:T(...) while((s32[]{:T(128)}, f32[144,16,128]{2,1,0:T(8,128)S(1)}, ...), condition=%wide.region_25.25_spmd, body=%wide.region_24.24_spmd.sunk | while | flops 1198082 | bytes 5270637 | solution.py:126
  1574.7 154.3 %while.277 = (s32[]{:T(128)}, f32[144,16,128]{2,1,0:T(8,128)S(1)}, f32[16,144,128]{2,1,0:T(8,128)S(1)}, f32[16,144,128]{2,1,0:T(8,128)}, f32[16,144,16]{2,1,0:T(...) while((s32[]{:T(128)}, f32[144,16,128]{2,1,0:T(8,128)S(1)}, ...), condition=%wide.region_32.32_spmd, body=%wide.region_26.31_spmd.sunk | while | flops 5633539 | bytes 5138637 | solution.py:168
  1749.3 74.9 %while.273 = (s32[]{:T(128)}, f32[144,16,128]{2,1,0:T(8,128)S(1)}, f32[16,144,128]{2,1,0:T(8,128)S(1)}, f32[16,128]{1,0:T(8,128)S(1)}, f32[16,144,16]{2,1,0:T(8,...) while((s32[]{:T(128)}, f32[144,16,128]{2,1,0:T(8,128)S(1)}, ...), condition=%wide.region_19.19_spmd.clone, body=%wide.region_18.18_spmd.clone.sunk | while | flops 1474564 | bytes 2837635 | solution.py:135
  1828.0 20.7 while.274
  1852.7 48.6 %while.275 = (s32[]{:T(128)}, f32[2,16,128]{2,1,0:T(8,128)S(1)}, f32[64,2,16,128]{3,2,1,0:T(8,128)S(1)}, f32[64,2,16,128]{3,2,1,0:T(8,128)}, f32[64,2,16,128]{3,2,0,1:T(8,128)}, /*index=5*/s32[]{:T(128)}, s32[]{:T(128)}) while((s32[]{:T(128)}, f32[2,16,128]{2,1,0:T(8,128)S(1)}, f32[64,2,16,128]{3,2,1,0:T(8,128)S(1)}, ...), condition=%wide.region_23.23_spmd, body=%wide.region_22.22_spmd.sunk | while | flops 8195 | bytes 98409 | solution.py:57
  1914.0 56.7 %while.276 = (s32[]{:T(128)}, f32[144,16,128]{2,1,0:T(8,128)S(1)}, f32[16,144,16,128]{3,2,1,0:T(8,128)}, f32[16,144,128]{2,1,0:T(8,128)S(1)}, f32[16,128]{1,0:T(...) while((s32[]{:T(128)}, f32[144,16,128]{2,1,0:T(8,128)S(1)}, ...), condition=%wide.region_25.25_spmd, body=%wide.region_24.24_spmd.sunk | while | flops 1198082 | bytes 5270637 | solution.py:126
  1974.8 154.3 %while.277 = (s32[]{:T(128)}, f32[144,16,128]{2,1,0:T(8,128)S(1)}, f32[16,144,128]{2,1,0:T(8,128)S(1)}, f32[16,144,128]{2,1,0:T(8,128)}, f32[16,144,16]{2,1,0:T(...) while((s32[]{:T(128)}, f32[144,16,128]{2,1,0:T(8,128)S(1)}, ...), condition=%wide.region_32.32_spmd, body=%wide.region_26.31_spmd.sunk | while | flops 5633539 | bytes 5138637 | solution.py:168
  2149.3 74.9 %while.273 = (s32[]{:T(128)}, f32[144,16,128]{2,1,0:T(8,128)S(1)}, f32[16,144,128]{2,1,0:T(8,128)S(1)}, f32[16,128]{1,0:T(8,128)S(1)}, f32[16,144,16]{2,1,0:T(8,...) while((s32[]{:T(128)}, f32[144,16,128]{2,1,0:T(8,128)S(1)}, ...), condition=%wide.region_19.19_spmd.clone, body=%wide.region_18.18_spmd.clone.sunk | while | flops 1474564 | bytes 2837635 | solution.py:135
  2228.1 20.7 while.274
  2252.7 48.6 %while.275 = (s32[]{:T(128)}, f32[2,16,128]{2,1,0:T(8,128)S(1)}, f32[64,2,16,128]{3,2,1,0:T(8,128)S(1)}, f32[64,2,16,128]{3,2,1,0:T(8,128)}, f32[64,2,16,128]{3,2,0,1:T(8,128)}, /*index=5*/s32[]{:T(128)}, s32[]{:T(128)}) while((s32[]{:T(128)}, f32[2,16,128]{2,1,0:T(8,128)S(1)}, f32[64,2,16,128]{3,2,1,0:T(8,128)S(1)}, ...), condition=%wide.region_23.23_spmd, body=%wide.region_22.22_spmd.sunk | while | flops 8195 | bytes 98409 | solution.py:57
  2314.1 56.7 %while.276 = (s32[]{:T(128)}, f32[144,16,128]{2,1,0:T(8,128)S(1)}, f32[16,144,16,128]{3,2,1,0:T(8,128)}, f32[16,144,128]{2,1,0:T(8,128)S(1)}, f32[16,128]{1,0:T(...) while((s32[]{:T(128)}, f32[144,16,128]{2,1,0:T(8,128)S(1)}, ...), condition=%wide.region_25.25_spmd, body=%wide.region_24.24_spmd.sunk | while | flops 1198082 | bytes 5270637 | solution.py:126
  2374.8 154.3 %while.277 = (s32[]{:T(128)}, f32[144,16,128]{2,1,0:T(8,128)S(1)}, f32[16,144,128]{2,1,0:T(8,128)S(1)}, f32[16,144,128]{2,1,0:T(8,128)}, f32[16,144,16]{2,1,0:T(...) while((s32[]{:T(128)}, f32[144,16,128]{2,1,0:T(8,128)S(1)}, ...), condition=%wide.region_32.32_spmd, body=%wide.region_26.31_spmd.sunk | while | flops 5633539 | bytes 5138637 | solution.py:168
  2549.5 79.0 %all-reduce.21 = bf16[2304,160]{0,1:T(8,128)(2,1)S(1)} all-reduce(f32[2304,160]{0,1:T(8,128)S(1)} %pad_maximum_fusion.4), channel_id=1, replica_groups=mesh['grp'=4,'row'=2,'col'=4] {'row','col'}, use_global_device_ids=true, to_apply=%region_37.38 | all-reduce | flops 368640 | bytes 2211840 | tf_op jit(solution)/shard_map/psum | solution.py:368
  2647.2 140.5 %while.264 = (s32[]{:T(128)}, f32[144,16,512]{2,1,0:T(8,128)}, f32[16,144,512]{2,1,0:T(8,128)}, f32[16,144,512]{2,1,0:T(8,128)}, f32[16,512]{1,0:T(8,128)S(1)}, ...) while((s32[]{:T(128)}, f32[144,16,512]{2,1,0:T(8,128)}, ...), condition=%wide.region_13.14_spmd, body=%wide.region_11.13_spmd.sunk | while | flops 7077890 | bytes 12474485 | solution.py:107
  2842.3 108.4 %all-gather.21.cloned.1.call-done = bf16[2304,2,1024]{2,0,1:T(8,128)(2,1)} async-done(((bf16[2304,2,512]{2,0,1:T(8,128)(2,1)}), bf16[2304,2,1024]{2,0,1:T(8,128)(2,1)}) %all-gather.21.cloned.1.call-update) | async-done | bytes 9437200 | tf_op jit(solution)/shard_map/all_gather | solution.py:396
  2950.7 16.1 fusion.31
  2966.9 16.2 convolution_bitcast_fusion.1
  2983.2 31.8 all-gather.15.cloned.1.call-done
  3045.6 66.9 %reduce-scatter.21.cloned.1.call-done = f32[1024,2,256]{2,0,1:T(8,128)} async-done(((f32[1024,2,1024]{2,0,1:T(8,128)}), f32[1024,2,256]{2,0,1:T(8,128)}) %reduce-scatter.21.cloned.1.call-update) | async-done | bytes 2097168 | tf_op jit(solution)/shard_map/reduce_scatter | solution.py:422
  3117.0 159.8 %reduce-scatter.19.cloned.1.call-done = f32[576,1024]{1,0:T(8,128)} async-done(((f32[2304,1024]{1,0:T(8,128)}), f32[576,1024]{1,0:T(8,128)}) %reduce-scatter.19.cloned.1.call-update) | async-done | bytes 2359312 | tf_op jit(solution)/shard_map/reduce_scatter | solution.py:398
  3280.9 34.5 all-reduce.15
  3316.1 12.1 all-reduce.16
  3332.7 34.0 reduce-scatter.15.cloned.1.call-done
  3370.4 18.1 reduce-scatter.27.cloned.1.call-done
  3388.5 22.9 reduce-scatter.25.cloned.1.call-done
  3411.5 23.5 reduce-scatter.23.cloned.1.call-done
  3435.0 47.5 %reduce-scatter.29.cloned.1.call-done = f32[1024,256]{1,0:T(8,128)} async-done(((f32[1024,1024]{1,0:T(8,128)}), f32[1024,256]{1,0:T(8,128)}) %reduce-scatter.29.cloned.1.call-update) | async-done | bytes 1048592 | tf_op jit(solution)/shard_map/reduce_scatter | solution.py:430
  (2452 shorter events, 2229.2 us)
Async XLA Ops:
  7.2 38.2 %all-gather.13.cloned.1.call-start = ((), (), s32[]{:S(2)}) async-start(), calls=%async_computation.11 | async-start | bytes 5242880 | tf_op jit(solution)/shard_map/all_gather | solution.py:273
  9.6 125.2 %all-gather.11.cloned.1.call-start = ((), (), s32[]{:S(2)}) async-start(), calls=%async_computation.10 | async-start | bytes 5898240 | tf_op jit(solution)/shard_map/all_gather | solution.py:286
  10.3 149.0 %all-gather.17.cloned.1.call-start = ((), (), s32[]{:S(2)}) async-start(), calls=%async_computation.15 | async-start | bytes 2621440 | tf_op jit(solution)/shard_map/all_gather | solution.py:281
  11.1 237.5 %all-gather.19.cloned.1.call-start = ((), (), s32[]{:S(2)}) async-start(), calls=%async_computation.17 | async-start | bytes 5898240 | tf_op jit(solution)/shard_map/all_gather | solution.py:287
  11.7 451.3 %reduce-scatter.13.cloned.1.call-start = ((), (), s32[]{:S(2)}) async-start(), calls=%async_computation.12 | async-start | bytes 28311552 | tf_op jit(solution)/shard_map/reduce_scatter | solution.py:296
  16.8 134.6 %copy-start.51 = (f32[4,1,256]{2,1,0:T(1,128)}, f32[4,1,256]{2,1,0:T(1,128)S(1)}, u32[]{:S(2)}) copy-start(f32[4,1,256]{2,1,0:T(1,128)S(1)} %convert_element_type.114) | copy-start | bytes 12292
  151.4 424.3 %reduce-scatter.17.cloned.1.call-start = ((), (), s32[]{:S(2)}) async-start(), calls=%async_computation.18 | async-start | bytes 14155776 | tf_op jit(solution)/shard_map/reduce_scatter | solution.py:351
  258.9 10.7 copy-start.58
  258.9 16.3 copy-start.54
  258.9 22.1 copy-start.61
  258.9 22.7 copy-start.55
  258.9 27.7 copy-start.48
  259.0 33.1 copy-start.47
  259.0 416.8 %all-reduce.20.cloned.1.call-start = ((), (), s32[]{:S(2)}) async-start(), calls=%async_computation.13 | async-start | bytes 2949120 | tf_op jit(solution)/shard_map/psum | solution.py:323
  292.1 383.7 %copy-start.31 = (bf16[128,512]{1,0:T(8,128)(2,1)}, bf16[128,512]{1,0:T(8,128)(2,1)S(1)}, u32[]{:S(2)}) copy-start(bf16[128,512]{1,0:T(8,128)(2,1)S(1)} %all_gather.48) | copy-start | bytes 393220
  297.6 287.1 %copy-start.33 = (bf16[512,160]{0,1:T(8,128)(2,1)}, bf16[512,160]{0,1:T(8,128)(2,1)S(1)}, u32[]{:S(2)}) copy-start(bf16[512,160]{0,1:T(8,128)(2,1)S(1)} %all_gather.47) | copy-start | bytes 491524
  297.6 184.6 %copy-start.39 = (f32[1,512]{1,0:T(1,128)}, f32[1,512]{1,0:T(1,128)S(1)}, u32[]{:S(2)}) copy-start(f32[1,512]{1,0:T(1,128)S(1)} %get-tuple-element.1754) | copy-start | bytes 6148
  297.6 184.6 %copy-start.41 = (f32[1,512]{1,0:T(1,128)}, f32[1,512]{1,0:T(1,128)S(1)}, u32[]{:S(2)}) copy-start(f32[1,512]{1,0:T(1,128)S(1)} %get-tuple-element.1755) | copy-start | bytes 6148
  297.6 184.6 %copy-start.43 = (f32[1,512]{1,0:T(1,128)}, f32[1,512]{1,0:T(1,128)S(1)}, u32[]{:S(2)}) copy-start(f32[1,512]{1,0:T(1,128)S(1)} %get-tuple-element.1756) | copy-start | bytes 6148
  297.7 184.6 %copy-start.45 = (f32[1,512]{1,0:T(1,128)}, f32[1,512]{1,0:T(1,128)S(1)}, u32[]{:S(2)}) copy-start(f32[1,512]{1,0:T(1,128)S(1)} %get-tuple-element.1757) | copy-start | bytes 6148
  322.1 145.3 %copy-start.37 = (f32[2304]{0:T(1024)}, f32[2304]{0:T(1024)S(1)}, u32[]{:S(2)}) copy-start(f32[2304]{0:T(1024)S(1)} %get-tuple-element.1718) | copy-start | bytes 27652
  471.0 11.2 copy-start.26
  471.9 10.4 copy-start.35
  482.6 113.1 %copy-start.21 = (f32[2,128,512]{2,1,0:T(8,128)}, f32[2,128,512]{2,1,0:T(8,128)S(1)}, u32[]{:S(2)}) copy-start(f32[2,128,512]{2,1,0:T(8,128)S(1)} %multiply_add_fusion.4) | copy-start | bytes 1572868
  588.2 2362.5 %all-gather.21.cloned.1.call-start = ((), (), s32[]{:S(2)}) async-start(), calls=%async_computation.19 | async-start | bytes 14155776 | tf_op jit(solution)/shard_map/all_gather | solution.py:396
  811.7 100.9 %slice-start.12 = ((f32[144,16,512]{2,1,0:T(8,128)}), f32[16,16,512]{2,1,0:T(8,128)S(1)}, s32[]{:S(2)}) async-start(f32[144,16,512]{2,1,0:T(8,128)} %copy-done.11), calls=%async_computation.39 | async-start | bytes 1048576 | tf_op jit(solution)/shard_map/slice | solution.py:90
  919.1 7.4 copy-start.23
  2548.5 80.0 %copy-start.22 = (f32[2,128,512]{2,1,0:T(8,128)S(1)}, f32[2,128,512]{2,1,0:T(8,128)}, u32[]{:S(2)}) copy-start(f32[2,128,512]{2,1,0:T(8,128)} %copy-done.21) | copy-start | bytes 1572868
  2548.5 80.0 %copy-start.34 = (bf16[512,160]{0,1:T(8,128)(2,1)S(1)}, bf16[512,160]{0,1:T(8,128)(2,1)}, u32[]{:S(2)}) copy-start(bf16[512,160]{0,1:T(8,128)(2,1)} %copy-done.33) | copy-start | bytes 491524
  2548.5 80.0 %copy-start.53 = (f32[4,1,128]{2,1,0:T(1,128)S(1)}, f32[4,1,128]{2,1,0:T(1,128)}, u32[]{:S(2)}) copy-start(f32[4,1,128]{2,1,0:T(1,128)} %convert_element_type.116) | copy-start | bytes 6148
  2795.0 23.0 slice-start
  2795.0 23.0 slice-start.1
  2795.0 23.0 slice-start.8
  2803.6 14.4 slice-start.2
  2803.6 14.4 slice-start.9
  2812.7 10.7 slice-start.5
  2831.2 183.8 %all-gather.15.cloned.1.call-start = ((), (), s32[]{:S(2)}) async-start(), calls=%async_computation.14 | async-start | bytes 7077888 | tf_op jit(solution)/shard_map/all_gather | solution.py:341
  2831.9 212.2 %reduce-scatter.31.cloned.1.call-start = ((), (), s32[]{:S(2)}) async-start(), calls=%async_computation.26 | async-start | bytes 327680
  2839.7 111.0 %copy-start.52 = (f32[4,1,256]{2,1,0:T(1,128)S(1)}, f32[4,1,256]{2,1,0:T(1,128)}, u32[]{:S(2)}) copy-start(f32[4,1,256]{2,1,0:T(1,128)} %copy-done.51) | copy-start | bytes 12292
  2842.2 270.2 %reduce-scatter.21.cloned.1.call-start = ((), (), s32[]{:S(2)}) async-start(), calls=%async_computation.21 | async-start | bytes 10485760 | tf_op jit(solution)/shard_map/reduce_scatter | solution.py:422
  2966.8 310.0 %reduce-scatter.19.cloned.1.call-start = ((), (), s32[]{:S(2)}) async-start(), calls=%async_computation.20 | async-start | bytes 11796480 | tf_op jit(solution)/shard_map/reduce_scatter | solution.py:398
  2983.1 383.6 %reduce-scatter.15.cloned.1.call-start = ((), (), s32[]{:S(2)}) async-start(), calls=%async_computation.16 | async-start | bytes 5898240 | tf_op jit(solution)/shard_map/reduce_scatter | solution.py:342
  3024.4 364.2 %reduce-scatter.27.cloned.1.call-start = ((), (), s32[]{:S(2)}) async-start(), calls=%async_computation.24 | async-start | bytes 40960 | tf_op jit(solution)/shard_map/reduce_scatter | solution.py:428
  3025.7 385.7 %reduce-scatter.25.cloned.1.call-start = ((), (), s32[]{:S(2)}) async-start(), calls=%async_computation.23 | async-start | bytes 327680 | tf_op jit(solution)/shard_map/reduce_scatter | solution.py:426
  3029.1 406.0 %reduce-scatter.23.cloned.1.call-start = ((), (), s32[]{:S(2)}) async-start(), calls=%async_computation.22 | async-start | bytes 409600 | tf_op jit(solution)/shard_map/reduce_scatter | solution.py:425
  3030.5 452.1 %reduce-scatter.29.cloned.1.call-start = ((), (), s32[]{:S(2)}) async-start(), calls=%async_computation.25 | async-start | bytes 5242880 | tf_op jit(solution)/shard_map/reduce_scatter | solution.py:430
  3040.2 236.6 %copy-start.16 = (bf16[576,1024]{1,0:T(8,128)(2,1)S(1)}, bf16[576,1024]{1,0:T(8,128)(2,1)}, u32[]{:S(2)}) copy-start(bf16[576,1024]{1,0:T(8,128)(2,1)} %param.33) | copy-start | bytes 3538948
  3276.8 89.9 %copy-start.17 = (f32[576,1024]{1,0:T(8,128)S(1)}, f32[576,1024]{1,0:T(8,128)}, u32[]{:S(2)}) copy-start(f32[576,1024]{1,0:T(8,128)} %reduce-scatter.19.cloned.1.call-done) | copy-start | bytes 7077892
  (56 other events, 204.9 us)
Sparse Core Ops, SparseCore 0:
  10.1 35.1 all-gather.12
  47.0 87.7 all-gather.10
  136.4 22.8 all-gather.16
  160.7 87.7 all-gather.18
  250.7 212.2 reduce-scatter.12
  465.1 110.5 reduce-scatter.16
  588.3 87.4 all-reduce.19
  2831.3 119.3 all-gather.20
  2952.3 62.6 all-gather.14
  3018.0 20.0 reduce-scatter.30
  3040.7 71.7 reduce-scatter.20
  3114.8 161.9 reduce-scatter.18
  3279.2 87.4 reduce-scatter.14
  3369.7 18.8 reduce-scatter.26
  3391.4 20.0 reduce-scatter.24
  3414.5 20.4 reduce-scatter.22
  3438.0 44.5 reduce-scatter.28
where the time goes:
time: 3550 us; the launch traced here: 3490 us
  other arithmetic  1250 us (35%)
  waiting for transfers between devices  1040 us (29%)
  local copies, waits for them, and re-layouts  887 us (25%)
  blocking collectives  186 us (5%)
  matrix products  99.1 us (3%)
    add x288, other arithmetic, backward_link(): return (pair[1] + pair[0] * carried, carried)  236 us
    reduce_sum x64, other arithmetic, descend(): rate_term = jnp.sum(weighted * step_t[:, None, :], axis=0)  208 us
    mul x128, local copies, waits for them, and re-layouts, retreat(): grad_sum = read_t[:, :, None] * grad_t[:, None, :] + carried  197 us
    reduce_scatter x1, waiting for transfers between devices, per_device(): lax.psum_scatter(jnp.einsum('tke,dke->td', d_proj_full, in_block, preferr...  160 us
    reduce_scatter x1, waiting for transfers between devices, per_device(): lax.psum_scatter(partial_value, 'row', scatter_dimension=2, tiled=True)  141 us
    mul x128, local copies, waits for them, and re-layouts, descend(): grad_sum = read_t[:, :, None] * grad_t[:, None, :] + carried  114 us
    all_gather x1, waiting for transfers between devices, per_device(): d_proj_full = lax.all_gather(d_proj, 'row', axis=2, tiled=True)  108 us
    mul x64, other arithmetic, retreat(): return (factor * grad_sum, None)  101 us
  transfers between devices with their start and end apart: 17, of which 16 were waited for; matrix products, arithmetic and copies ran while one was open for 4% of the time, Pallas kernels for 0%

commit v1 on v0

v1 whole, which is shorter than its diff:
```python
import functools

import jax
import jax.numpy as jnp
from jax import lax
from jax.experimental import pallas as pl
from jax.experimental.pallas import tpu as pltpu
from jax.sharding import PartitionSpec as P

D = 2048
NSTATE = 16
KCONV = 4
RANK = 128
NPROMPT = 2
LP = 1024
LC = 128
NCONT = 2

eps = 1e-05
CH = 128
SUB = 16
PC = LP // CH
SEQ = LP + LC
NCH = SEQ // CH
XW = RANK + 2 * NSTATE
SPAN = SUB * NSTATE
LOG2E = 1.4426950408889634
VMEM_LIMIT = 56 * 1024 * 1024

f32 = jnp.float32
bf16 = jnp.bfloat16


def dot_nn(a, b):
    return lax.dot_general(a, b, (((1,), (0,)), ((), ())), preferred_element_type=f32)


def dot_nt(a, b):
    return lax.dot_general(a, b, (((1,), (1,)), ((), ())), preferred_element_type=f32)


def dot_tn(a, b):
    return lax.dot_general(a, b, (((0,), (0,)), ((), ())), preferred_element_type=f32)


def expand_tile():
    lane = lax.broadcasted_iota(jnp.int32, (NSTATE, SPAN), 1)
    row = lax.broadcasted_iota(jnp.int32, (NSTATE, SPAN), 0)
    return jnp.where(lane % NSTATE == row, 1.0, 0.0)


def own_token(rows):
    lane = lax.broadcasted_iota(jnp.int32, (rows, SPAN), 1)
    row = lax.broadcasted_iota(jnp.int32, (rows, SPAN), 0)
    return lane // NSTATE == row % SUB


def conv_forward(inner_ref, inv_ref, tail_ref, conv_ref, xproj_ref, xconv_ref, xdbl_ref, buf):
    i = pl.program_id(0)

    @pl.when(i == 0)
    def _():
        buf[0:8] = jnp.zeros_like(buf[0:8])

    @pl.when(i == PC)
    def _():
        buf[0:8] = tail_ref[...]

    @pl.when((i > 0) & (i < PC))
    def _():
        buf[0:8] = buf[CH : CH + 8]

    buf[8 : CH + 8] = inv_ref[...] * inner_ref[...]
    out = conv_ref[4:5]
    for k in range(KCONV):
        out = out + conv_ref[k : k + 1] * buf[5 + k : 5 + k + CH]
    xconv = (out * jax.nn.sigmoid(out)).astype(bf16)
    xconv_ref[...] = xconv
    xdbl_ref[...] = dot_nt(xproj_ref[...], xconv)


def softplus(v):
    return jnp.maximum(v, 0.0) + jnp.log1p(jnp.exp(-jnp.abs(v)))


def by_sub(v):
    return v.reshape(CH // SUB, SUB, v.shape[-1])


def scan_forward(kept, xdbl_ref, xconv_ref, gate_ref, inv_ref, dtp_ref, vec_ref, rate_ref, start_ref, *refs):
    gated_ref, yfull_ref, starts_ref, final_ref, dt_s, u_s, cb_s, h_s, y_s = refs[kept:]
    i = pl.program_id(0)

    @pl.when(i == 0)
    def _():
        final_ref[...] = start_ref[...]

    starts_ref[0] = final_ref[...]
    xconv = xconv_ref[...].astype(f32)
    step = softplus(dot_tn(xdbl_ref[:RANK].astype(bf16), dtp_ref[...]) + vec_ref[0:1])
    dt_s[...] = by_sub(step)
    u_s[...] = by_sub(step * xconv)
    reads = dot_tn(xdbl_ref[RANK + NSTATE :].astype(bf16), expand_tile().astype(bf16))
    cb_s[...] = jnp.where(own_token(CH), reads, 0.0).astype(bf16)
    rate = rate_ref[...] * LOG2E

    def block(j, carried):
        h, maps = carried
        for t in range(SUB):
            a = jnp.exp2(dt_s[j, t : t + 1, :] * rate)
            h = a * h + u_s[j, t : t + 1, :] * maps[:, t : t + 1]
            h_s[t * NSTATE : (t + 1) * NSTATE, :] = h.astype(bf16)
        rows = pl.ds(pl.multiple_of(j * SUB, SUB), SUB)
        y_s[rows, :] = dot_nn(cb_s[rows, :], h_s[...])
        return (h, pltpu.roll(maps, CH - SUB, 1))

    h, _ = lax.fori_loop(0, CH // SUB, block, (final_ref[...], xdbl_ref[RANK : RANK + NSTATE]))
    final_ref[...] = h
    yfull = y_s[...] + vec_ref[1:2] * xconv
    gate = inv_ref[...] * gate_ref[...]
    gated_ref[...] = (yfull * (gate * jax.nn.sigmoid(gate))).astype(bf16)
    yfull_ref[...] = yfull.astype(bf16)


def scan_backward(kept, xdbl_ref, xconv_ref, dy_ref, dtp_ref, vec_ref, rate_ref, starts_ref, carry_ref, alog0_ref, sums0_ref, dtpg0_ref, *refs):
    dxdbl_ref, dxc_ref, alog_ref, sums_ref, dtpg_ref, first_ref = refs[kept : kept + 6]
    dt_s, u_s, x_s, dy_s, a_s, h_s, g_s, w_s, b_s, m1_s, m2_s, ds_s, dx_s, sig_s = refs[kept + 6 :]
    i = pl.program_id(0)

    @pl.when(i == 0)
    def _():
        alog_ref[...] = alog0_ref[...]
        sums_ref[...] = sums0_ref[...]
        dtpg_ref[...] = dtpg0_ref[...]
        first_ref[...] = carry_ref[...]

    low = xdbl_ref[:RANK].astype(bf16)
    step_inner = dot_tn(low, dtp_ref[...]) + vec_ref[0:1]
    step = softplus(step_inner)
    sig_s[...] = jax.nn.sigmoid(step_inner)
    xconv = xconv_ref[...].astype(f32)
    dy = dy_ref[...]
    dt_s[...] = by_sub(step)
    u_s[...] = by_sub(step * xconv)
    x_s[...] = by_sub(xconv)
    dy_s[...] = by_sub(dy)
    tile = expand_tile().astype(bf16)
    b_s[...] = jnp.where(own_token(CH), dot_tn(xdbl_ref[RANK : RANK + NSTATE].astype(bf16), tile), 0.0).astype(bf16)
    rate = rate_ref[...]
    rate2 = rate * LOG2E
    h_s[0:NSTATE] = starts_ref[0]

    def ahead(j, carried):
        h, maps = carried
        for t in range(SUB):
            a = jnp.exp2(dt_s[j, t : t + 1, :] * rate2)
            h = a * h + u_s[j, t : t + 1, :] * maps[:, t : t + 1]
            a_s[j, t * NSTATE : (t + 1) * NSTATE, :] = a
            at = pl.multiple_of(j * SPAN + (t + 1) * NSTATE, NSTATE)
            h_s[pl.ds(at, NSTATE), :] = h
        return (h, pltpu.roll(maps, CH - SUB, 1))

    lax.fori_loop(0, CH // SUB, ahead, (starts_ref[0], xdbl_ref[RANK : RANK + NSTATE]))
    ones = jnp.where(own_token(SUB), 1.0, 0.0).astype(bf16)
    mine_sub = own_token(SUB)

    def back(jj, carried):
        g, alog, maps = carried
        j = CH // SUB - 1 - jj
        maps = pltpu.roll(maps, SUB, 1)
        for t in reversed(range(SUB)):
            dt = dt_s[j, t : t + 1, :]
            gs = maps[:, t : t + 1] * dy_s[j, t : t + 1, :] + g
            g = a_s[j, t * NSTATE : (t + 1) * NSTATE, :] * gs
            prior = h_s[pl.ds(pl.multiple_of(j * SPAN + t * NSTATE, NSTATE), NSTATE), :]
            w = g * prior
            alog = alog + w * dt
            g_s[t * NSTATE : (t + 1) * NSTATE, :] = gs.astype(bf16)
            w_s[t * NSTATE : (t + 1) * NSTATE, :] = (w * rate).astype(bf16)
        rows = pl.ds(pl.multiple_of(j * SUB, SUB), SUB)
        gs_all = g_s[...]
        through = dot_nn(b_s[rows, :], gs_all)
        ds_s[rows, :] = dot_nn(ones, w_s[...]) + x_s[j] * through
        dx_s[rows, :] = dt_s[j] * through + vec_ref[1:2] * dy_s[j]
        hs = h_s[pl.ds(pl.multiple_of(j * SPAN + NSTATE, NSTATE), SPAN), :].astype(bf16)
        m1_s[rows, :] = jnp.where(mine_sub, dot_nt(u_s[j].astype(bf16), gs_all), 0.0).astype(bf16)
        m2_s[rows, :] = jnp.where(mine_sub, dot_nt(dy_s[j].astype(bf16), hs), 0.0).astype(bf16)
        return (g, alog, maps)

    g, alog, _ = lax.fori_loop(0, CH // SUB, back, (first_ref[...], alog_ref[...], xdbl_ref[RANK + NSTATE :]))
    first_ref[...] = g
    alog_ref[...] = alog
    d_inner = ds_s[...] * sig_s[...]
    d_low = d_inner.astype(bf16)
    sums_ref[0:1] = sums_ref[0:1] + jnp.sum(d_inner, axis=0, keepdims=True)
    sums_ref[1:2] = sums_ref[1:2] + jnp.sum(dy * xconv, axis=0, keepdims=True)
    dtpg_ref[...] = dtpg_ref[...] + dot_nn(low, d_low)
    dxdbl_ref[:RANK] = dot_nt(dtp_ref[...], d_low)
    dxdbl_ref[RANK : RANK + NSTATE] = dot_nt(tile, m1_s[...])
    dxdbl_ref[RANK + NSTATE :] = dot_nt(tile, m2_s[...])
    dxc_ref[...] = dx_s[...]


def conv_backward(kept, chunks, first, inner_ref, halo_ref, inv_ref, halo_inv_ref, tail_ref, conv_ref, xproj_ref, dxc_ref, dxdbl_ref, follow_ref, sums0_ref, xprojg0_ref, *refs):
    dproj_ref, dscale_ref, sums_ref, xprojg_ref, head_ref, buf, dbuf = refs[kept:]
    i = pl.program_id(0)
    chunk = first + chunks - 1 - i

    @pl.when(i == 0)
    def _():
        sums_ref[...] = sums0_ref[...]
        xprojg_ref[...] = xprojg0_ref[...]
        head_ref[...] = follow_ref[...]

    projected = inner_ref[...]
    inv = inv_ref[...]
    before = halo_inv_ref[...] * halo_ref[...]
    before = jnp.where(chunk == 0, 0.0, jnp.where(chunk == PC, tail_ref[...], before))
    buf[0:8] = before
    buf[8 : CH + 8] = inv * projected
    out = conv_ref[4:5]
    for k in range(KCONV):
        out = out + conv_ref[k : k + 1] * buf[5 + k : 5 + k + CH]
    sig = jax.nn.sigmoid(out)
    xconv = (out * sig).astype(bf16)
    dxdbl = dxdbl_ref[...].astype(bf16)
    xprojg_ref[...] = xprojg_ref[...] + dot_nn(dxdbl, xconv)
    d_x = dxc_ref[...] + dot_tn(dxdbl, xproj_ref[...])
    d_conv = d_x * (sig * (1.0 + out * (1.0 - sig)))
    dbuf[CH : CH + 8] = head_ref[...]
    dbuf[0:CH] = d_conv
    d_inner = conv_ref[3:4] * d_conv
    for k in range(KCONV - 1):
        d_inner = d_inner + conv_ref[k : k + 1] * dbuf[3 - k : 3 - k + CH]
    for k in range(KCONV):
        sums_ref[k : k + 1] = sums_ref[k : k + 1] + jnp.sum(buf[5 + k : 5 + k + CH] * d_conv, axis=0, keepdims=True)
    sums_ref[4:5] = sums_ref[4:5] + jnp.sum(d_conv, axis=0, keepdims=True)
    dproj_ref[...] = (inv * d_inner).astype(bf16)
    dscale_ref[...] = jnp.sum(d_inner * projected, axis=1, keepdims=True)
    head_ref[...] = d_conv[0:8]


def call(body, chunks, args, in_specs, outs, out_specs, scratch, micros, aliases=None):
    return pl.pallas_call(
        body,
        grid=(chunks,),
        in_specs=in_specs,
        out_specs=out_specs,
        scratch_shapes=scratch,
        out_shape=outs,
        input_output_aliases=aliases or {},
        compiler_params=pltpu.CompilerParams(dimension_semantics=("arbitrary",), vmem_limit_bytes=VMEM_LIMIT),
        cost_estimate=pl.CostEstimate(flops=micros * 1000000000, bytes_accessed=1000000, transcendentals=0),
    )(*args)


def shaped(*shape, dtype=f32):
    return jax.ShapeDtypeStruct(shape, dtype)


def rows_of(width, place):
    return pl.BlockSpec((CH, width), lambda i: (place(i), 0))


def lanes_of(height, place):
    return pl.BlockSpec((height, CH), lambda i: (0, place(i)))


def whole(*shape):
    return pl.BlockSpec(shape, lambda i: (0,) * len(shape))


ANY = pl.BlockSpec(memory_space=pl.ANY)


def run_conv_forward(inner, inv, tail, conv, xproj):
    w = inner.shape[1]
    at = lambda i: i
    return call(
        conv_forward,
        NCH,
        (inner, inv, tail, conv, xproj),
        [rows_of(w, at), rows_of(1, at), whole(8, w), whole(8, w), whole(XW, w)],
        (shaped(SEQ, w, dtype=bf16), shaped(XW, SEQ)),
        (rows_of(w, at), lanes_of(XW, at)),
        [pltpu.VMEM((CH + 8, w), f32)],
        12,
    )


def run_scan_forward(first, chunks, xdbl, xconv, gate, inv, dtp, vec, rate, start, kept=()):
    w = xconv.shape[1]
    at = lambda i: first + i
    return call(
        functools.partial(scan_forward, len(kept)),
        chunks,
        (xdbl, xconv, gate, inv, dtp, vec, rate, start, *kept),
        [lanes_of(XW, at), rows_of(w, at), rows_of(w, at), rows_of(1, at), whole(RANK, w), whole(8, w), whole(NSTATE, w), whole(NSTATE, w)] + [ANY] * len(kept),
        (shaped(SEQ, w, dtype=bf16), shaped(SEQ, w, dtype=bf16), shaped(NCH, NSTATE, w), shaped(NSTATE, w)),
        (rows_of(w, at), rows_of(w, at), pl.BlockSpec((1, NSTATE, w), lambda i: (first + i, 0, 0)), whole(NSTATE, w)),
        [
            pltpu.VMEM((CH // SUB, SUB, w), f32),
            pltpu.VMEM((CH // SUB, SUB, w), f32),
            pltpu.VMEM((CH, SPAN), bf16),
            pltpu.VMEM((SPAN, w), bf16),
            pltpu.VMEM((CH, w), f32),
        ],
        5 * chunks,
        {8 + k: k for k in range(len(kept))},
    )


def run_scan_backward(first, chunks, xdbl, xconv, dy, dtp, vec, rate, starts, carry, sums, kept=()):
    w = xconv.shape[1]
    at = lambda i: first + chunks - 1 - i
    local = lambda i: chunks - 1 - i
    sub = pltpu.VMEM((CH // SUB, SUB, w), f32)
    return call(
        functools.partial(scan_backward, len(kept)),
        chunks,
        (xdbl, xconv, dy, dtp, vec, rate, starts, carry, *sums, *kept),
        [
            lanes_of(XW, at),
            rows_of(w, at),
            rows_of(w, at),
            whole(RANK, w),
            whole(8, w),
            whole(NSTATE, w),
            pl.BlockSpec((1, NSTATE, w), lambda i: (at(i), 0, 0)),
            whole(NSTATE, w),
            whole(NSTATE, w),
            whole(8, w),
            whole(RANK, w),
        ]
        + [ANY] * len(kept),
        (shaped(XW, chunks * CH), shaped(SEQ, w), shaped(NSTATE, w), shaped(8, w), shaped(RANK, w), shaped(NSTATE, w)),
        (lanes_of(XW, local), rows_of(w, at), whole(NSTATE, w), whole(8, w), whole(RANK, w), whole(NSTATE, w)),
        [
            sub,
            sub,
            sub,
            sub,
            pltpu.VMEM((CH // SUB, SPAN, w), f32),
            pltpu.VMEM(((CH + 1) * NSTATE, w), f32),
            pltpu.VMEM((SPAN, w), bf16),
            pltpu.VMEM((SPAN, w), bf16),
            pltpu.VMEM((CH, SPAN), bf16),
            pltpu.VMEM((CH, SPAN), bf16),
            pltpu.VMEM((CH, SPAN), bf16),
            pltpu.VMEM((CH, w), f32),
            pltpu.VMEM((CH, w), f32),
            pltpu.VMEM((CH, w), f32),
        ],
        11 * chunks,
        {11 + k: 1 + k for k in range(len(kept))},
    )


def run_conv_backward(first, chunks, inner, inv, tail, conv, xproj, dxc, dxdbl, follow, sums, kept=()):
    w = inner.shape[1]
    at = lambda i: first + chunks - 1 - i
    local = lambda i: chunks - 1 - i
    before = lambda i: (jnp.maximum(at(i) * (CH // 8) - 1, 0), 0)
    return call(
        functools.partial(conv_backward, len(kept), chunks, first),
        chunks,
        (inner, inner, inv, inv, tail, conv, xproj, dxc, dxdbl, follow, *sums, *kept),
        [
            rows_of(w, at),
            pl.BlockSpec((8, w), before),
            rows_of(1, at),
            pl.BlockSpec((8, 1), before),
            whole(8, w),
            whole(8, w),
            whole(XW, w),
            rows_of(w, at),
            lanes_of(XW, local),
            whole(8, w),
            whole(8, w),
            whole(XW, w),
        ]
        + [ANY] * len(kept),
        (shaped(SEQ, w, dtype=bf16), shaped(SEQ, 1), shaped(8, w), shaped(XW, w), shaped(8, w)),
        (rows_of(w, at), rows_of(1, at), whole(8, w), whole(XW, w), whole(8, w)),
        [pltpu.VMEM((CH + 8, w), f32), pltpu.VMEM((CH + 8, w), f32)],
        2 * chunks,
        {12 + k: k for k in range(len(kept))},
    )


MESH = pl.DeviceIdType.MESH
SLOTS = 4


def remote(src, dst, send, recv, device):
    return pltpu.make_async_remote_copy(src_ref=src, dst_ref=dst, send_sem=send, recv_sem=recv, device_id=device, device_id_type=MESH)


def xor_bit(a, b):
    return a + b - 2 * a * b


def token_pieces(c, local):
    cut = local - LC
    low = cut - LC
    if c == 0:
        return [(0, local, 0, 0)]
    if c == 1:
        return [(0, cut, 0, local), (cut, local, 1, 0)]
    if c == 2:
        return [(0, local, 1, LC)]
    return [(0, low, 1, LC + local), (low, cut, 0, LP), (cut, local, 1, LP)]


def gather_start(tokens, in_i, in_g, out_w, small, raw, wi, wg, wo, small_all, w_send, w_recv, t_send, t_recv, here):
    g, r, c = lax.axis_index("grp"), lax.axis_index("row"), lax.axis_index("col")
    x, core = g // 2, g % 2
    local = tokens.shape[0]
    odd = c % 2
    same_half = xor_bit(r, odd)
    same_col = 2 * same_half + c // 2
    other_col = 2 * (1 - same_half) + c // 2
    alone = same_col == c
    gx = (1 - x) * 2 + core
    gc = x * 2 + 1 - core
    gxc = (1 - x) * 2 + 1 - core

    barrier = pltpu.get_barrier_semaphore()
    for dr in range(2):
        for dc in range(4):
            if dr or dc:
                pl.semaphore_signal(barrier, inc=1, device_id=(g, (r + dr) % 2, (c + dc) % 4), device_id_type=MESH)
    pl.semaphore_signal(barrier, inc=1, device_id=(gx, r, c), device_id_type=MESH)
    pl.semaphore_signal(barrier, inc=1, device_id=(gc, r, c), device_id_type=MESH)
    pl.semaphore_wait(barrier, 9)

    natural = lambda k, d: 2 * (g, gx, gc, gxc)[k] + d
    relative = lambda k, d: 2 * k + d
    origin = (r, 1 - r)
    by_row = lambda k, d: origin[d] * 4 + (g, gx, gc, gxc)[k]
    weights = [(small, small_all, by_row), (in_i, wi, natural), (in_g, wg, natural), (out_w, wo, relative)]

    def first_hop(n, d):
        src, dst, slot = weights[n]
        if slot is by_row:
            at = r * 4 + g
        else:
            at = slot(0, d)
        device = (g, r, same_col) if d == 0 else (g, 1 - r, other_col)
        return remote(src, dst.at[at], w_send.at[n, d], w_recv.at[n, d], device)

    def hop(n, d, k, device, came):
        src, dst, slot = weights[n]
        at = slot(k, d)
        to = relative(came, d) if slot is relative else at
        i = (0, 2, 4, 6)[came] + d
        return remote(dst.at[at], dst.at[to], w_send.at[n, i], w_recv.at[n, i], device)

    def begin(n):
        src, dst, slot = weights[n]

        @pl.when(alone)
        def _():
            pltpu.make_async_copy(src, dst.at[by_row(0, 0) if slot is by_row else slot(0, 0)], here.at[n]).start()

        @pl.when(jnp.logical_not(alone))
        def _():
            first_hop(n, 0).start()

        first_hop(n, 1).start()

    def arrived_first(n, d):
        src, dst, slot = weights[n]
        if d == 0:

            @pl.when(alone)
            def _():
                pltpu.make_async_copy(src, dst.at[by_row(0, 0) if slot is by_row else slot(0, 0)], here.at[n]).wait()

            @pl.when(jnp.logical_not(alone))
            def _():
                first_hop(n, 0).wait_recv()
        else:
            first_hop(n, 1).wait_recv()

    x_dev, core_dev = (gx, r, c), (gc, r, c)

    def forward(n):
        for d in range(2):
            arrived_first(n, d)
            hop(n, d, 0, x_dev, 1).start()
            hop(n, d, 0, core_dev, 2).start()

    def forward_again(n):
        for d in range(2):
            hop(n, d, 0, x_dev, 1).wait_recv()
            hop(n, d, 1, core_dev, 3).start()

    def token_copies(k):
        copies, mine = [], []
        for a, b, s, at in token_pieces(k, local):
            for dr in range(2):
                for dc in range(2):
                    target = 2 * s + dc
                    dst = raw.at[dr, pl.ds(at, b - a)]
                    src = tokens.at[pl.ds(a, b - a)]
                    if dr == 0 and target == k:
                        mine.append(pltpu.make_async_copy(src, dst, here.at[4 + len(mine)]))
                    else:
                        device = (g, r if dr == 0 else 1 - r, target)
                        copies.append(remote(src, dst, t_send.at[len(copies)], t_recv.at[dr], device))
        return copies, mine

    begin(0)
    begin(1)
    for k in range(4):

        @pl.when(c == k)
        def _(k=k):
            copies, mine = token_copies(k)
            for copy in mine + copies:
                copy.start()

    begin(2)
    begin(3)
    for n in range(4):
        forward(n)
    for n in range(4):
        forward_again(n)
    for k in range(4):

        @pl.when(c == k)
        def _(k=k):
            copies, mine = token_copies(k)
            held = sum(b - a for a, b, s, at in token_pieces(k, local) if s == k // 2)
            rest = raw.at[0, pl.ds(0, SEQ - held)]
            pltpu.make_async_copy(rest, rest, t_recv.at[0]).wait()
            pltpu.make_async_copy(raw.at[1], raw.at[1], t_recv.at[1]).wait()
            for copy in mine:
                copy.wait()
            for copy in copies:
                copy.wait_send()

    for n in range(4):
        for d in range(2):
            hop(n, d, 0, core_dev, 2).wait_recv()
            hop(n, d, 1, core_dev, 3).wait_recv()
            hop(n, d, 0, x_dev, 1).wait_send()
            hop(n, d, 0, core_dev, 2).wait_send()
            hop(n, d, 1, core_dev, 3).wait_send()

        @pl.when(jnp.logical_not(alone))
        def _(n=n):
            first_hop(n, 0).wait_send()

        first_hop(n, 1).wait_send()


def run_gather_start(tokens, in_i, in_g, out_w, small):
    rows, width = tokens.shape
    return pl.pallas_call(
        gather_start,
        in_specs=[ANY] * 5,
        out_specs=[ANY] * 5,
        out_shape=(
            shaped(2, SEQ, width, dtype=bf16),
            shaped(8, *in_i.shape, dtype=bf16),
            shaped(8, *in_g.shape, dtype=bf16),
            shaped(8, *out_w.shape, dtype=bf16),
            shaped(8, *small.shape, dtype=bf16),
        ),
        scratch_shapes=[
            pltpu.SemaphoreType.DMA((4, 8)),
            pltpu.SemaphoreType.DMA((4, 8)),
            pltpu.SemaphoreType.DMA((12,)),
            pltpu.SemaphoreType.DMA((2,)),
            pltpu.SemaphoreType.DMA((6,)),
        ],
        compiler_params=pltpu.CompilerParams(collective_id=0, has_side_effects=True, vmem_limit_bytes=VMEM_LIMIT),
    )(tokens, in_i, in_g, out_w, small)


def project_first(raw_ref, gain_ref, w_ref, normed_ref, inv_ref, out_ref):
    low = raw_ref[0].astype(f32)
    high = raw_ref[1].astype(f32)
    squares = jnp.sum(low * low + high * high, axis=1, keepdims=True)
    inv_ref[...] = lax.rsqrt(squares / D + eps)
    low = (low * gain_ref[0:1]).astype(bf16)
    high = (high * gain_ref[1:2]).astype(bf16)
    normed_ref[0] = low
    normed_ref[1] = high
    n = w_ref.shape[2]
    for k in range(SLOTS):
        out_ref[:, k * n : (k + 1) * n] = dot_nn(low, w_ref[2 * k]) + dot_nn(high, w_ref[2 * k + 1])


def project_second(normed_ref, w_ref, out_ref):
    n = w_ref.shape[2]
    for k in range(SLOTS):
        out_ref[:, k * n : (k + 1) * n] = dot_nn(normed_ref[0], w_ref[2 * k]) + dot_nn(normed_ref[1], w_ref[2 * k + 1])


def split_rows(width, at):
    return pl.BlockSpec((2, CH, width), lambda i: (0, at(i), 0))


def run_project_first(raw, gain, w):
    width = raw.shape[2]
    at = lambda i: i
    n = SLOTS * w.shape[2]
    return call(
        project_first,
        NCH,
        (raw, gain, w),
        [split_rows(width, at), whole(2, width), whole(*w.shape)],
        (shaped(2, SEQ, width, dtype=bf16), shaped(SEQ, 1), shaped(SEQ, n)),
        (split_rows(width, at), rows_of(1, at), rows_of(n, at)),
        [],
        9,
    )


def run_project_second(normed, w):
    width = normed.shape[2]
    at = lambda i: i
    n = SLOTS * w.shape[2]
    return call(
        project_second,
        NCH,
        (normed, w),
        [split_rows(width, at), whole(*w.shape)],
        shaped(SEQ, n),
        rows_of(n, at),
        [],
        7,
    )


def gate_backward(cot_ref, wo_ref, gate_ref, yfull_ref, inv_ref, dy_ref, dproj_ref, dscale_ref):
    n = wo_ref.shape[2]
    d_gated = jnp.zeros(dy_ref.shape, f32)
    for k in range(SLOTS):
        for d in range(2):
            d_gated = d_gated + dot_nt(cot_ref[d, :, k * n : (k + 1) * n], wo_ref[2 * k + d])
    gate_in = gate_ref[...]
    inv = inv_ref[...]
    gate = inv * gate_in
    sig = jax.nn.sigmoid(gate)
    dy_ref[...] = d_gated * (gate * sig)
    d_gate = d_gated * yfull_ref[...].astype(f32) * (sig * (1.0 + gate * (1.0 - sig)))
    dproj_ref[...] = (inv * d_gate).astype(bf16)
    dscale_ref[...] = jnp.sum(d_gate * gate_in, axis=1, keepdims=True)


def run_gate_backward(cot, wo, gate_in, yfull, inv):
    width = cot.shape[2]
    w = gate_in.shape[1]
    at = lambda i: i
    return call(
        gate_backward,
        NCH,
        (cot, wo, gate_in, yfull, inv),
        [split_rows(width, at), whole(*wo.shape), rows_of(w, at), rows_of(w, at), rows_of(1, at)],
        (shaped(SEQ, w), shaped(SEQ, w, dtype=bf16), shaped(SEQ, 1)),
        (rows_of(w, at), rows_of(w, at), rows_of(1, at)),
        [],
        9,
    )


def branch_forward(gated_ref, wo_ref, own_ref, oth_ref):
    n = wo_ref.shape[2]
    for k in range(SLOTS):
        own_ref[:, k * n : (k + 1) * n] = dot_nn(gated_ref[...], wo_ref[2 * k])
        oth_ref[:, k * n : (k + 1) * n] = dot_nn(gated_ref[...], wo_ref[2 * k + 1]).astype(bf16)


def run_branch(gated, wo):
    w = gated.shape[1]
    at = lambda i: i
    n = SLOTS * wo.shape[2]
    return call(
        branch_forward,
        NCH,
        (gated, wo),
        [rows_of(w, at), whole(*wo.shape)],
        (shaped(SEQ, n), shaped(SEQ, n, dtype=bf16)),
        (rows_of(n, at), rows_of(n, at)),
        [],
        7,
    )


def normed_backward(inner_ref, gate_ref, wi_ref, wg_ref, own_ref, oth_ref):
    n = wi_ref.shape[2]
    for d, out_ref in ((1, oth_ref), (0, own_ref)):
        total = jnp.zeros(out_ref.shape, f32)
        for k in range(SLOTS):
            total = total + dot_nt(inner_ref[:, k * n : (k + 1) * n], wi_ref[2 * k + d])
            total = total + dot_nt(gate_ref[:, k * n : (k + 1) * n], wg_ref[2 * k + d])
        out_ref[...] = total.astype(out_ref.dtype)


def run_normed_backward(d_inner, d_gate, wi, wg):
    w = d_inner.shape[1]
    width = wi.shape[1]
    at = lambda i: i
    return call(
        normed_backward,
        NCH,
        (d_inner, d_gate, wi, wg),
        [rows_of(w, at), rows_of(w, at), whole(*wi.shape), whole(*wg.shape)],
        (shaped(SEQ, width), shaped(SEQ, width, dtype=bf16)),
        (rows_of(width, at), rows_of(width, at)),
        [],
        12,
    )


def per_device(
    tokens,
    gain,
    in_proj,
    conv_weight,
    conv_bias,
    x_proj,
    dt_proj,
    dt_bias,
    a_log,
    d_skip,
    out_proj,
    table,
    cotangent,
):
    row = lax.axis_index("row")
    col = lax.axis_index("col")
    grp = lax.axis_index("grp")
    low_row = row == 0
    low_pair = col % 2 == 0
    half = col // 2
    places = [(r, c) for r in range(2) for c in range(4)]
    quick = lax.axis_size("grp") == 4

    def spot(r, c):
        return r * 4 + c

    def send(v, pairs):
        return lax.ppermute(v, ("row", "col"), [(spot(*a), spot(*b)) for a, b in pairs])

    def swap(v):
        return send(v, [((r, c), (1 - r, c)) for r, c in places])

    def pair(v):
        return send(v, [((r, c), (r, c ^ 1)) for r, c in places])

    def across(v):
        return send(v, [((r, c), (1 - r, c ^ 2)) for r, c in places])

    def quarter_spot(q, s):
        return ((q & 1) ^ s, 2 * s + (q >> 1))

    same = [((r, q), quarter_spot(q, r ^ (q & 1))) for r, q in places]
    other = [((r, q), quarter_spot(q, 1 ^ r ^ (q & 1))) for r, q in places]
    spread = [((r, q), quarter_spot(q, r)) for r, q in places]

    def back(pairs):
        return [(b, a) for a, b in pairs]

    def flip(v, bit):
        return lax.ppermute(v, "grp", [(g, g ^ bit) for g in range(4)])

    def scatter_grp(v, axis):
        return lax.psum_scatter(v, "grp", scatter_dimension=axis, tiled=True)

    def exchange_blocks(p):
        p = [jnp.where(grp < 2, p[k], p[k ^ 2]) for k in range(4)]
        return [jnp.where(grp % 2 == 0, p[k], p[k ^ 1]) for k in range(4)]

    def to_relative(v, axis):
        if not quick:
            return v
        p = exchange_blocks(jnp.split(v, 4, axis=axis))
        return jnp.concatenate([p[0], p[2], p[1], p[3]], axis=axis)

    def from_relative(v, axis):
        if not quick:
            return v
        p = jnp.split(v, 4, axis=axis)
        return jnp.concatenate(exchange_blocks([p[0], p[2], p[1], p[3]]), axis=axis)

    def by_pair(own, paired):
        return jnp.where(low_pair, own, paired), jnp.where(low_pair, paired, own)

    local = tokens.shape[0]
    cut = local - LC
    tail_at = cut - LC

    def to_sequences(v):
        got = send(jnp.where(col == 3, v[tail_at:cut], v[cut:]), [((r, a), (r, b)) for r in range(2) for a, b in ((1, 2), (2, 3), (3, 1))])
        low = jnp.concatenate([v[:cut], jnp.where(col == 0, v[cut:], got)], axis=0)
        two = jnp.concatenate([got, v[:cut]], axis=0)
        three = jnp.concatenate([got, v[:tail_at], v[cut:]], axis=0)
        return jnp.where(col < 2, low, jnp.where(col == 2, two, three))

    def from_sequences(v):
        got = send(jnp.where(col == 1, v[cut:], v[:LC]), [((r, b), (r, a)) for r in range(2) for a, b in ((1, 2), (2, 3), (3, 1))])
        low = jnp.concatenate([v[:cut], jnp.where(col == 0, v[cut:], got)], axis=0)
        two = jnp.concatenate([v[LC:], got], axis=0)
        three = jnp.concatenate([v[LC:cut], got, v[cut:]], axis=0)
        return jnp.where(col < 2, low, jnp.where(col == 2, two, three))

    def gather_quad(v):
        swapped = swap(v)
        paired = pair(v)
        mid = v.shape[0] // 2
        diagonal = jnp.concatenate([pair(swapped[:mid]), swap(paired[mid:])], axis=0)
        first_own, second_own = by_pair(v, paired)
        first_oth, second_oth = by_pair(swapped, diagonal)
        return jnp.stack([jnp.concatenate([first_own, second_own], axis=0), jnp.concatenate([first_oth, second_oth], axis=0)])

    def scatter_quad(own, oth):
        v = own + swap(oth.astype(bf16)).astype(f32)
        first, second = v[:local], v[local:]
        kept, sent = jnp.where(low_pair, first, second), jnp.where(low_pair, second, first)
        return kept + pair(sent.astype(bf16)).astype(f32)

    own_table = jnp.where(half == 0, table[0], table[1])
    oth_table = jnp.where(half == 0, table[1], table[0])
    resumes_own = own_table == half
    resumed_by_other = oth_table == half

    small = jnp.concatenate([conv_weight, conv_bias[None], dt_bias[None], d_skip[None], a_log, dt_proj, x_proj.T], axis=0)
    lanes = small.shape[1]
    used = small.shape[0]
    gain_rows = gain.size // lanes
    width = tokens.shape[1]
    if quick:
        small = jnp.concatenate([small, gain.reshape(gain_rows, lanes)], axis=0)
        small = jnp.pad(small, ((0, -small.shape[0] % 16), (0, 0)))
        raw, wi, wg, wo, small = run_gather_start(tokens, in_proj[:, 0], in_proj[:, 1], out_proj, small)
        gain_all = small[:, used : used + gain_rows].reshape(2, width).astype(f32)
        small = jnp.swapaxes(small, 0, 1).reshape(small.shape[1], 8 * lanes)
    else:
        raw = gather_quad(to_sequences(tokens))

        def weight(shard):
            v = lax.all_gather(jnp.stack([send(shard, same), send(shard, other)]), "grp", axis=2, tiled=True)
            v = v.reshape(2, v.shape[1], SLOTS, v.shape[2] // SLOTS)
            return jnp.transpose(v, (2, 0, 1, 3)).reshape(2 * SLOTS, v.shape[1], v.shape[3])

        wi, wg, wo = weight(in_proj[:, 0]), weight(in_proj[:, 1]), weight(out_proj)
        small = send(lax.all_gather(small, ("row", "grp"), axis=1, tiled=True), spread)
        gain_all = lax.all_gather(gain, ("row", "grp"), axis=0, tiled=True).astype(f32).reshape(2, width)
    w = small.shape[1]
    zero_row = jnp.zeros((1, w), f32)
    conv = jnp.concatenate([small[0:5].astype(f32)] + [zero_row] * 3, axis=0)
    vec = jnp.concatenate([small[5:7].astype(f32)] + [zero_row] * 6, axis=0)
    rate = -jnp.exp(small[7 : 7 + NSTATE].astype(f32))
    dtp = small[7 + NSTATE : 7 + NSTATE + RANK]
    xproj = small[7 + NSTATE + RANK : 7 + NSTATE + RANK + XW]
    gain_own = jnp.where(low_row, gain_all[0], gain_all[1])
    gain_two = jnp.stack([gain_own, jnp.where(low_row, gain_all[1], gain_all[0])])

    normed, inv, inner = run_project_first(raw, gain_two, wi)
    tail_own = (inv * inner)[LP - 8 : LP]
    tail = jnp.where(resumes_own, tail_own, across(tail_own))
    gate_in = run_project_second(normed, wg)
    xconv, xdbl_part = run_conv_forward(inner, inv, tail, conv, xproj)

    low_part, map_part = xdbl_part[:RANK], xdbl_part[RANK:]
    for move in (swap, pair):
        low_part = low_part + move(low_part.astype(bf16)).astype(f32)
        map_part = map_part + move(map_part)
    xdbl = jnp.concatenate([low_part, map_part], axis=0)

    zero_state = jnp.zeros((NSTATE, w), f32)
    *kept, final = run_scan_forward(0, PC, xdbl, xconv, gate_in, inv, dtp, vec, rate, zero_state)
    resumed = jnp.where(resumes_own, final, across(final))
    gated, yfull, starts, _ = run_scan_forward(PC, NCH - PC, xdbl, xconv, gate_in, inv, dtp, vec, rate, resumed, kept)

    cot = gather_quad(to_sequences(to_relative(cotangent, 1)))
    d_yfull, d_gate_proj, gate_scale = run_gate_backward(cot, wo, gate_in, yfull, inv)

    branch = scatter_quad(*run_branch(gated, wo))
    output = (tokens.astype(f32) + from_sequences(from_relative(branch, 1).astype(bf16)).astype(f32)).astype(bf16)

    def collect(v):
        return send(v[0].astype(bf16), back(same)).astype(f32) + send(v[1].astype(bf16), back(other)).astype(f32)

    def rows_product(a, b, out_dtype):
        return lax.dot_general(a, b, (((1,), (0,)), ((), ())), preferred_element_type=f32).astype(out_dtype)

    if quick:
        n = width // 4
        part = [[dot_tn(gated, cot[d, :, k * 2 * n : (k + 1) * 2 * n]) for k in range(2)] for d in range(2)]
        part = [part[d][0] + flip(part[d][1].astype(bf16), 1).astype(f32) for d in range(2)]
        part = [part[d][:, :n] + flip(part[d][:, n:].astype(bf16), 2).astype(f32) for d in range(2)]
    else:
        part = [scatter_grp(dot_tn(gated, cot[d]), 1) for d in range(2)]
    out_grad = collect(part)

    mid = PC // 2
    sums = (zero_state, jnp.zeros((8, w), f32), jnp.zeros((RANK, w), f32))
    scan = functools.partial(run_scan_backward, xdbl=xdbl, xconv=xconv, dy=d_yfull, dtp=dtp, vec=vec, rate=rate, starts=starts)
    dx_c, dxc, *sums, g_first = scan(PC, NCH - PC, carry=zero_state, sums=sums)
    g_into = jnp.where(resumes_own, g_first, 0.0) + jnp.where(resumed_by_other, across(g_first), 0.0)
    dx_hi, dxc, *sums, g_first = scan(mid, PC - mid, carry=g_into, sums=sums, kept=(dxc,))

    def sum_quad(v):
        for move in (swap, pair):
            v = v + move(v.astype(bf16)).astype(f32)
        return v

    late = sum_quad(jnp.concatenate([dx_hi, dx_c], axis=1))
    dx_lo, dxc, *sums, _ = scan(0, mid, carry=g_first, sums=sums, kept=(dxc,))
    alog_grad, scan_sums, dtp_grad = sums
    early = sum_quad(dx_lo)

    conv_back = functools.partial(run_conv_backward, inner=inner, inv=inv, tail=tail, conv=conv, xproj=xproj, dxc=dxc)
    sums = (jnp.zeros((8, w), f32), jnp.zeros((XW, w), f32))
    zero_head = jnp.zeros((8, w), f32)
    hi_width = (PC - mid) * CH
    dp, ds, *sums, head = conv_back(PC, NCH - PC, dxdbl=late[:, hi_width:], follow=zero_head, sums=sums)
    follow = jnp.where(resumes_own, head, 0.0) + jnp.where(resumed_by_other, across(head), 0.0)
    dp, ds, *sums, head = conv_back(mid, PC - mid, dxdbl=late[:, :hi_width], follow=follow, sums=sums, kept=(dp, ds))
    d_inner_proj, inner_scale, conv_sums, xproj_grad, _ = conv_back(0, mid, dxdbl=early, follow=head, sums=sums, kept=(dp, ds))

    d_normed = scatter_quad(*run_normed_backward(d_inner_proj, d_gate_proj, wi, wg))
    scale = gate_scale + inner_scale
    scale = scale + swap(scale)
    first, second = scale[:local], scale[local:]
    scale_own = jnp.where(low_pair, first, second) + pair(jnp.where(low_pair, second, first))
    inv_own = jnp.where(low_pair, inv[:local], inv[local:])
    fixed_wide = jnp.where(low_pair, raw[0, :local], raw[0, local:]).astype(f32)
    gain_part = jnp.sum(d_normed * fixed_wide, axis=0)
    pulled = d_normed * gain_own - (scale_own * inv_own * inv_own * inv_own / D) * fixed_wide
    input_grad = (cotangent.astype(f32) + from_sequences(pulled.astype(bf16)).astype(f32)).astype(bf16)

    def in_grad(d_proj):
        if not quick:
            return collect([scatter_grp(dot_tn(normed[d], d_proj), 1) for d in range(2)])
        n = w // 4
        blocks = [d_proj[:, k * n : (k + 1) * n] for k in range(4)]
        low_core = grp % 2 == 0
        kept = jnp.concatenate([jnp.where(low_core, blocks[0], blocks[1]), jnp.where(low_core, blocks[2], blocks[3])], axis=1)
        sent = jnp.concatenate([jnp.where(low_core, blocks[1], blocks[0]), jnp.where(low_core, blocks[3], blocks[2])], axis=1)
        part = rows_product(normed, kept, f32) + flip(rows_product(normed, sent, bf16), 1).astype(f32)
        low, high = part[:, :, :n], part[:, :, n:]
        part = jnp.where(grp < 2, low, high) + flip(jnp.where(grp < 2, high, low).astype(bf16), 2).astype(f32)
        return collect(part)

    in_grads = jnp.stack([in_grad(d_inner_proj), in_grad(d_gate_proj)], axis=1)
    gain_grad = lax.psum_scatter(lax.psum(gain_part, "col"), "grp", scatter_dimension=0, tiled=True)
    small_grad = jnp.concatenate([conv_sums[0:5], scan_sums[0:2], alog_grad * rate, dtp_grad, xproj_grad], axis=0)
    small_grad = jnp.pad(small_grad, ((0, -small_grad.shape[0] % 8), (0, 0)))
    small_grad = send(small_grad, back(spread))
    small_grad = lax.psum_scatter(small_grad, ("row", "grp"), scatter_dimension=1, tiled=True)
    return (
        output,
        input_grad,
        gain_grad,
        in_grads,
        small_grad[0:4],
        small_grad[4],
        small_grad[7 + NSTATE + RANK : 7 + NSTATE + RANK + XW].T,
        small_grad[7 + NSTATE : 7 + NSTATE + RANK],
        small_grad[5],
        small_grad[7 : 7 + NSTATE],
        small_grad[6],
        out_grad,
    )


def solution(mesh):
    placed = (
        P(("grp", "col"), "row"),
        P(("row", "grp")),
        P("row", None, ("col", "grp")),
        P(None, ("col", "row", "grp")),
        P(("col", "row", "grp")),
        P(("col", "row", "grp"), None),
        P(None, ("col", "row", "grp")),
        P(("col", "row", "grp")),
        P(None, ("col", "row", "grp")),
        P(("col", "row", "grp")),
        P("col", ("row", "grp")),
        P("grp"),
        P(("grp", "col"), "row"),
    )
    return jax.shard_map(
        per_device,
        mesh=mesh,
        in_specs=placed,
        out_specs=(
            P(("grp", "col"), "row"),
            P(("grp", "col"), "row"),
            P(("row", "grp")),
            P("row", None, ("col", "grp")),
            P(None, ("col", "row", "grp")),
            P(("col", "row", "grp")),
            P(("col", "row", "grp"), None),
            P(None, ("col", "row", "grp")),
            P(("col", "row", "grp")),
            P(None, ("col", "row", "grp")),
            P(("col", "row", "grp")),
            P("col", ("row", "grp")),
        ),
        check_vma=False,
    )
```

time: 3550 us -> 760 us (0.21); the launches traced: 3490 us -> 750 us
  other arithmetic: 1250 us -> 57.6 us
  waiting for transfers between devices: 1040 us -> 124 us
  local copies, waits for them, and re-layouts: 887 us -> 39 us
  Pallas kernels: 0 us -> 404 us
  blocking collectives: 186 us -> 12.7 us
  matrix products: 99.1 us -> 32.7 us
  starting transfers between devices: 0.69 us -> 61.2 us
    reduce_scatter x9 -> x1, waiting for transfers between devices: 607 us -> 0.02 us  [per_device(): lax.psum_scatter(small_grad, ('row', 'grp'), scatter_dimension=1, tiled=T...]
    mul x580 -> x0, local copies, waits for them, and re-layouts: 476 us -> none  [the longest x128 197 us: retreat(): grad_sum = read_t[:, :, None] * grad_t[:, None, :] + carried]
    pallas_call x0 -> x15, Pallas kernels: none -> 404 us  [the longest x14 262 us: call(): pl.pallas_call(body, grid=(chunks,), in_specs=in_specs, out_specs=out_spe...]
    add x445 -> x13, other arithmetic: 416 us -> 14.3 us  [the longest x2 5.1 us: scatter_quad(): v = own + swap(oth.astype(bf16)).astype(f32)]
    all_gather x6 -> x0, waiting for transfers between devices: 355 us -> none  [the longest x1 108 us: per_device(): d_proj_full = lax.all_gather(d_proj, 'row', axis=2, tiled=True)]
    reduce_sum x100 -> x1, other arithmetic: 333 us -> 4.29 us  [per_device(): gain_part = jnp.sum(d_normed * fixed_wide, axis=0)]
    mul x227 -> x2, other arithmetic: 263 us -> 2.33 us  [the longest x1 1.49 us: per_device(): alog_grad * rate]
    dynamic_update_slice x481 -> x0, local copies, waits for them, and re-layouts: 185 us -> none  [the longest x128 80.9 us: group_grads(): lax.scan(descend, incoming, inputs + (read_steps, grad_steps, previous),...]
  transfers between devices with their start and end apart: 17 -> 41, of which waited for: 16 -> 17; matrix products, arithmetic and copies ran while one was open for 4% -> 16% of each run, Pallas kernels for 0% -> 54%
where the time goes in v1:
time: 760 us; the launch traced here: 750 us
  Pallas kernels  404 us (53%)
  waiting for transfers between devices  124 us (16%)
  starting transfers between devices  61.2 us (8%)
  other arithmetic  57.6 us (8%)
  local copies, waits for them, and re-layouts  39 us (5%)
  matrix products  32.7 us (4%)
  between operations  18.7 us (2%)
  blocking collectives  12.7 us (2%)
    pallas_call x14, Pallas kernels, call(): pl.pallas_call(body, grid=(chunks,), in_specs=in_specs, out_specs=out_spe...  262 us
    pallas_call x1, Pallas kernels, run_gather_start(): pl.pallas_call(gather_start, in_specs=[ANY] * 5, out_specs=[ANY] * 5, out...  142 us
    ppermute x32, waiting for transfers between devices, send(): lax.ppermute(v, ('row', 'col'), [(spot(*a), spot(*b)) for a, b in pairs])  108 us
    ppermute x32, starting transfers between devices, send(): lax.ppermute(v, ('row', 'col'), [(spot(*a), spot(*b)) for a, b in pairs])  56.6 us
    dot_general x4, matrix products, rows_product(): lax.dot_general(a, b, (((1,), (0,)), ((), ())), preferred_element_type=f32)  20.4 us
    ppermute x8, waiting for transfers between devices, flip(): return lax.ppermute(v, 'grp', [(g, g ^ bit) for g in range(4)])  16 us
  transfers between devices with their start and end apart: 41, of which 17 were waited for; matrix products, arithmetic and copies ran while one was open for 16% of the time, Pallas kernels for 54%

profile of v1, /device:TPU:14, one launch (start us, length us, event | category | flops | bytes accessed | tf_op | source)
XLA Modules:
  0.0 750.2 jit_solution(6346066929969710939)
XLA Ops:
  9.5 3.5 collective-permute-start.9
  17.2 141.9 %shard_map.220 = (bf16[2,1152,1024]{2,1,0:T(8,128)(2,1)}, bf16[8,1024,256]{2,1,0:T(8,128)(2,1)}, bf16[8,1024,256]{2,1,0:T(8,128)(2,1)}, bf16[8,1024,256]{2,1,0:T(8,128)(2,1)}, bf16[8,320,128]{2,1,0:T(8,128)(2,1)}) custom-call(bf16[576,1024]{1,0:T(8,128)(2,1)} %tokens.1, bf16[1024,256]{1,0:T(8,128)(2,1)} %get-tuple-element.204.in_i, ...), custom_call_target="tpu_custom_call" | custom-call | tf_op jit(solution)/shard_map/pallas_call | solution.py:561
  160.6 13.4 %shard_map.221 = (bf16[2,1152,1024]{2,1,0:T(8,128)(2,1)}, f32[1152,1]{1,0:T(8,128)}, f32[1152,1024]{1,0:T(8,128)}) custom-call(bf16[2,1152,1024]{2,1,0:T(8,128)(2,1)} %get-tuple-element.67.raw_ref, f32[2,1024]{1,0:T(2,128)} %pad_maximum_fusion.8.gain_ref, bf16[8,1024,256]{2,1,0:T(8,128)(2,1)} %get-tuple-element.69.w_ref.wi_ref), custom_call_target="tpu_custom_call" | custom-call | flops 8999999488 | bytes 1000000 | tf_op jit(solution)/shard_map/pallas_call | solution.py:244
  179.1 11.8 %shard_map.223.gate_ref = f32[1152,1024]{1,0:T(8,128)} custom-call(bf16[2,1152,1024]{2,1,0:T(8,128)(2,1)} %get-tuple-element.74.normed_ref, bf16[8,1024,256]{2,1,0:T(8,128)(2,1)} %get-tuple-element.75.w_ref.wg_ref), custom_call_target="tpu_custom_call" | custom-call | flops 7000000000 | bytes 1000000 | tf_op jit(solution)/shard_map/pallas_call | solution.py:244
  194.3 10.0 %shard_map.222 = (bf16[1152,1024]{1,0:T(8,128)(2,1)}, f32[160,1152]{1,0:T(8,128)}) custom-call(f32[1152,1024]{1,0:T(8,128)} %get-tuple-element.70.inner_ref.halo_ref, f32[1152,1]{1,0:T(8,128)} %get-tuple-element.71.inv_ref.halo_inv_ref, f32[8,1024]{1,0:T(8,128)} %broadcast_select_fusion.24.tail_ref, f32[8,1024]{1,0:T(8,128)} %pad_convert_fusion.1.conv_ref, ...), custom_call_target="tpu_custom_call" | custom-call | flops 12000000000 | bytes 1000000 | tf_op jit(solution)/shard_map/pallas_call | solution.py:244
  208.9 3.9 collective-permute-done.3
  213.9 4.7 collective-permute-done.1
  223.6 5.0 collective-permute-done.2
  230.2 33.8 %shard_map.224 = (bf16[1152,1024]{1,0:T(8,128)(2,1)}, bf16[1152,1024]{1,0:T(8,128)(2,1)}, f32[9,16,1024]{2,1,0:T(8,128)}, f32[16,1024]{1,0:T(8,128)}) custom-call(f32[160,1152]{1,0:T(8,128)} %pad_maximum_fusion.6.xdbl_ref, bf16[1152,1024]{1,0:T(8,128)(2,1)} %get-tuple-element.73.xconv_ref, f32[1152,1024]{1,0:T(8,128)} %shard_map.223.gate_ref, ...), custom_call_target="tpu_custom_call" | custom-call | flops 40000000000 | bytes 1000000 | tf_op jit(solution)/shard_map/pallas_call | solution.py:244
  264.1 3.6 collective-permute-start.5
  271.9 6.0 shard_map.225
  279.4 11.5 %shard_map.226 = (f32[1152,1024]{1,0:T(8,128)}, bf16[1152,1024]{1,0:T(8,128)(2,1)}) custom-call(bf16[1152,1024]{1,0:T(8,128)(2,1)} %get-tuple-element.80.gated_ref, bf16[8,1024,256]{2,1,0:T(8,128)(2,1)} %get-tuple-element.81.wo_ref), custom_call_target="tpu_custom_call" | custom-call | flops 7000000000 | bytes 1000000 | tf_op jit(solution)/shard_map/pallas_call | solution.py:244
  304.3 18.9 %shard_map.227 = (f32[1152,1024]{1,0:T(8,128)}, bf16[1152,1024]{1,0:T(8,128)(2,1)}, f32[1152,1]{1,0:T(8,128)}) custom-call(bf16[2,1152,1024]{2,1,0:T(8,128)(2,1)} %pad_maximum_fusion.cot_ref, bf16[8,1024,256]{2,1,0:T(8,128)(2,1)} %get-tuple-element.81.wo_ref, f32[1152,1024]{1,0:T(8,128)} %shard_map.223.gate_ref, ...), custom_call_target="tpu_custom_call" | custom-call | flops 8999999488 | bytes 1000000 | tf_op jit(solution)/shard_map/pallas_call | solution.py:244
  324.7 13.2 %shard_map.228 = (f32[160,128]{1,0:T(8,128)}, f32[1152,1024]{1,0:T(8,128)}, f32[16,1024]{1,0:T(8,128)}, f32[8,1024]{1,0:T(8,128)}, f32[128,1024]{1,0:T(8,128)}, /*index=5*/f32[16,1024]{1,0:T(8,128)}) custom-call(f32[160,1152]{1,0:T(8,128)} %pad_maximum_fusion.6.xdbl_ref, bf16[1152,1024]{1,0:T(8,128)(2,1)} %get-tuple-element.73.xconv_ref, ...), custom_call_target="tpu_custom_call" | custom-call | flops 11000000512 | bytes 1000000 | tf_op jit(solution)/shard_map/pallas_call | solution.py:244
  337.9 3.8 collective-permute-start.14
  343.0 4.4 convolution_convert_fusion
  348.0 45.0 %shard_map.229 = (f32[160,512]{1,0:T(8,128)}, f32[1152,1024]{1,0:T(8,128)}, f32[16,1024]{1,0:T(8,128)}, f32[8,1024]{1,0:T(8,128)}, f32[128,1024]{1,0:T(8,128)}, /*index=5*/f32[16,1024]{1,0:T(8,128)}) custom-call(f32[160,1152]{1,0:T(8,128)} %pad_maximum_fusion.6.xdbl_ref, ...), custom_call_target="tpu_custom_call", output_to_operand_aliasing={{1}: (11, {})} | custom-call | flops 44000002048 | bytes 1000000 | tf_op jit(solution)/shard_map/pallas_call | solution.py:244
  394.2 44.9 %shard_map.230 = (f32[160,512]{1,0:T(8,128)}, f32[1152,1024]{1,0:T(8,128)}, f32[16,1024]{1,0:T(8,128)}, f32[8,1024]{1,0:T(8,128)}, f32[128,1024]{1,0:T(8,128)}, /*index=5*/f32[16,1024]{1,0:T(8,128)}) custom-call(f32[160,1152]{1,0:T(8,128)} %pad_maximum_fusion.6.xdbl_ref, ...), custom_call_target="tpu_custom_call", output_to_operand_aliasing={{1}: (11, {})} | custom-call | flops 44000002048 | bytes 1000000 | tf_op jit(solution)/shard_map/pallas_call | solution.py:244
  444.4 4.6 collective-permute-done.15
  452.0 3.9 collective-permute-done.18
  459.2 4.1 shard_map.231
  464.9 4.3 collective-permute-done.19
  470.7 9.7 %shard_map.232 = (bf16[1152,1024]{1,0:T(8,128)(2,1)}, f32[1152,1]{1,0:T(8,128)}, f32[8,1024]{1,0:T(8,128)}, f32[160,1024]{1,0:T(8,128)}, f32[8,1024]{1,0:T(8,128)}) custom-call(f32[1152,1024]{1,0:T(8,128)} %get-tuple-element.70.inner_ref.halo_ref, f32[1152,1024]{1,0:T(8,128)} %get-tuple-element.70.inner_ref.halo_ref, ...), custom_call_target="tpu_custom_call", output_to_operand_aliasing={{0}: (12, {}), {1}: (13, {})} | custom-call | flops 8000000000 | bytes 1000000 | tf_op jit(solution)/shard_map/pallas_call | solution.py:244
  480.3 9.5 %shard_map.233 = (bf16[1152,1024]{1,0:T(8,128)(2,1)}, f32[1152,1]{1,0:T(8,128)}, f32[8,1024]{1,0:T(8,128)}, f32[160,1024]{1,0:T(8,128)}, f32[8,1024]{1,0:T(8,128)}) custom-call(f32[1152,1024]{1,0:T(8,128)} %get-tuple-element.70.inner_ref.halo_ref, f32[1152,1024]{1,0:T(8,128)} %get-tuple-element.70.inner_ref.halo_ref, ...), custom_call_target="tpu_custom_call", output_to_operand_aliasing={{0}: (12, {}), {1}: (13, {})} | custom-call | flops 8000000000 | bytes 1000000 | tf_op jit(solution)/shard_map/pallas_call | solution.py:244
  492.6 29.9 %shard_map.234 = (f32[1152,1024]{1,0:T(8,128)}, bf16[1152,1024]{1,0:T(8,128)(2,1)}) custom-call(bf16[1152,1024]{1,0:T(8,128)(2,1)} %get-tuple-element.111.inner_ref, bf16[1152,1024]{1,0:T(8,128)(2,1)} %get-tuple-element.112.gate_ref, bf16[8,1024,256]{2,1,0:T(8,128)(2,1)} %get-tuple-element.69.w_ref.wi_ref, bf16[8,1024,256]{2,1,0:T(8,128)(2,1)} %get-tuple-element.75.w_ref.wg_ref), custom_call_target="tpu_custom_call" | custom-call | flops 12000000000 | bytes 1000000 | tf_op jit(solution)/shard_map/pallas_call | solution.py:244
  527.4 3.6 convert_add_fusion.7
  532.6 3.6 convert_add_fusion.6
  538.8 4.5 convolution_convert_fusion.1
  545.9 2.6 collective-permute-start.33
  557.7 4.4 collective-permute-start.39
  562.1 3.9 convert_add_fusion.1
  568.4 11.8 %collective-permute-done.33 = f32[312,1024]{1,0:T(8,128)} collective-permute-done((f32[312,1024]{1,0:T(8,128)S(1)}, f32[312,1024]{1,0:T(8,128)}, u32[]{:S(2)}, u32[]{:S(2)}) %collective-permute-start.33) | collective-permute-done | bytes 1277984 | tf_op jit(solution)/shard_map/ppermute | solution.py:748
  580.8 9.7 %collective-permute-done.36 = bf16[1024,256]{1,0:T(8,128)(2,1)} collective-permute-done((bf16[1024,256]{1,0:T(8,128)(2,1)}, bf16[1024,256]{1,0:T(8,128)(2,1)}, u32[]{:S(2)}, u32[]{:S(2)}) %collective-permute-start.36) | collective-permute-done | bytes 524320 | tf_op jit(solution)/shard_map/ppermute | solution.py:748
  593.1 4.5 collective-permute-done.39
  599.8 6.8 convert_add_fusion.2
  607.9 14.3 %collective-permute-done.7 = bf16[576,1024]{1,0:T(8,128)(2,1)S(1)} collective-permute-done((bf16[576,1024]{1,0:T(8,128)(2,1)S(1)}, bf16[576,1024]{1,0:T(8,128)(2,1)S(1)}, u32[]{:S(2)}, u32[]{:S(2)}) %collective-permute-start.7) | collective-permute-done | bytes 1179680 | tf_op jit(solution)/shard_map/ppermute | solution.py:748
  623.3 3.5 collective-permute-start.8
  627.0 6.1 collective-permute-done.8
  635.4 4.7 convert_add_fusion.3
  649.5 14.6 %collective-permute-done.26 = bf16[2,1024,256]{2,1,0:T(8,128)(2,1)S(1)} collective-permute-done((bf16[2,1024,256]{2,1,0:T(8,128)(2,1)S(1)}, bf16[2,1024,256]{2,1,0:T(8,128)(2,1)S(1)}, u32[]{:S(2)}, u32[]{:S(2)}) %collective-permute-start.26) | collective-permute-done | bytes 1048608 | tf_op jit(solution)/shard_map/ppermute | solution.py:770
  665.6 5.5 collective-permute-start.27
  671.1 13.8 %collective-permute-done.31 = bf16[1024,256]{1,0:T(8,128)(2,1)S(1)} collective-permute-done((bf16[1024,256]{1,0:T(8,128)(2,1)S(1)}, bf16[1024,256]{1,0:T(8,128)(2,1)S(1)}, u32[]{:S(2)}, u32[]{:S(2)}) %collective-permute-start.31) | collective-permute-done | bytes 524320 | tf_op jit(solution)/shard_map/ppermute | solution.py:748
  692.0 19.9 %collective-permute-done.21 = bf16[576,1024]{1,0:T(8,128)(2,1)S(1)} collective-permute-done((bf16[576,1024]{1,0:T(8,128)(2,1)S(1)}, bf16[576,1024]{1,0:T(8,128)(2,1)S(1)}, u32[]{:S(2)}, u32[]{:S(2)}) %collective-permute-start.21) | collective-permute-done | bytes 1179680 | tf_op jit(solution)/shard_map/ppermute | solution.py:748
  712.0 4.3 fusion.2
  716.3 7.2 collective-permute-start.24
  723.5 5.7 all-reduce.4
  729.3 7.1 psum.8
  738.1 2.9 copy.65
  (281 shorter events, 121.1 us)
Async XLA Ops:
  7.2 677.9 %reduce-scatter.2.cloned.1.call-start = ((), (), s32[]{:S(2)}) async-start(), calls=%async_computation.1 | async-start | bytes 1437696 | tf_op jit(solution)/shard_map/reduce_scatter | solution.py:957
  9.5 209.1 %collective-permute-start.9 = (bf16[128,1024]{1,0:T(8,128)(2,1)}, bf16[128,1024]{1,0:T(8,128)(2,1)}, u32[]{:S(2)}, u32[]{:S(2)}) collective-permute-start(bf16[128,1024]{1,0:T(8,128)(2,1)} %get-tuple-element.158), channel_id=1, source_target_pairs={{1,2},{2,3},{3,1},{5,6},{6,7},{7,5},{9,10},{10,11},{11,9},{13,14},... | collective-permute-start | bytes 786440 | tf_op jit(solution)/shard_map/ppermute | solution.py:748
  176.2 16.6 %collective-permute-start = (f32[8,1024]{1,0:T(8,128)S(1)}, f32[8,1024]{1,0:T(8,128)S(1)}, u32[]{:S(2)}, u32[]{:S(2)}) collective-permute-start(f32[8,1024]{1,0:T(8,128)S(1)} %slice_multiply_fusion), channel_id=1, source_target_pairs={{0,6},{1,7},{2,4},{3,5},{4,2},{5,3},{6,0},{7,1},{8,14},{9,15},{10,... | collective-permute-start | bytes 98312 | tf_op jit(solution)/shard_map/ppermute | solution.py:748
  205.9 7.0 collective-permute-start.3
  207.0 11.5 %collective-permute-start.1 = (bf16[128,1152]{1,0:T(8,128)(2,1)S(1)}, bf16[128,1152]{1,0:T(8,128)(2,1)S(1)}, u32[]{:S(2)}, u32[]{:S(2)}) collective-permute-start(bf16[128,1152]{1,0:T(8,128)(2,1)S(1)} %slice.494), channel_id=1, source_target_pairs={{0,4},{1,5},{2,6},{3,7},{4,0},{5,1},{6,2},{7,3},{8,12},{9,13},{10,... | collective-permute-start | bytes 884744 | tf_op jit(solution)/shard_map/ppermute | solution.py:748
  213.8 9.8 %collective-permute-start.4 = (f32[32,1152]{1,0:T(8,128)S(1)}, f32[32,1152]{1,0:T(8,128)S(1)}, u32[]{:S(2)}, u32[]{:S(2)}) collective-permute-start(f32[32,1152]{1,0:T(8,128)S(1)} %slice_add_fusion.2), channel_id=1, source_target_pairs={{0,1},{1,0},{2,3},{3,2},{4,5},{5,4},{6,7},{7,6},{8,9},{9,8},{10,11... | collective-permute-start | bytes 442376 | tf_op jit(solution)/shard_map/ppermute | solution.py:748
  218.6 10.0 %collective-permute-start.2 = (bf16[128,1152]{1,0:T(8,128)(2,1)S(1)}, bf16[128,1152]{1,0:T(8,128)(2,1)S(1)}, u32[]{:S(2)}, u32[]{:S(2)}) collective-permute-start(bf16[128,1152]{1,0:T(8,128)(2,1)S(1)} %fusion.18), channel_id=1, source_target_pairs={{0,1},{1,0},{2,3},{3,2},{4,5},{5,4},{6,7},{7,6},{8,9},{9,8},{10,11... | collective-permute-start | bytes 884744 | tf_op jit(solution)/shard_map/ppermute | solution.py:748
  221.3 56.6 %collective-permute-start.11 = (bf16[576,1024]{1,0:T(8,128)(2,1)S(1)}, bf16[576,1024]{1,0:T(8,128)(2,1)S(1)}, u32[]{:S(2)}, u32[]{:S(2)}) collective-permute-start(bf16[576,1024]{1,0:T(8,128)(2,1)S(1)} %fusion.4), channel_id=1, source_target_pairs={{0,4},{1,5},{2,6},{3,7},{4,0},{5,1},{6,2},{7,3},{8,12},{9,13},{10,... | collective-permute-start | bytes 3538952 | tf_op jit(solution)/shard_map/ppermute | solution.py:748
  221.6 56.4 %collective-permute-start.10 = (bf16[576,1024]{1,0:T(8,128)(2,1)S(1)}, bf16[576,1024]{1,0:T(8,128)(2,1)}, u32[]{:S(2)}, u32[]{:S(2)}) collective-permute-start(bf16[576,1024]{1,0:T(8,128)(2,1)S(1)} %fusion.4), channel_id=1, source_target_pairs={{0,1},{1,0},{2,3},{3,2},{4,5},{5,4},{6,7},{7,6},{8,9},{9,8},{10,11... | collective-permute-start | bytes 3538952 | tf_op jit(solution)/shard_map/ppermute | solution.py:748
  230.2 38.8 %copy-start.40 = (u32[32]{0:T(128)S(1)}, u32[32]{0:T(128)}, u32[]{:S(2)}) copy-start(u32[32]{0:T(128)} %constant.88) | copy-start | bytes 388
  264.1 6.3 collective-permute-start.5
  277.9 16.2 %collective-permute-start.12 = (bf16[288,1024]{1,0:T(8,128)(2,1)S(1)}, bf16[288,1024]{1,0:T(8,128)(2,1)S(1)}, u32[]{:S(2)}, u32[]{:S(2)}) collective-permute-start(bf16[288,1024]{1,0:T(8,128)(2,1)S(1)} %slice.352), channel_id=1, source_target_pairs={{0,1},{1,0},{2,3},{3,2},{4,5},{5,4},{6,7},{7,6},{8,9},{9,8},{10,11... | collective-permute-start | bytes 1769480 | tf_op jit(solution)/shard_map/ppermute | solution.py:748
  279.1 15.0 %collective-permute-start.13 = (bf16[288,1024]{1,0:T(8,128)(2,1)S(1)}, bf16[288,1024]{1,0:T(8,128)(2,1)S(1)}, u32[]{:S(2)}, u32[]{:S(2)}) collective-permute-start(bf16[288,1024]{1,0:T(8,128)(2,1)S(1)} %slice.353), channel_id=1, source_target_pairs={{0,4},{1,5},{2,6},{3,7},{4,0},{5,1},{6,2},{7,3},{8,12},{9,13},{10,... | collective-permute-start | bytes 1769480 | tf_op jit(solution)/shard_map/ppermute | solution.py:748
  290.9 266.8 %collective-permute-start.6 = (bf16[1152,1024]{1,0:T(8,128)(2,1)}, bf16[1152,1024]{1,0:T(8,128)(2,1)}, u32[]{:S(2)}, u32[]{:S(2)}) collective-permute-start(bf16[1152,1024]{1,0:T(8,128)(2,1)} %get-tuple-element.83), channel_id=1, source_target_pairs={{0,4},{1,5},{2,6},{3,7},{4,0},{5,1},{6,2},{7,3},{8,12},{9,13},{10,... | collective-permute-start | bytes 7077896 | tf_op jit(solution)/shard_map/ppermute | solution.py:748
  303.8 223.6 %collective-permute-start.34 = (bf16[1024,512]{1,0:T(8,128)(2,1)}, bf16[1024,512]{1,0:T(8,128)(2,1)}, u32[]{:S(2)}, u32[]{:S(2)}) collective-permute-start(bf16[1024,512]{1,0:T(8,128)(2,1)} %convolution_convert_fusion.3), channel_id=1, source_target_pairs={{0,8},{8,0},{16,24},{24,16},{1,9},{9,1},{17,25},{25,17},{2,10},{10... | collective-permute-start | bytes 3145736 | tf_op jit(solution)/shard_map/ppermute | solution.py:770
  303.8 228.8 %collective-permute-start.37 = (bf16[1024,512]{1,0:T(8,128)(2,1)}, bf16[1024,512]{1,0:T(8,128)(2,1)}, u32[]{:S(2)}, u32[]{:S(2)}) collective-permute-start(bf16[1024,512]{1,0:T(8,128)(2,1)} %convolution_convert_fusion.2), channel_id=1, source_target_pairs={{0,8},{8,0},{16,24},{24,16},{1,9},{9,1},{17,25},{25,17},{2,10},{10... | collective-permute-start | bytes 3145736 | tf_op jit(solution)/shard_map/ppermute | solution.py:770
  304.3 38.6 %slice-start.4 = ((s8[4718592]{0:T(1024)(128)(4,1)}), s8[4194304]{0:T(1024)(128)(4,1)S(1)}, s32[]{:S(2)}) async-start(s8[4718592]{0:T(1024)(128)(4,1)} %bitcast.122), calls=%async_computation.6 | async-start | bytes 8388608
  337.9 9.4 %collective-permute-start.14 = (f32[16,1024]{1,0:T(8,128)}, f32[16,1024]{1,0:T(8,128)S(1)}, u32[]{:S(2)}, u32[]{:S(2)}) collective-permute-start(f32[16,1024]{1,0:T(8,128)} %get-tuple-element.87), channel_id=1, source_target_pairs={{0,6},{1,7},{2,4},{3,5},{4,2},{5,3},{6,0},{7,1},{8,14},{9,15},{10,... | collective-permute-start | bytes 196616 | tf_op jit(solution)/shard_map/ppermute | solution.py:748
  347.3 252.5 %collective-permute-start.29 = (bf16[2,1024,512]{2,1,0:T(8,128)(2,1)}, bf16[2,1024,512]{2,1,0:T(8,128)(2,1)}, u32[]{:S(2)}, u32[]{:S(2)}) collective-permute-start(bf16[2,1024,512]{2,1,0:T(8,128)(2,1)} %convolution_convert_fusion), channel_id=1, source_target_pairs={{0,8},{8,0},{16,24},{24,16},{1,9},{9,1},{17,25},{25,17},{2,10},{10... | collective-permute-start | bytes 6291464 | tf_op jit(solution)/shard_map/ppermute | solution.py:770
  348.0 46.0 %copy-start.26 = (f32[160,128]{1,0:T(8,128)S(1)}, f32[160,128]{1,0:T(8,128)}, u32[]{:S(2)}) copy-start(f32[160,128]{1,0:T(8,128)} %get-tuple-element.100) | copy-start | bytes 245764
  394.1 48.3 %collective-permute-start.17 = (bf16[160,640]{1,0:T(8,128)(2,1)S(1)}, bf16[160,640]{1,0:T(8,128)(2,1)S(1)}, u32[]{:S(2)}, u32[]{:S(2)}) collective-permute-start(bf16[160,640]{1,0:T(8,128)(2,1)S(1)} %convert_element_type.205), channel_id=1, source_target_pairs={{0,4},{1,5},{2,6},{3,7},{4,0},{5,1},{6,2},{7,3},{8,12},{9,13},{10,... | collective-permute-start | bytes 614408 | tf_op jit(solution)/shard_map/ppermute | solution.py:748
  442.4 6.6 collective-permute-start.15
  449.0 6.8 collective-permute-start.18
  455.8 7.5 collective-permute-start.16
  463.3 6.0 collective-permute-start.19
  491.1 33.0 %collective-permute-start.22 = (f32[1152,1]{0,1:T(1,128)S(1)}, f32[1152,1]{0,1:T(1,128)S(1)}, u32[]{:S(2)}, u32[]{:S(2)}) collective-permute-start(f32[1152,1]{0,1:T(1,128)S(1)} %copy.59), channel_id=1, source_target_pairs={{0,4},{1,5},{2,6},{3,7},{4,0},{5,1},{6,2},{7,3},{8,12},{9,13},{10,... | collective-permute-start | bytes 13832 | tf_op jit(solution)/shard_map/ppermute | solution.py:748
  492.6 29.9 %copy-start.13 = (bf16[1152,1024]{1,0:T(8,128)(2,1)S(1)}, bf16[1152,1024]{1,0:T(8,128)(2,1)}, u32[]{:S(2)}) copy-start(bf16[1152,1024]{1,0:T(8,128)(2,1)} %get-tuple-element.111.inner_ref) | copy-start | bytes 7077892
  527.1 18.8 %collective-permute-start.23 = (f32[576,1]{1,0:T(8,128)}, f32[576,1]{1,0:T(8,128)}, u32[]{:S(2)}, u32[]{:S(2)}) collective-permute-start(f32[576,1]{1,0:T(8,128)} %slice_select_fusion.5), channel_id=1, source_target_pairs={{0,1},{1,0},{2,3},{3,2},{4,5},{5,4},{6,7},{7,6},{8,9},{9,8},{10,11... | collective-permute-start | bytes 6920 | tf_op jit(solution)/shard_map/ppermute | solution.py:748
  531.9 17.8 %collective-permute-start.35 = (bf16[1024,256]{1,0:T(8,128)(2,1)}, bf16[1024,256]{1,0:T(8,128)(2,1)}, u32[]{:S(2)}, u32[]{:S(2)}) collective-permute-start(bf16[1024,256]{1,0:T(8,128)(2,1)} %slice.493), channel_id=1, source_target_pairs={{0,16},{8,24},{16,0},{24,8},{1,17},{9,25},{17,1},{25,9},{2,18},{10... | collective-permute-start | bytes 1572872 | tf_op jit(solution)/shard_map/ppermute | solution.py:770
  537.7 15.5 %collective-permute-start.38 = (bf16[1024,256]{1,0:T(8,128)(2,1)}, bf16[1024,256]{1,0:T(8,128)(2,1)}, u32[]{:S(2)}, u32[]{:S(2)}) collective-permute-start(bf16[1024,256]{1,0:T(8,128)(2,1)} %slice.492), channel_id=1, source_target_pairs={{0,16},{8,24},{16,0},{24,8},{1,17},{9,25},{17,1},{25,9},{2,18},{10... | collective-permute-start | bytes 1572872 | tf_op jit(solution)/shard_map/ppermute | solution.py:770
  545.9 34.2 %collective-permute-start.33 = (f32[312,1024]{1,0:T(8,128)S(1)}, f32[312,1024]{1,0:T(8,128)}, u32[]{:S(2)}, u32[]{:S(2)}) collective-permute-start(f32[312,1024]{1,0:T(8,128)S(1)} %pad.13), channel_id=1, source_target_pairs={{0,0},{4,1},{1,2},{5,3},{6,4},{2,5},{7,6},{3,7},{8,8},{12,9},{9,10... | collective-permute-start | bytes 3833864 | tf_op jit(solution)/shard_map/ppermute | solution.py:748
  549.8 85.6 %collective-permute-start.25 = (bf16[2,1024,512]{2,1,0:T(8,128)(2,1)}, bf16[2,1024,512]{2,1,0:T(8,128)(2,1)}, u32[]{:S(2)}, u32[]{:S(2)}) collective-permute-start(bf16[2,1024,512]{2,1,0:T(8,128)(2,1)} %convolution_convert_fusion.1), channel_id=1, source_target_pairs={{0,8},{8,0},{16,24},{24,16},{1,9},{9,1},{17,25},{25,17},{2,10},{10... | collective-permute-start | bytes 6291464 | tf_op jit(solution)/shard_map/ppermute | solution.py:770
  553.2 37.3 %collective-permute-start.36 = (bf16[1024,256]{1,0:T(8,128)(2,1)}, bf16[1024,256]{1,0:T(8,128)(2,1)}, u32[]{:S(2)}, u32[]{:S(2)}) collective-permute-start(bf16[1024,256]{1,0:T(8,128)(2,1)} %fusion.17), channel_id=1, source_target_pairs={{0,0},{2,1},{1,2},{3,3},{6,4},{4,5},{7,6},{5,7},{8,8},{10,9},{9,10... | collective-permute-start | bytes 1572872 | tf_op jit(solution)/shard_map/ppermute | solution.py:748
  557.7 39.9 %collective-permute-start.39 = (bf16[1024,256]{1,0:T(8,128)(2,1)}, bf16[1024,256]{1,0:T(8,128)(2,1)}, u32[]{:S(2)}, u32[]{:S(2)}) collective-permute-start(bf16[1024,256]{1,0:T(8,128)(2,1)} %fusion.16), channel_id=1, source_target_pairs={{6,0},{4,1},{7,2},{5,3},{0,4},{2,5},{1,6},{3,7},{14,8},{12,9},{15,... | collective-permute-start | bytes 1572872 | tf_op jit(solution)/shard_map/ppermute | solution.py:748
  580.1 63.2 %collective-permute-start.20 = (bf16[1152,1024]{1,0:T(8,128)(2,1)}, bf16[1152,1024]{1,0:T(8,128)(2,1)S(1)}, u32[]{:S(2)}, u32[]{:S(2)}) collective-permute-start(bf16[1152,1024]{1,0:T(8,128)(2,1)} %get-tuple-element.114), channel_id=1, source_target_pairs={{0,4},{1,5},{2,6},{3,7},{4,0},{5,1},{6,2},{7,3},{8,12},{9,13},{10,... | collective-permute-start | bytes 7077896 | tf_op jit(solution)/shard_map/ppermute | solution.py:748
  590.5 31.6 %collective-permute-start.7 = (bf16[576,1024]{1,0:T(8,128)(2,1)S(1)}, bf16[576,1024]{1,0:T(8,128)(2,1)S(1)}, u32[]{:S(2)}, u32[]{:S(2)}) collective-permute-start(bf16[576,1024]{1,0:T(8,128)(2,1)S(1)} %select_convert_fusion.1), channel_id=1, source_target_pairs={{0,1},{1,0},{2,3},{3,2},{4,5},{5,4},{6,7},{7,6},{8,9},{9,8},{10,11... | collective-permute-start | bytes 3538952 | tf_op jit(solution)/shard_map/ppermute | solution.py:748
  599.8 22.4 %slice-start = ((s8[4718592]{0:T(1024)(128)(4,1)}), s8[4194304]{0:T(1024)(128)(4,1)S(1)}, s32[]{:S(2)}) async-start(s8[4718592]{0:T(1024)(128)(4,1)} %bitcast.103), calls=%async_computation.2 | async-start | bytes 8388608
  599.8 22.4 %slice-start.1 = ((s8[4718592]{0:T(1024)(128)(4,1)}), s8[524288]{0:T(1024)(128)(4,1)S(1)}, s32[]{:S(2)}) async-start(s8[4718592]{0:T(1024)(128)(4,1)} %bitcast.103), calls=%async_computation.3 | async-start | bytes 1048576
  606.8 38.0 %collective-permute-start.30 = (bf16[2,1024,256]{2,1,0:T(8,128)(2,1)S(1)}, bf16[2,1024,256]{2,1,0:T(8,128)(2,1)S(1)}, u32[]{:S(2)}, u32[]{:S(2)}) collective-permute-start(bf16[2,1024,256]{2,1,0:T(8,128)(2,1)S(1)} %select_convert_fusion.2), channel_id=1, source_target_pairs={{0,16},{8,24},{16,0},{24,8},{1,17},{9,25},{17,1},{25,9},{2,18},{10... | collective-permute-start | bytes 3145736 | tf_op jit(solution)/shard_map/ppermute | solution.py:770
  623.3 9.8 %collective-permute-start.8 = (bf16[128,1024]{1,0:T(8,128)(2,1)S(1)}, bf16[128,1024]{1,0:T(8,128)(2,1)S(1)}, u32[]{:S(2)}, u32[]{:S(2)}) collective-permute-start(bf16[128,1024]{1,0:T(8,128)(2,1)S(1)} %slice_select_fusion.7), channel_id=1, source_target_pairs={{2,1},{3,2},{1,3},{6,5},{7,6},{5,7},{10,9},{11,10},{9,11},{14,13},... | collective-permute-start | bytes 786440 | tf_op jit(solution)/shard_map/ppermute | solution.py:748
  640.3 23.8 %collective-permute-start.26 = (bf16[2,1024,256]{2,1,0:T(8,128)(2,1)S(1)}, bf16[2,1024,256]{2,1,0:T(8,128)(2,1)S(1)}, u32[]{:S(2)}, u32[]{:S(2)}) collective-permute-start(bf16[2,1024,256]{2,1,0:T(8,128)(2,1)S(1)} %select_convert_fusion.3), channel_id=1, source_target_pairs={{0,16},{8,24},{16,0},{24,8},{1,17},{9,25},{17,1},{25,9},{2,18},{10... | collective-permute-start | bytes 3145736 | tf_op jit(solution)/shard_map/ppermute | solution.py:770
  644.7 67.2 %collective-permute-start.21 = (bf16[576,1024]{1,0:T(8,128)(2,1)S(1)}, bf16[576,1024]{1,0:T(8,128)(2,1)S(1)}, u32[]{:S(2)}, u32[]{:S(2)}) collective-permute-start(bf16[576,1024]{1,0:T(8,128)(2,1)S(1)} %select_convert_fusion), channel_id=1, source_target_pairs={{0,1},{1,0},{2,3},{3,2},{4,5},{5,4},{6,7},{7,6},{8,9},{9,8},{10,11... | collective-permute-start | bytes 3538952 | tf_op jit(solution)/shard_map/ppermute | solution.py:748
  646.8 38.1 %collective-permute-start.31 = (bf16[1024,256]{1,0:T(8,128)(2,1)S(1)}, bf16[1024,256]{1,0:T(8,128)(2,1)S(1)}, u32[]{:S(2)}, u32[]{:S(2)}) collective-permute-start(bf16[1024,256]{1,0:T(8,128)(2,1)S(1)} %get-tuple-element.192), channel_id=1, source_target_pairs={{0,0},{2,1},{1,2},{3,3},{6,4},{4,5},{7,6},{5,7},{8,8},{10,9},{9,10... | collective-permute-start | bytes 1572872 | tf_op jit(solution)/shard_map/ppermute | solution.py:748
  649.4 35.5 %collective-permute-start.32 = (bf16[1024,256]{1,0:T(8,128)(2,1)S(1)}, bf16[1024,256]{1,0:T(8,128)(2,1)S(1)}, u32[]{:S(2)}, u32[]{:S(2)}) collective-permute-start(bf16[1024,256]{1,0:T(8,128)(2,1)S(1)} %get-tuple-element.193), channel_id=1, source_target_pairs={{6,0},{4,1},{7,2},{5,3},{0,4},{2,5},{1,6},{3,7},{14,8},{12,9},{15,... | collective-permute-start | bytes 1572872 | tf_op jit(solution)/shard_map/ppermute | solution.py:748
  664.5 47.4 %copy-start.30 = (f32[4,2,128]{2,1,0:T(2,128)S(1)}, f32[4,2,128]{2,1,0:T(2,128)}, u32[]{:S(2)}) copy-start(f32[4,2,128]{2,1,0:T(2,128)} %copy-done.29) | copy-start | bytes 12292
  665.6 71.0 %collective-permute-start.27 = (bf16[1024,256]{1,0:T(8,128)(2,1)}, bf16[1024,256]{1,0:T(8,128)(2,1)}, u32[]{:S(2)}, u32[]{:S(2)}) collective-permute-start(bf16[1024,256]{1,0:T(8,128)(2,1)} %get-tuple-element.190), channel_id=1, source_target_pairs={{0,0},{2,1},{1,2},{3,3},{6,4},{4,5},{7,6},{5,7},{8,8},{10,9},{9,10... | collective-permute-start | bytes 1572872 | tf_op jit(solution)/shard_map/ppermute | solution.py:748
  671.0 65.5 %collective-permute-start.28 = (bf16[1024,256]{1,0:T(8,128)(2,1)}, bf16[1024,256]{1,0:T(8,128)(2,1)}, u32[]{:S(2)}, u32[]{:S(2)}) collective-permute-start(bf16[1024,256]{1,0:T(8,128)(2,1)} %get-tuple-element.191), channel_id=1, source_target_pairs={{6,0},{4,1},{7,2},{5,3},{0,4},{2,5},{1,6},{3,7},{14,8},{12,9},{15,... | collective-permute-start | bytes 1572872 | tf_op jit(solution)/shard_map/ppermute | solution.py:748
  716.3 24.7 %collective-permute-start.24 = (bf16[128,1024]{1,0:T(8,128)(2,1)S(1)}, bf16[128,1024]{1,0:T(8,128)(2,1)S(1)}, u32[]{:S(2)}, u32[]{:S(2)}) collective-permute-start(bf16[128,1024]{1,0:T(8,128)(2,1)S(1)} %slice_select_fusion.6), channel_id=1, source_target_pairs={{2,1},{3,2},{1,3},{6,5},{7,6},{5,7},{10,9},{11,10},{9,11},{14,13},... | collective-permute-start | bytes 786440 | tf_op jit(solution)/shard_map/ppermute | solution.py:748
  (46 other events, 256.4 us)
Sparse Core Ops, SparseCore 0:
  580.9 41.0 reduce-scatter.1

commit v2 on v1

v2 whole, which is shorter than its diff:
```python
import functools

import jax
import jax.numpy as jnp
from jax import lax
from jax.experimental import pallas as pl
from jax.experimental.pallas import tpu as pltpu
from jax.sharding import PartitionSpec as P

D = 2048
NSTATE = 16
KCONV = 4
RANK = 128
NPROMPT = 2
LP = 1024
LC = 128
NCONT = 2

eps = 1e-05
CH = 128
SUB = 16
PC = LP // CH
SEQ = LP + LC
NCH = SEQ // CH
XW = RANK + 2 * NSTATE
SPAN = SUB * NSTATE
LOG2E = 1.4426950408889634
VMEM_LIMIT = 58 * 1024 * 1024

f32 = jnp.float32
bf16 = jnp.bfloat16


def dot_nn(a, b):
    return lax.dot_general(a, b, (((1,), (0,)), ((), ())), preferred_element_type=f32)


def dot_nt(a, b):
    return lax.dot_general(a, b, (((1,), (1,)), ((), ())), preferred_element_type=f32)


def dot_tn(a, b):
    return lax.dot_general(a, b, (((0,), (0,)), ((), ())), preferred_element_type=f32)


def expand_tile():
    lane = lax.broadcasted_iota(jnp.int32, (NSTATE, SPAN), 1)
    row = lax.broadcasted_iota(jnp.int32, (NSTATE, SPAN), 0)
    return jnp.where(lane % NSTATE == row, 1.0, 0.0)


def own_token(rows):
    lane = lax.broadcasted_iota(jnp.int32, (rows, SPAN), 1)
    row = lax.broadcasted_iota(jnp.int32, (rows, SPAN), 0)
    return lane // NSTATE == row % SUB


def conv_forward(inner_ref, inv_ref, tail_ref, conv_ref, xproj_ref, xconv_ref, xdbl_ref, buf):
    i = pl.program_id(0)

    @pl.when(i == 0)
    def _():
        buf[0:8] = jnp.zeros_like(buf[0:8])

    @pl.when(i == PC)
    def _():
        buf[0:8] = tail_ref[...]

    @pl.when((i > 0) & (i < PC))
    def _():
        buf[0:8] = buf[CH : CH + 8]

    buf[8 : CH + 8] = inv_ref[...] * inner_ref[...]
    out = conv_ref[4:5]
    for k in range(KCONV):
        out = out + conv_ref[k : k + 1] * buf[5 + k : 5 + k + CH]
    xconv = (out * jax.nn.sigmoid(out)).astype(bf16)
    xconv_ref[...] = xconv
    xdbl_ref[...] = dot_nt(xproj_ref[...], xconv)


def softplus(v):
    return jnp.maximum(v, 0.0) + jnp.log1p(jnp.exp(-jnp.abs(v)))


def by_sub(v):
    return v.reshape(CH // SUB, SUB, v.shape[-1])


def scan_chunk(xdbl_ref, xconv, dtp_ref, vec_ref, rate_ref, state, dt_s, u_s, cb_s, h_s, y_s):
    step = softplus(dot_tn(xdbl_ref[:RANK].astype(bf16), dtp_ref[...]) + vec_ref[0:1])
    dt_s[...] = by_sub(step)
    u_s[...] = by_sub(step * xconv)
    reads = dot_tn(xdbl_ref[RANK + NSTATE :].astype(bf16), expand_tile().astype(bf16))
    cb_s[...] = jnp.where(own_token(CH), reads, 0.0).astype(bf16)
    rate = rate_ref[...] * LOG2E

    def block(j, carried):
        h, maps = carried
        for t in range(SUB):
            a = jnp.exp2(dt_s[j, t : t + 1, :] * rate)
            h = a * h + u_s[j, t : t + 1, :] * maps[:, t : t + 1]
            h_s[t * NSTATE : (t + 1) * NSTATE, :] = h.astype(bf16)
        rows = pl.ds(pl.multiple_of(j * SUB, SUB), SUB)
        y_s[rows, :] = dot_nn(cb_s[rows, :], h_s[...])
        return (h, pltpu.roll(maps, CH - SUB, 1))

    h, _ = lax.fori_loop(0, CH // SUB, block, (state, xdbl_ref[RANK : RANK + NSTATE]))
    return h, y_s[...] + vec_ref[1:2] * xconv


def scan_scratch(w):
    return [
        pltpu.VMEM((CH // SUB, SUB, w), f32),
        pltpu.VMEM((CH // SUB, SUB, w), f32),
        pltpu.VMEM((CH, SPAN), bf16),
        pltpu.VMEM((SPAN, w), bf16),
        pltpu.VMEM((CH, w), f32),
    ]


def scan_forward(kept, xdbl_ref, xconv_ref, dtp_ref, vec_ref, rate_ref, start_ref, *refs):
    yfull_ref, starts_ref, final_ref, *scratch = refs[kept:]

    @pl.when(pl.program_id(0) == 0)
    def _():
        final_ref[...] = start_ref[...]

    starts_ref[0] = final_ref[...]
    h, yfull = scan_chunk(xdbl_ref, xconv_ref[...].astype(f32), dtp_ref, vec_ref, rate_ref, final_ref[...], *scratch)
    final_ref[...] = h
    yfull_ref[...] = yfull.astype(bf16)


def chunk_backward(xdbl_ref, xconv_ref, dy_ref, dtp_ref, vec_ref, rate_ref, starts_ref, dxdbl_ref, dxc_ref, alog_ref, sums_ref, dtpg_ref, first_ref,
                   dt_s, u_s, x_s, dy_s, a_s, h_s, g_s, w_s, b_s, m1_s, m2_s, ds_s, dx_s, sig_s):
    low = xdbl_ref[:RANK].astype(bf16)
    step_inner = dot_tn(low, dtp_ref[...]) + vec_ref[0:1]
    step = softplus(step_inner)
    sig_s[...] = jax.nn.sigmoid(step_inner)
    xconv = xconv_ref[...].astype(f32)
    dy = dy_ref[...]
    dt_s[...] = by_sub(step)
    u_s[...] = by_sub(step * xconv)
    x_s[...] = by_sub(xconv)
    dy_s[...] = by_sub(dy)
    tile = expand_tile().astype(bf16)
    b_s[...] = jnp.where(own_token(CH), dot_tn(xdbl_ref[RANK : RANK + NSTATE].astype(bf16), tile), 0.0).astype(bf16)
    rate = rate_ref[...]
    rate2 = rate * LOG2E
    h_s[0:NSTATE] = starts_ref[0]

    def ahead(j, carried):
        h, maps = carried
        for t in range(SUB):
            a = jnp.exp2(dt_s[j, t : t + 1, :] * rate2)
            h = a * h + u_s[j, t : t + 1, :] * maps[:, t : t + 1]
            a_s[j, t * NSTATE : (t + 1) * NSTATE, :] = a
            at = pl.multiple_of(j * SPAN + (t + 1) * NSTATE, NSTATE)
            h_s[pl.ds(at, NSTATE), :] = h
        return (h, pltpu.roll(maps, CH - SUB, 1))

    lax.fori_loop(0, CH // SUB, ahead, (starts_ref[0], xdbl_ref[RANK : RANK + NSTATE]))
    ones = jnp.where(own_token(SUB), 1.0, 0.0).astype(bf16)
    mine_sub = own_token(SUB)

    def back(jj, carried):
        g, alog, maps = carried
        j = CH // SUB - 1 - jj
        maps = pltpu.roll(maps, SUB, 1)
        for t in reversed(range(SUB)):
            dt = dt_s[j, t : t + 1, :]
            gs = maps[:, t : t + 1] * dy_s[j, t : t + 1, :] + g
            g = a_s[j, t * NSTATE : (t + 1) * NSTATE, :] * gs
            prior = h_s[pl.ds(pl.multiple_of(j * SPAN + t * NSTATE, NSTATE), NSTATE), :]
            w = g * prior
            alog = alog + w * dt
            g_s[t * NSTATE : (t + 1) * NSTATE, :] = gs.astype(bf16)
            w_s[t * NSTATE : (t + 1) * NSTATE, :] = (w * rate).astype(bf16)
        rows = pl.ds(pl.multiple_of(j * SUB, SUB), SUB)
        gs_all = g_s[...]
        through = dot_nn(b_s[rows, :], gs_all)
        ds_s[rows, :] = dot_nn(ones, w_s[...]) + x_s[j] * through
        dx_s[rows, :] = dt_s[j] * through + vec_ref[1:2] * dy_s[j]
        hs = h_s[pl.ds(pl.multiple_of(j * SPAN + NSTATE, NSTATE), SPAN), :].astype(bf16)
        m1_s[rows, :] = jnp.where(mine_sub, dot_nt(u_s[j].astype(bf16), gs_all), 0.0).astype(bf16)
        m2_s[rows, :] = jnp.where(mine_sub, dot_nt(dy_s[j].astype(bf16), hs), 0.0).astype(bf16)
        return (g, alog, maps)

    g, alog, _ = lax.fori_loop(0, CH // SUB, back, (first_ref[...], alog_ref[...], xdbl_ref[RANK + NSTATE :]))
    first_ref[...] = g
    alog_ref[...] = alog
    d_inner = ds_s[...] * sig_s[...]
    d_low = d_inner.astype(bf16)
    sums_ref[0:1] = sums_ref[0:1] + jnp.sum(d_inner, axis=0, keepdims=True)
    sums_ref[1:2] = sums_ref[1:2] + jnp.sum(dy * xconv, axis=0, keepdims=True)
    dtpg_ref[...] = dtpg_ref[...] + dot_nn(low, d_low)
    dxdbl_ref[:RANK] = dot_nt(dtp_ref[...], d_low)
    dxdbl_ref[RANK : RANK + NSTATE] = dot_nt(tile, m1_s[...])
    dxdbl_ref[RANK + NSTATE :] = dot_nt(tile, m2_s[...])
    dxc_ref[...] = dx_s[...]


def scan_backward(kept, *refs):
    given, sums0, out = refs[:7], refs[7:11], refs[11 + kept :]
    dxdbl_ref, dxc_ref, alog_ref, sums_ref, dtpg_ref, first_ref = out[:6]

    @pl.when(pl.program_id(0) == 0)
    def _():
        first_ref[...] = sums0[0][...]
        alog_ref[...] = sums0[1][...]
        sums_ref[...] = sums0[2][...]
        dtpg_ref[...] = sums0[3][...]

    chunk_backward(*given, dxdbl_ref, dxc_ref, alog_ref, sums_ref, dtpg_ref, first_ref, *out[6:])


def backward_scratch(w):
    sub = pltpu.VMEM((CH // SUB, SUB, w), f32)
    return [
        sub,
        sub,
        sub,
        sub,
        pltpu.VMEM((CH // SUB, SPAN, w), f32),
        pltpu.VMEM(((CH + 1) * NSTATE, w), f32),
        pltpu.VMEM((SPAN, w), bf16),
        pltpu.VMEM((SPAN, w), bf16),
        pltpu.VMEM((CH, SPAN), bf16),
        pltpu.VMEM((CH, SPAN), bf16),
        pltpu.VMEM((CH, SPAN), bf16),
        pltpu.VMEM((CH, w), f32),
        pltpu.VMEM((CH, w), f32),
        pltpu.VMEM((CH, w), f32),
    ]


def conv_backward(kept, chunks, first, inner_ref, halo_ref, inv_ref, halo_inv_ref, tail_ref, conv_ref, xproj_ref, dxc_ref, dxdbl_ref, follow_ref, sums0_ref, xprojg0_ref, *refs):
    dproj_ref, dscale_ref, sums_ref, xprojg_ref, head_ref, buf, dbuf = refs[kept:]
    i = pl.program_id(0)
    chunk = first + chunks - 1 - i

    @pl.when(i == 0)
    def _():
        sums_ref[...] = sums0_ref[...]
        xprojg_ref[...] = xprojg0_ref[...]
        head_ref[...] = follow_ref[...]

    projected = inner_ref[...]
    inv = inv_ref[...]
    before = halo_inv_ref[...] * halo_ref[...]
    before = jnp.where(chunk == 0, 0.0, jnp.where(chunk == PC, tail_ref[...], before))
    buf[0:8] = before
    buf[8 : CH + 8] = inv * projected
    out = conv_ref[4:5]
    for k in range(KCONV):
        out = out + conv_ref[k : k + 1] * buf[5 + k : 5 + k + CH]
    sig = jax.nn.sigmoid(out)
    xconv = (out * sig).astype(bf16)
    dxdbl = dxdbl_ref[...].astype(bf16)
    xprojg_ref[...] = xprojg_ref[...] + dot_nn(dxdbl, xconv)
    d_x = dxc_ref[...] + dot_tn(dxdbl, xproj_ref[...])
    d_conv = d_x * (sig * (1.0 + out * (1.0 - sig)))
    dbuf[CH : CH + 8] = head_ref[...]
    dbuf[0:CH] = d_conv
    d_inner = conv_ref[3:4] * d_conv
    for k in range(KCONV - 1):
        d_inner = d_inner + conv_ref[k : k + 1] * dbuf[3 - k : 3 - k + CH]
    for k in range(KCONV):
        sums_ref[k : k + 1] = sums_ref[k : k + 1] + jnp.sum(buf[5 + k : 5 + k + CH] * d_conv, axis=0, keepdims=True)
    sums_ref[4:5] = sums_ref[4:5] + jnp.sum(d_conv, axis=0, keepdims=True)
    dproj_ref[...] = (inv * d_inner).astype(bf16)
    dscale_ref[...] = jnp.sum(d_inner * projected, axis=1, keepdims=True)
    head_ref[...] = d_conv[0:8]


def call(body, chunks, args, in_specs, outs, out_specs, scratch, micros, aliases=None):
    return pl.pallas_call(
        body,
        grid=(chunks,),
        in_specs=in_specs,
        out_specs=out_specs,
        scratch_shapes=scratch,
        out_shape=outs,
        input_output_aliases=aliases or {},
        compiler_params=pltpu.CompilerParams(dimension_semantics=("arbitrary",), vmem_limit_bytes=VMEM_LIMIT),
        cost_estimate=pl.CostEstimate(flops=micros * 1000000000, bytes_accessed=1000000, transcendentals=0),
    )(*args)


def shaped(*shape, dtype=f32):
    return jax.ShapeDtypeStruct(shape, dtype)


def rows_of(width, place, tall=CH):
    return pl.BlockSpec((tall, width), lambda i: (place(i), 0))


def lanes_of(height, place):
    return pl.BlockSpec((height, CH), lambda i: (0, place(i)))


def whole(*shape):
    return pl.BlockSpec(shape, lambda i: (0,) * len(shape))


ANY = pl.BlockSpec(memory_space=pl.ANY)


def run_conv_forward(inner, inv, tail, conv, xproj):
    w = inner.shape[1]
    at = lambda i: i
    return call(
        conv_forward,
        NCH,
        (inner, inv, tail, conv, xproj),
        [rows_of(w, at), rows_of(1, at), whole(8, w), whole(8, w), whole(XW, w)],
        (shaped(SEQ, w, dtype=bf16), shaped(XW, SEQ)),
        (rows_of(w, at), lanes_of(XW, at)),
        [pltpu.VMEM((CH + 8, w), f32)],
        12,
    )


def chunk_of(height, place):
    return pl.BlockSpec((None, height, CH), lambda i: (place(i), 0, 0))


def run_scan_forward(first, chunks, xdbl, xconv, dtp, vec, rate, start, kept=()):
    w = xconv.shape[1]
    at = lambda i: first + i
    return call(
        functools.partial(scan_forward, len(kept)),
        chunks,
        (xdbl, xconv, dtp, vec, rate, start, *kept),
        [chunk_of(XW, at), rows_of(w, at), whole(RANK, w), whole(8, w), whole(NSTATE, w), whole(NSTATE, w)] + [ANY] * len(kept),
        (shaped(SEQ, w, dtype=bf16), shaped(NCH, NSTATE, w), shaped(NSTATE, w)),
        (rows_of(w, at), pl.BlockSpec((1, NSTATE, w), lambda i: (first + i, 0, 0)), whole(NSTATE, w)),
        scan_scratch(w),
        5 * chunks,
        {6 + k: k for k in range(len(kept))},
    )


def run_scan_backward(first, chunks, xdbl, xconv, dy, dtp, vec, rate, starts, carry, sums, kept=()):
    w = xconv.shape[1]
    at = lambda i: first + chunks - 1 - i
    local = lambda i: chunks - 1 - i
    return call(
        functools.partial(scan_backward, len(kept)),
        chunks,
        (xdbl, xconv, dy, dtp, vec, rate, starts, carry, *sums, *kept),
        [
            chunk_of(XW, at),
            rows_of(w, at),
            rows_of(w, at),
            whole(RANK, w),
            whole(8, w),
            whole(NSTATE, w),
            pl.BlockSpec((1, NSTATE, w), lambda i: (at(i), 0, 0)),
            whole(NSTATE, w),
            whole(NSTATE, w),
            whole(8, w),
            whole(RANK, w),
        ]
        + [ANY] * len(kept),
        (shaped(XW, chunks * CH), shaped(SEQ, w), shaped(NSTATE, w), shaped(8, w), shaped(RANK, w), shaped(NSTATE, w)),
        (lanes_of(XW, local), rows_of(w, at), whole(NSTATE, w), whole(8, w), whole(RANK, w), whole(NSTATE, w)),
        backward_scratch(w),
        11 * chunks,
        {11 + k: 1 + k for k in range(len(kept))},
    )


def run_conv_backward(first, chunks, inner, inv, tail, conv, xproj, dxc, dxdbl, follow, sums, kept=()):
    w = inner.shape[1]
    at = lambda i: first + chunks - 1 - i
    before = lambda i: (jnp.maximum(at(i) * (CH // 8) - 1, 0), 0)
    return call(
        functools.partial(conv_backward, len(kept), chunks, first),
        chunks,
        (inner, inner, inv, inv, tail, conv, xproj, dxc, dxdbl, follow, *sums, *kept),
        [
            rows_of(w, at),
            pl.BlockSpec((8, w), before),
            rows_of(1, at),
            pl.BlockSpec((8, 1), before),
            whole(8, w),
            whole(8, w),
            whole(XW, w),
            rows_of(w, at),
            chunk_of(XW, at),
            whole(8, w),
            whole(8, w),
            whole(XW, w),
        ]
        + [ANY] * len(kept),
        (shaped(SEQ, w, dtype=bf16), shaped(SEQ, 1), shaped(8, w), shaped(XW, w), shaped(8, w)),
        (rows_of(w, at), rows_of(1, at), whole(8, w), whole(XW, w), whole(8, w)),
        [pltpu.VMEM((CH + 8, w), f32), pltpu.VMEM((CH + 8, w), f32)],
        2 * chunks,
        {12 + k: k for k in range(len(kept))},
    )


MESH = pl.DeviceIdType.MESH
BIG = 384
BIG_STEPS = SEQ // BIG
SLOTS = 4


def remote(src, dst, send, recv, device):
    return pltpu.make_async_remote_copy(src_ref=src, dst_ref=dst, send_sem=send, recv_sem=recv, device_id=device, device_id_type=MESH)


def xor_bit(a, b):
    return a + b - 2 * a * b


def token_pieces(c, local):
    cut = local - LC
    low = cut - LC
    if c == 0:
        return [(0, local, 0, 0)]
    if c == 1:
        return [(0, cut, 0, local), (cut, local, 1, 0)]
    if c == 2:
        return [(0, local, 1, LC)]
    return [(0, low, 1, LC + local), (low, cut, 0, LP), (cut, local, 1, LP)]


class Gather:
    def __init__(self, weights, tokens, raw, w_send, w_recv, t_send, t_recv, here):
        g, r, c = lax.axis_index("grp"), lax.axis_index("row"), lax.axis_index("col")
        x, core = g // 2, g % 2
        self.g, self.r, self.c = g, r, c
        half = xor_bit(r, c % 2)
        self.firsts = ((g, r, 2 * half + c // 2), (g, 1 - r, 2 * (1 - half) + c // 2))
        self.alone = 2 * half + c // 2 == c
        self.ranks = (g, (1 - x) * 2 + core, x * 2 + 1 - core)
        self.x_dev, self.core_dev = (self.ranks[1], r, c), (self.ranks[2], r, c)
        self.weights, self.tokens, self.raw = weights, tokens, raw
        self.w_send, self.w_recv, self.t_send, self.t_recv, self.here = w_send, w_recv, t_send, t_recv, here

    def greet(self):
        barrier = pltpu.get_barrier_semaphore()
        for dr in range(2):
            for dc in range(4):
                if dr or dc:
                    device = (self.g, (self.r + dr) % 2, (self.c + dc) % 4)
                    pl.semaphore_signal(barrier, inc=1, device_id=device, device_id_type=MESH)
        for device in (self.x_dev, self.core_dev):
            pl.semaphore_signal(barrier, inc=1, device_id=device, device_id_type=MESH)
        pl.semaphore_wait(barrier, 9)

    def slot(self, n, k, d):
        if self.weights[n][2]:
            return (self.r if d == 0 else 1 - self.r) * 4 + self.ranks[k]
        return 2 * self.ranks[k] + d

    def first_hop(self, n, d):
        src, dst, by_row = self.weights[n]
        at = self.slot(n, 0, 0) if by_row else self.slot(n, 0, d)
        return remote(src, dst.at[at], self.w_send.at[n, d], self.w_recv.at[n, d], self.firsts[d])

    def at_home(self, n):
        src, dst, _ = self.weights[n]
        return pltpu.make_async_copy(src, dst.at[self.slot(n, 0, 0)], self.here.at[n])

    def hop(self, n, d, k, came):
        dst = self.weights[n][1]
        at = self.slot(n, k, d)
        i = (0, 2, 4, 6)[came] + d
        device = self.x_dev if came == 1 else self.core_dev
        return remote(dst.at[at], dst.at[at], self.w_send.at[n, i], self.w_recv.at[n, i], device)

    def begin(self, n):
        @pl.when(self.alone)
        def _():
            self.at_home(n).start()

        @pl.when(jnp.logical_not(self.alone))
        def _():
            self.first_hop(n, 0).start()

        self.first_hop(n, 1).start()

    def forward(self, n):
        for d in range(2):
            if d == 0:

                @pl.when(self.alone)
                def _():
                    self.at_home(n).wait()

                @pl.when(jnp.logical_not(self.alone))
                def _():
                    self.first_hop(n, 0).wait_recv()
            else:
                self.first_hop(n, 1).wait_recv()
            self.hop(n, d, 0, 1).start()
            self.hop(n, d, 0, 2).start()

    def forward_again(self, n):
        for d in range(2):
            self.hop(n, d, 0, 1).wait_recv()
            self.hop(n, d, 1, 3).start()

    def end(self, n):
        for d in range(2):
            self.hop(n, d, 0, 2).wait_recv()
            self.hop(n, d, 1, 3).wait_recv()
            self.hop(n, d, 0, 1).wait_send()
            self.hop(n, d, 0, 2).wait_send()
            self.hop(n, d, 1, 3).wait_send()

        @pl.when(jnp.logical_not(self.alone))
        def _():
            self.first_hop(n, 0).wait_send()

        self.first_hop(n, 1).wait_send()

    def token_copies(self, k):
        copies, mine = [], []
        for a, b, s, at in token_pieces(k, self.tokens.shape[0]):
            for dr in range(2):
                for dc in range(2):
                    target = 2 * s + dc
                    dst = self.raw.at[dr, pl.ds(at, b - a)]
                    src = self.tokens.at[pl.ds(a, b - a)]
                    if dr == 0 and target == k:
                        mine.append(pltpu.make_async_copy(src, dst, self.here.at[2 + len(mine)]))
                    else:
                        device = (self.g, self.r if dr == 0 else 1 - self.r, target)
                        copies.append(remote(src, dst, self.t_send.at[len(copies)], self.t_recv.at[dr], device))
        return copies, mine

    def begin_tokens(self):
        for k in range(4):

            @pl.when(self.c == k)
            def _(k=k):
                copies, mine = self.token_copies(k)
                for copy in mine + copies:
                    copy.start()

    def end_tokens(self):
        for k in range(4):

            @pl.when(self.c == k)
            def _(k=k):
                copies, mine = self.token_copies(k)
                held = sum(b - a for a, b, s, at in token_pieces(k, self.tokens.shape[0]) if s == k // 2)
                rest = self.raw.at[0, pl.ds(0, SEQ - held)]
                pltpu.make_async_copy(rest, rest, self.t_recv.at[0]).wait()
                pltpu.make_async_copy(self.raw.at[1], self.raw.at[1], self.t_recv.at[1]).wait()
                for copy in mine:
                    copy.wait()
                for copy in copies:
                    copy.wait_send()


def gather_semaphores():
    return [pltpu.SemaphoreType.DMA(shape) for shape in ((2, 8), (2, 8), (12,), (2,), (4,))]


def gather_start(tokens, in_i, small, raw, wi, small_all, *sems):
    gather = Gather([(small, small_all, True), (in_i, wi, False)], tokens, raw, *sems)
    gather.greet()
    gather.begin(0)
    gather.begin(1)
    gather.begin_tokens()
    for n in range(2):
        gather.forward(n)
    for n in range(2):
        gather.forward_again(n)
    gather.end_tokens()
    for n in range(2):
        gather.end(n)


def run_gather_start(tokens, in_i, small):
    width = tokens.shape[1]
    return pl.pallas_call(
        gather_start,
        in_specs=[ANY] * 3,
        out_specs=[ANY] * 3,
        out_shape=(
            shaped(2, SEQ, width, dtype=bf16),
            shaped(8, *in_i.shape, dtype=bf16),
            shaped(8, *small.shape, dtype=bf16),
        ),
        scratch_shapes=gather_semaphores(),
        compiler_params=pltpu.CompilerParams(collective_id=0, has_side_effects=True, vmem_limit_bytes=VMEM_LIMIT),
    )(tokens, in_i, small)


LAG = 2


def forward(inner_ref, inv_ref, tail_ref, inv_tail_ref, mix_ref, conv_ref, xproj_ref, dtp_ref, vec_ref, rate_ref, in_g, out_w, cot_in,
            xconv_ref, yfull_ref, starts_ref, xdbl_ref, joined_ref, wg, wo, cot,
            buf, xc_s, part, yr, zs, zr, tail_s, tail_r, state, last, last_r,
            dt_s, u_s, cb_s, h_s, y_s, y_send, y_recv, z_send, z_recv, e_send, e_recv, *sems):
    i = pl.program_id(0)
    gather = Gather([(in_g, wg, False), (out_w, wo, False)], cot_in, cot, *sems)
    g, r, c = gather.g, gather.r, gather.c
    y_dev, z_dev = (g, 1 - r, c), (g, r, c + 1 - 2 * (c % 2))
    far_dev = (g, 1 - r, (c + 2) % 4)
    to_tail = remote(tail_s, tail_r, e_send.at[0], e_recv.at[0], far_dev)
    to_last = remote(last, last_r, e_send.at[1], e_recv.at[1], far_dev)

    def to_y(k):
        return remote(part.at[k], yr.at[k], y_send.at[k], y_recv.at[k], y_dev)

    def to_z(k):
        return remote(zs.at[k], zr.at[k], z_send.at[k], z_recv.at[k], z_dev)

    @pl.when(i == 0)
    def _():
        gather.greet()
        tail_s[...] = inv_tail_ref[...] * tail_ref[...]
        to_tail.start()
        gather.begin(0)
        gather.begin(1)
        buf[0:8] = jnp.zeros_like(buf[0:8])
        state[...] = jnp.zeros_like(state)

    mix = mix_ref[...]

    @pl.when(i == PC)
    def _():
        to_tail.wait()
        joined = mix * tail_s[...] + (1.0 - mix) * tail_r[...]
        buf[0:8] = joined
        joined_ref[...] = joined

    @pl.when((i > 0) & (i < PC))
    def _():
        buf[0:8] = buf[CH : CH + 8]

    @pl.when(i < NCH)
    def _():
        buf[8 : CH + 8] = inv_ref[...] * inner_ref[...]
        out = conv_ref[4:5]
        for k in range(KCONV):
            out = out + conv_ref[k : k + 1] * buf[5 + k : 5 + k + CH]
        xconv = (out * jax.nn.sigmoid(out)).astype(bf16)
        xconv_ref[...] = xconv
        xc_s[i] = xconv
        part[i] = dot_nt(xproj_ref[...], xconv)
        to_y(i).start()

    @pl.when((i >= LAG) & (i < NCH + LAG))
    def _():
        k = i - LAG
        to_y(k).wait_recv()
        zs[k] = part[k] + yr[k]
        to_z(k).start()

    @pl.when((i >= 2 * LAG) & (i < NCH + 2 * LAG))
    def _():
        k = i - 2 * LAG
        to_z(k).wait_recv()
        xdbl_ref[k] = zs[k] + zr[k]

    @pl.when(i == NCH)
    def _():
        gather.begin_tokens()

    @pl.when(i == NCH + 2)
    def _():
        gather.forward(0)

    @pl.when(i == NCH + 4)
    def _():
        gather.forward(1)

    @pl.when(i == NCH + 6)
    def _():
        gather.forward_again(0)

    @pl.when(i == 2 * NCH - 1)
    def _():
        to_last.wait()
        state[...] = mix_ref[0:1] * last[...] + (1.0 - mix_ref[0:1]) * last_r[...]

    @pl.when(i >= NCH)
    def _():
        k = i - NCH
        starts_ref[0] = state[...]
        h, yfull = scan_chunk(xdbl_ref.at[k], xc_s[k].astype(f32), dtp_ref, vec_ref, rate_ref, state[...], dt_s, u_s, cb_s, h_s, y_s)
        state[...] = h
        yfull_ref[...] = yfull.astype(bf16)

    @pl.when(i == 2 * NCH - 2)
    def _():
        last[...] = state[...]
        to_last.start()

    @pl.when(i == 2 * NCH - 1)
    def _():
        gather.forward_again(1)
        gather.end_tokens()
        gather.end(0)
        gather.end(1)

        def sent(k, _):
            to_y(k).wait_send()
            to_z(k).wait_send()
            return 0

        lax.fori_loop(0, NCH, sent, 0)


def run_forward(inner, inv, mix, conv, xproj, dtp, vec, rate, in_g, out_w, cot):
    w = inner.shape[1]
    first = lambda i: jnp.minimum(i, NCH - 1)
    second = lambda i: jnp.maximum(i - NCH, 0)
    tail = lambda i: (LP // 8 - 1, 0)
    dma = pltpu.SemaphoreType.DMA
    sums = pltpu.VMEM((NCH, XW, CH), f32)
    return pl.pallas_call(
        forward,
        grid=(2 * NCH,),
        in_specs=[
            rows_of(w, first),
            rows_of(1, first),
            pl.BlockSpec((8, w), tail),
            pl.BlockSpec((8, 1), tail),
            whole(8, w),
            whole(8, w),
            whole(XW, w),
            whole(RANK, w),
            whole(8, w),
            whole(NSTATE, w),
            ANY,
            ANY,
            ANY,
        ],
        out_specs=(
            rows_of(w, first),
            rows_of(w, second),
            pl.BlockSpec((1, NSTATE, w), lambda i: (second(i), 0, 0)),
            whole(NCH, XW, CH),
            whole(8, w),
            ANY,
            ANY,
            ANY,
        ),
        out_shape=(
            shaped(SEQ, w, dtype=bf16),
            shaped(SEQ, w, dtype=bf16),
            shaped(NCH, NSTATE, w),
            shaped(NCH, XW, CH),
            shaped(8, w),
            shaped(8, *in_g.shape, dtype=bf16),
            shaped(8, *out_w.shape, dtype=bf16),
            shaped(2, SEQ, cot.shape[1], dtype=bf16),
        ),
        scratch_shapes=[
            pltpu.VMEM((CH + 8, w), f32),
            pltpu.VMEM((NCH, CH, w), bf16),
            sums,
            sums,
            sums,
            sums,
            pltpu.VMEM((8, w), f32),
            pltpu.VMEM((8, w), f32),
            pltpu.VMEM((NSTATE, w), f32),
            pltpu.VMEM((NSTATE, w), f32),
            pltpu.VMEM((NSTATE, w), f32),
            *scan_scratch(w),
            dma((NCH,)),
            dma((NCH,)),
            dma((NCH,)),
            dma((NCH,)),
            dma((2,)),
            dma((2,)),
            *gather_semaphores(),
        ],
        compiler_params=pltpu.CompilerParams(
            dimension_semantics=("arbitrary",), collective_id=2, has_side_effects=True, vmem_limit_bytes=VMEM_LIMIT
        ),
        cost_estimate=pl.CostEstimate(flops=60 * 1000000000, bytes_accessed=1000000, transcendentals=0),
    )(inner, inv, inner, inv, mix, conv, xproj, dtp, vec, rate, in_g, out_w, cot)


def project_first(raw_ref, gain_ref, w_ref, normed_ref, inv_ref, out_ref):
    low = raw_ref[0].astype(f32)
    high = raw_ref[1].astype(f32)
    squares = jnp.sum(low * low + high * high, axis=1, keepdims=True)
    inv_ref[...] = lax.rsqrt(squares / D + eps)
    low = (low * gain_ref[0:1]).astype(bf16)
    high = (high * gain_ref[1:2]).astype(bf16)
    normed_ref[0] = low
    normed_ref[1] = high
    n = w_ref.shape[2]
    for k in range(SLOTS):
        out_ref[:, k * n : (k + 1) * n] = dot_nn(low, w_ref[2 * k]) + dot_nn(high, w_ref[2 * k + 1])


def split_rows(width, at, tall=CH):
    return pl.BlockSpec((2, tall, width), lambda i: (0, at(i), 0))


def run_project_first(raw, gain, w):
    width = raw.shape[2]
    at = lambda i: i
    n = SLOTS * w.shape[2]
    return call(
        project_first,
        BIG_STEPS,
        (raw, gain, w),
        [split_rows(width, at, BIG), whole(2, width), whole(*w.shape)],
        (shaped(2, SEQ, width, dtype=bf16), shaped(SEQ, 1), shaped(SEQ, n)),
        (split_rows(width, at, BIG), rows_of(1, at, BIG), rows_of(n, at, BIG)),
        [],
        9,
    )


def gate_backward(normed_ref, wg_ref, cot_ref, wo_ref, yfull_ref, inv_ref, gated_ref, dy_ref, dproj_ref, dscale_ref, own_ref, oth_ref, gate_s):
    n = wo_ref.shape[2]
    for k in range(SLOTS):
        gate_s[:, k * n : (k + 1) * n] = dot_nn(normed_ref[0], wg_ref[2 * k]) + dot_nn(normed_ref[1], wg_ref[2 * k + 1])
    d_gated = jnp.zeros(dy_ref.shape, f32)
    for k in range(SLOTS):
        for d in range(2):
            d_gated = d_gated + dot_nt(cot_ref[d, :, k * n : (k + 1) * n], wo_ref[2 * k + d])
    gate_in = gate_s[...]
    inv = inv_ref[...]
    yfull = yfull_ref[...].astype(f32)
    gate = inv * gate_in
    sig = jax.nn.sigmoid(gate)
    passed = gate * sig
    gated = (yfull * passed).astype(bf16)
    gated_ref[...] = gated
    for k in range(SLOTS):
        own_ref[:, k * n : (k + 1) * n] = dot_nn(gated, wo_ref[2 * k])
        oth_ref[:, k * n : (k + 1) * n] = dot_nn(gated, wo_ref[2 * k + 1]).astype(bf16)
    dy_ref[...] = d_gated * passed
    d_gate = d_gated * yfull * (sig * (1.0 + gate * (1.0 - sig)))
    dproj_ref[...] = (inv * d_gate).astype(bf16)
    dscale_ref[...] = jnp.sum(d_gate * gate_in, axis=1, keepdims=True)


def run_gate_backward(normed, wg, cot, wo, yfull, inv):
    width = cot.shape[2]
    w = yfull.shape[1]
    at = lambda i: i
    return call(
        gate_backward,
        BIG_STEPS,
        (normed, wg, cot, wo, yfull, inv),
        [split_rows(width, at, BIG), whole(*wg.shape), split_rows(width, at, BIG), whole(*wo.shape), rows_of(w, at, BIG), rows_of(1, at, BIG)],
        (shaped(SEQ, w, dtype=bf16), shaped(SEQ, w), shaped(SEQ, w, dtype=bf16), shaped(SEQ, 1), shaped(SEQ, width), shaped(SEQ, width, dtype=bf16)),
        (rows_of(w, at, BIG), rows_of(w, at, BIG), rows_of(w, at, BIG), rows_of(1, at, BIG), rows_of(width, at, BIG), rows_of(width, at, BIG)),
        [pltpu.VMEM((BIG, w), f32)],
        22,
    )


def normed_backward(inner_ref, gate_ref, wi_ref, wg_ref, own_ref, oth_ref):
    n = wi_ref.shape[2]
    for d, out_ref in ((1, oth_ref), (0, own_ref)):
        total = jnp.zeros(out_ref.shape, f32)
        for k in range(SLOTS):
            total = total + dot_nt(inner_ref[:, k * n : (k + 1) * n], wi_ref[2 * k + d])
            total = total + dot_nt(gate_ref[:, k * n : (k + 1) * n], wg_ref[2 * k + d])
        out_ref[...] = total.astype(out_ref.dtype)


def run_normed_backward(d_inner, d_gate, wi, wg):
    w = d_inner.shape[1]
    width = wi.shape[1]
    at = lambda i: i
    return call(
        normed_backward,
        BIG_STEPS,
        (d_inner, d_gate, wi, wg),
        [rows_of(w, at, BIG), rows_of(w, at, BIG), whole(*wi.shape), whole(*wg.shape)],
        (shaped(SEQ, width), shaped(SEQ, width, dtype=bf16)),
        (rows_of(width, at, BIG), rows_of(width, at, BIG)),
        [],
        12,
    )


def finish(inner_hbm, gate_hbm, normed_hbm, raw_hbm, wi_hbm, wg_hbm, dn_ref, grad_ref, gain_ref,
           inner, gate, normed, raw, wi, wg, cs, cr, kept, xs, xr, fs, fr, ys, yr, zs, zr, own, gs, gr,
           loc, c_send, c_recv, x_send, x_recv, f_send, f_recv, y_send, y_recv, z_send, z_recv, b_send, b_recv, g_send, g_recv):
    g, r, c = lax.axis_index("grp"), lax.axis_index("row"), lax.axis_index("col")
    x, core, s, p = g // 2, g % 2, c // 2, c % 2
    tall, width = raw.shape
    part = tall // 2
    n = wi.shape[2]
    q = 2 * p + xor_bit(r, s)
    y_dev, z_dev = (g, 1 - r, c), (g, r, 2 * s + 1 - p)
    x_dev, core_dev = ((1 - x) * 2 + core, r, c), (2 * x + 1 - core, r, c)
    alone = q == c

    loads = [
        pltpu.make_async_copy(normed_hbm, normed, loc.at[0]),
        pltpu.make_async_copy(inner_hbm, inner, loc.at[1]),
        pltpu.make_async_copy(gate_hbm, gate, loc.at[2]),
        pltpu.make_async_copy(wi_hbm, wi, loc.at[3]),
        pltpu.make_async_copy(wg_hbm, wg, loc.at[4]),
        pltpu.make_async_copy(raw_hbm.at[0, pl.ds(pl.multiple_of(p * tall, 64), tall)], raw, loc.at[5]),
    ]
    for copy in loads:
        copy.start()

    barrier = pltpu.get_barrier_semaphore()
    for dg in range(4):
        for dc in range(4):
            if dg or dc:
                pl.semaphore_signal(barrier, inc=1, device_id=((g + dg) % 4, r, (c + dc) % 4), device_id_type=MESH)
    for dc in range(4):
        pl.semaphore_signal(barrier, inc=1, device_id=(g, 1 - r, (c + dc) % 4), device_id_type=MESH)
    pl.semaphore_wait(barrier, 19)

    def weight_grad(d, block, store):
        cols = pl.ds(pl.multiple_of(block * n, 128), n)

        def tile(t, _):
            rows = pl.ds(pl.multiple_of(t * n, 128), n)
            store(rows, dot_tn(normed[d, :, rows], inner[:, cols]))
            return 0

        lax.fori_loop(0, width // n, tile, 0)

    def to_core(i, d):
        return remote(cs.at[i, d], cr.at[i, d], c_send.at[2 * i + d], c_recv.at[2 * i + d], core_dev)

    def to_x(d):
        return remote(xs.at[d], xr.at[d], x_send.at[d], x_recv.at[d], x_dev)

    def to_owner(d):
        return remote(fs.at[d], fr.at[d], f_send.at[d], f_recv.at[d], (g, r if d == 0 else 1 - r, q))

    def grad_to_core(i):
        block = 2 * (1 - x if i == 0 else x) + 1 - core
        for d in range(2):

            def store(rows, v, d=d):
                cs[i, d, rows, :] = v.astype(bf16)

            weight_grad(d, block, store)
            to_core(i, d).start()

    def start_of(mine, h):
        return pl.multiple_of((p if mine else 1 - p) * tall + h * part, 32)

    def normed_part(mine, h, d, store):
        rows = pl.ds(start_of(mine, h), part)

        def tile(t, _):
            cols = pl.ds(pl.multiple_of(t * n, 128), n)
            total = dot_nt(inner[rows, 0:n], wi[d, cols, :])
            for j in range(1, SLOTS):
                total = total + dot_nt(inner[rows, j * n : (j + 1) * n], wi[2 * j + d, cols, :])
            for j in range(SLOTS):
                total = total + dot_nt(gate[rows, j * n : (j + 1) * n], wg[2 * j + d, cols, :])
            store(cols, total)
            return 0

        lax.fori_loop(0, width // n, tile, 0)

    def to_y(i):
        return remote(ys.at[i], yr.at[i], y_send.at[i], y_recv.at[i], y_dev)

    def to_z(i):
        return remote(zs.at[i], zr.at[i], z_send.at[i], z_recv.at[i], z_dev)

    def into(ref, i, added=None):
        def store(cols, v):
            if added is not None:
                v = v + added[0, :, cols].astype(f32)
            ref[i, :, cols] = v.astype(bf16)

        return store

    loads[0].wait()
    loads[1].wait()
    grad_to_core(0)
    for copy in loads[2:5]:
        copy.wait()
    normed_part(False, 0, 1, into(ys, 0))
    to_y(0).start()
    normed_part(False, 1, 1, into(zs, 0))
    to_z(0).start()
    grad_to_core(1)

    for d in range(2):

        def hold(rows, v, d=d):
            kept[d, rows, :] = v

        weight_grad(d, 2 * (1 - x) + core, hold)
    for d in range(2):
        to_core(0, d).wait_recv()
        xs[d] = (kept[d] + cr[0, d].astype(f32)).astype(bf16)
        to_x(d).start()

    normed_part(False, 1, 0, into(zs, 2))
    to_z(2).start()
    normed_part(True, 0, 1, into(ys, 1))
    to_y(1).start()
    to_y(0).wait_recv()
    normed_part(False, 0, 0, into(zs, 1, yr))
    to_z(1).start()
    to_z(0).wait_recv()
    normed_part(True, 1, 1, into(ys, 2, zr))
    to_y(2).start()

    for d in range(2):

        def hold(rows, v, d=d):
            kept[d, rows, :] = v

        weight_grad(d, 2 * x + core, hold)
    for d in range(2):
        to_core(1, d).wait_recv()
        to_x(d).wait_recv()
        fs[d] = (kept[d] + cr[1, d].astype(f32) + xr[d].astype(f32)).astype(bf16)
        if d == 0:

            @pl.when(alone)
            def _():
                fr[0] = fs[0]

            @pl.when(jnp.logical_not(alone))
            def _():
                to_owner(0).start()
        else:
            to_owner(1).start()

    for h in range(2):

        def store(cols, v, h=h):
            own[h * part : (h + 1) * part, cols] = v

        normed_part(True, h, 0, store)

    loads[5].wait()
    for h in range(2):
        to_y(1 + h).wait_recv()
        to_z(1 + h).wait_recv()
        total = own[h * part : (h + 1) * part, :] + yr[1 + h].astype(f32) + zr[1 + h].astype(f32)
        own[h * part : (h + 1) * part, :] = total
        product = total * raw[h * part : (h + 1) * part, :].astype(f32)
        folded = jnp.sum(product.reshape(part // 8, 8, width), axis=0)
        for b in range(SLOTS):
            if h == 0:
                gs[b] = folded[:, b * n : (b + 1) * n]
            else:
                gs[b] = gs[b] + folded[:, b * n : (b + 1) * n]

    cut = tall - LC
    low = cut - LC
    moves = {
        0: ([(0, tall, 0)], None),
        1: ([(0, cut, 0)], (cut, 3, low)),
        2: ([(LC, tall, 0)], (0, 1, cut)),
        3: ([(LC, cut, 0), (cut, tall, cut)], (0, 2, cut)),
    }

    def border(k):
        stays, leaves = moves[k]
        mine = [pltpu.make_async_copy(own.at[a:b], dn_ref.at[at : at + b - a], loc.at[i]) for i, (a, b, at) in enumerate(stays)]
        if leaves is None:
            return mine, None
        a, to, at = leaves
        return mine, remote(own.at[a : a + LC], dn_ref.at[at : at + LC], b_send.at[0], b_recv.at[0], (g, r, to))

    for k in range(4):

        @pl.when(c == k)
        def _(k=k):
            mine, gone = border(k)
            if gone is not None:
                gone.start()
            for copy in mine:
                copy.start()

    def gain_copy(dg, dc):
        to = ((g + dg) % 4, r, (c + dc) % 4)
        i = 4 * dg + dc - 1
        return remote(gs.at[(g + dg) % 4], gr.at[i], g_send.at[i], g_recv.at[0], to)

    pairs = [(dg, dc) for dg in range(4) for dc in range(4) if dg or dc]
    for dg, dc in pairs:
        gain_copy(dg, dc).start()

    @pl.when(jnp.logical_not(alone))
    def _():
        to_owner(0).wait_recv()

    to_owner(1).wait_recv()
    grad_ref[...] = fr[0].astype(f32) + fr[1].astype(f32)

    pltpu.make_async_copy(gr, gr, g_recv.at[0]).wait()
    gain_ref[...] = jnp.sum(gr[...], axis=0) + gs[g]

    for k in range(4):

        @pl.when(c == k)
        def _(k=k):
            mine, gone = border(k)
            for copy in mine:
                copy.wait()
            if gone is not None:
                gone.wait()

    for dg, dc in pairs:
        gain_copy(dg, dc).wait_send()
    for i in range(3):
        to_y(i).wait_send()
        to_z(i).wait_send()
    for d in range(2):
        for i in range(2):
            to_core(i, d).wait_send()
        to_x(d).wait_send()

    @pl.when(jnp.logical_not(alone))
    def _():
        to_owner(0).wait_send()

    to_owner(1).wait_send()


def run_finish(d_inner, d_gate, normed, raw, wi, wg):
    w = d_inner.shape[1]
    width, n = wi.shape[1], wi.shape[2]
    tall = SEQ // 2
    part = tall // 2
    dma = pltpu.SemaphoreType.DMA
    low = lambda *shape: pltpu.VMEM(shape, bf16)
    vmem = pl.BlockSpec(memory_space=pltpu.VMEM)
    return pl.pallas_call(
        finish,
        in_specs=[ANY] * 6,
        out_specs=[ANY, vmem, vmem],
        out_shape=(shaped(tall, width), shaped(width, n), shaped(8, n)),
        scratch_shapes=[
            low(SEQ, w),
            low(SEQ, w),
            low(2, SEQ, width),
            low(tall, width),
            low(2 * SLOTS, width, n),
            low(2 * SLOTS, width, n),
            low(2, 2, width, n),
            low(2, 2, width, n),
            pltpu.VMEM((2, width, n), f32),
            low(2, width, n),
            low(2, width, n),
            low(2, width, n),
            low(2, width, n),
            low(3, part, width),
            low(3, part, width),
            low(3, part, width),
            low(3, part, width),
            pltpu.VMEM((tall, width), f32),
            pltpu.VMEM((SLOTS, 8, n), f32),
            pltpu.VMEM((15, 8, n), f32),
            dma((6,)),
            dma((4,)),
            dma((4,)),
            dma((2,)),
            dma((2,)),
            dma((2,)),
            dma((2,)),
            dma((3,)),
            dma((3,)),
            dma((3,)),
            dma((3,)),
            dma((1,)),
            dma((1,)),
            dma((15,)),
            dma((1,)),
        ],
        compiler_params=pltpu.CompilerParams(collective_id=1, has_side_effects=True, vmem_limit_bytes=VMEM_LIMIT),
        cost_estimate=pl.CostEstimate(flops=60 * 1000000000, bytes_accessed=1000000, transcendentals=0),
    )(d_inner, d_gate, normed, raw, wi, wg)


def late_parts(order_ref, normed_ref, gate_ref, gated_ref, cot_ref, gate_sent, out_sent, gate_kept, out_kept):
    t = pl.program_id(0)
    for d in range(2):
        low = dot_tn(normed_ref[d], gate_ref[...])
        high = dot_tn(gated_ref[...], cot_ref[d])

        @pl.when(t < 2)
        def _(d=d, low=low, high=high):
            gate_sent[0, d] = low.astype(bf16)
            out_sent[0, d] = high.astype(bf16)

        @pl.when(t >= 2)
        def _(d=d, low=low, high=high):
            gate_kept[0, d] = low
            out_kept[0, d] = high


def run_late_parts(order, normed, d_gate, gated, cot):
    width = normed.shape[2]
    w = gated.shape[1]
    n = w // SLOTS
    sent = pl.BlockSpec((1, 2, width, n), lambda t, o: (jnp.minimum(t, 1), 0, 0, 0))
    kept = pl.BlockSpec((1, 2, width, n), lambda t, o: (jnp.maximum(t - 2, 0), 0, 0, 0))
    return pl.pallas_call(
        late_parts,
        grid_spec=pltpu.PrefetchScalarGridSpec(
            num_scalar_prefetch=1,
            grid=(SLOTS,),
            in_specs=[
                pl.BlockSpec((2, SEQ, width), lambda t, o: (0, 0, 0)),
                pl.BlockSpec((SEQ, n), lambda t, o: (0, o[t])),
                pl.BlockSpec((SEQ, w), lambda t, o: (0, 0)),
                pl.BlockSpec((2, SEQ, n), lambda t, o: (0, 0, o[t])),
            ],
            out_specs=(sent, sent, kept, kept),
        ),
        out_shape=(shaped(2, 2, width, n, dtype=bf16), shaped(2, 2, width, n, dtype=bf16), shaped(2, 2, width, n), shaped(2, 2, width, n)),
        compiler_params=pltpu.CompilerParams(dimension_semantics=("arbitrary",), vmem_limit_bytes=VMEM_LIMIT),
        cost_estimate=pl.CostEstimate(flops=14 * 1000000000, bytes_accessed=1000000, transcendentals=0),
    )(order, normed, d_gate, gated, cot)


PIECES = 8
PIECE = SEQ // PIECES
PIECE_STEP = (0, 0, 1, 1, 2, 3, 4, 5)


def border_moves(tall):
    cut = tall - LC
    low = cut - LC
    return {
        0: ([(0, tall, 0)], None),
        1: ([(0, cut, 0)], (cut, 3, low)),
        2: ([(LC, tall, 0)], (0, 1, cut)),
        3: ([(LC, cut, 0), (cut, tall, cut)], (0, 2, cut)),
    }


def backward(xdbl_ref, xconv_ref, dy_ref, dtp_ref, vec_ref, rate_ref, starts_ref, mix_ref, into_ref, sent_hbm, kept_hbm, own_hbm, oth_hbm,
             dxdbl_ref, dxc_ref, alog_ref, sums_ref, dtpg_ref, grad_ref, branch_ref,
             first, first_s, first_r, part, yr, zs, zr, cr, kp, xs, xr, fs, fr, out, own, by, bz_s, bz, fin,
             y_send, y_recv, z_send, z_recv, e_send, e_recv, c_send, c_recv, x_send, x_recv, f_send, f_recv,
             p_send, p_recv, q_send, q_recv, b_send, b_recv, load_k, load_o, stay, put, *scratch):
    i = pl.program_id(0)
    g, r, c = lax.axis_index("grp"), lax.axis_index("row"), lax.axis_index("col")
    x, core, s, p = g // 2, g % 2, c // 2, c % 2
    q = 2 * p + xor_bit(r, s)
    tall = SEQ // 2
    alone = q == c
    y_dev, z_dev, far_dev = (g, 1 - r, c), (g, r, 2 * s + 1 - p), (g, 1 - r, (c + 2) % 4)
    x_dev, core_dev = ((1 - x) * 2 + core, r, c), (2 * x + 1 - core, r, c)
    to_first = remote(first_s, first_r, e_send.at[0], e_recv.at[0], far_dev)

    def to_y(k):
        return remote(part.at[k], yr.at[k], y_send.at[k], y_recv.at[k], y_dev)

    def to_z(k):
        return remote(zs.at[k], zr.at[k], z_send.at[k], z_recv.at[k], z_dev)

    def to_core(n, j):
        return remote(sent_hbm[n].at[j], cr.at[n, j], c_send.at[n, j], c_recv.at[n, j], core_dev)

    def load(n, j):
        return pltpu.make_async_copy(kept_hbm[n].at[j], kp.at[n], load_k.at[n])

    def to_x(n):
        return remote(xs.at[n], xr.at[n], x_send.at[n], x_recv.at[n], x_dev)

    def to_owner(n, d):
        return remote(fs.at[n, d], fr.at[n, d], f_send.at[n, d], f_recv.at[n, d], (g, r if d == 0 else 1 - r, q))

    def rows_at(m):
        base = (1 - p) if m < PIECES // 2 else p
        return pl.ds(pl.multiple_of(base * tall + (m % (PIECES // 2)) * PIECE, 16), PIECE)

    def branch_y(m):
        return remote(oth_hbm.at[rows_at(m)], by.at[m], p_send.at[m], p_recv.at[m], y_dev)

    def branch_z(m):
        return remote(bz_s.at[m], bz.at[m], q_send.at[m], q_recv.at[m], z_dev)

    def border(k):
        stays, leaves = border_moves(tall)[k]
        mine = [pltpu.make_async_copy(fin.at[a:b], branch_ref.at[at : at + b - a], stay.at[n]) for n, (a, b, at) in enumerate(stays)]
        if leaves is None:
            return mine, None
        a, to, at = leaves
        return mine, remote(fin.at[a : a + LC], branch_ref.at[at : at + LC], b_send.at[0], b_recv.at[0], (g, r, to))

    def at_border(act):
        for k in range(4):

            @pl.when(c == k)
            def _(k=k):
                act(*border(k))

    @pl.when(i == 0)
    def _():
        barrier = pltpu.get_barrier_semaphore()
        for dr in range(2):
            for dc in range(4):
                if dr or dc:
                    pl.semaphore_signal(barrier, inc=1, device_id=(g, (r + dr) % 2, (c + dc) % 4), device_id_type=MESH)
        for device in (x_dev, core_dev):
            pl.semaphore_signal(barrier, inc=1, device_id=device, device_id_type=MESH)
        pl.semaphore_wait(barrier, 9)
        for n in range(2):
            for j in range(2):
                to_core(n, j).start()
            load(n, 0).start()
        pltpu.make_async_copy(own_hbm, own, load_o.at[0]).start()
        first[...] = jnp.zeros_like(first)
        alog_ref[...] = jnp.zeros_like(alog_ref)
        sums_ref[...] = jnp.zeros_like(sums_ref)
        dtpg_ref[...] = jnp.zeros_like(dtpg_ref)

    @pl.when(i == 1)
    def _():
        to_first.wait()
        first[...] = mix_ref[0:1] * first_s[...] + into_ref[0:1] * first_r[...]

    chunk_backward(xdbl_ref, xconv_ref, dy_ref, dtp_ref, vec_ref, rate_ref, starts_ref, part.at[i], dxc_ref, alog_ref, sums_ref, dtpg_ref, first, *scratch)

    @pl.when(i == 0)
    def _():
        first_s[...] = first[...]
        to_first.start()

    @pl.when(i == 1)
    def _():
        pltpu.make_async_copy(own_hbm, own, load_o.at[0]).wait()
        for n in range(2):
            to_core(n, 0).wait_recv()
            load(n, 0).wait()
            xs[n] = (kp[n] + cr[n, 0].astype(f32)).astype(bf16)
            to_x(n).start()
            load(n, 1).start()

    for n in range(2):

        @pl.when(i == 3 + n)
        def _(n=n):
            load(n, 1).wait()
            to_core(n, 1).wait_recv()
            to_x(n).wait_recv()
            fs[n] = (kp[n] + cr[n, 1].astype(f32) + xr[n].astype(f32)).astype(bf16)

            @pl.when(alone)
            def _():
                fr[n, 0] = fs[n, 0]

            @pl.when(jnp.logical_not(alone))
            def _():
                to_owner(n, 0).start()

            to_owner(n, 1).start()

        @pl.when(i == 6 + n)
        def _(n=n):
            @pl.when(jnp.logical_not(alone))
            def _():
                to_owner(n, 0).wait_recv()

            to_owner(n, 1).wait_recv()
            out[n] = fr[n, 0].astype(f32) + fr[n, 1].astype(f32)
            pltpu.make_async_copy(out.at[n], grad_ref.at[n], put.at[n]).start()

    for m in range(PIECES):

        @pl.when(i == PIECE_STEP[m] + 1)
        def _(m=m):
            branch_y(m).wait_recv()
            total = own[rows_at(m), :] + by[m].astype(f32)
            if m < PIECES // 2:
                bz_s[m] = total.astype(bf16)
                branch_z(m).start()
            else:
                j = m - PIECES // 2
                branch_z(j).wait_recv()
                fin[j * PIECE : (j + 1) * PIECE, :] = (total + bz[j].astype(f32)).astype(bf16)

    @pl.when(i == 7)
    def _():
        def begin(mine, gone):
            if gone is not None:
                gone.start()
            for copy in mine:
                copy.start()

        at_border(begin)

    @pl.when((i >= 1) & (i <= NCH - 1))
    def _():
        k = i - 1
        to_y(k).wait_recv()
        zs[k] = part[k] + yr[k]
        to_z(k).start()

    @pl.when(i >= 3)
    def _():
        k = i - 3
        to_z(k).wait_recv()
        dxdbl_ref[NCH - 1 - k] = zs[k] + zr[k]

    to_y(i).start()
    for m in range(PIECES):

        @pl.when(i == PIECE_STEP[m])
        def _(m=m):
            branch_y(m).start()

    @pl.when(i == NCH - 1)
    def _():
        to_y(NCH - 1).wait_recv()
        zs[NCH - 1] = part[NCH - 1] + yr[NCH - 1]
        to_z(NCH - 1).start()
        for k in (NCH - 3, NCH - 2, NCH - 1):
            to_z(k).wait_recv()
            dxdbl_ref[NCH - 1 - k] = zs[k] + zr[k]

        def finish_border(mine, gone):
            for copy in mine:
                copy.wait()
            if gone is not None:
                gone.wait()

        at_border(finish_border)

        def sent(k, _):
            to_y(k).wait_send()
            to_z(k).wait_send()
            return 0

        lax.fori_loop(0, NCH, sent, 0)
        for n in range(2):
            for j in range(2):
                to_core(n, j).wait_send()
            to_x(n).wait_send()

            @pl.when(jnp.logical_not(alone))
            def _(n=n):
                to_owner(n, 0).wait_send()

            to_owner(n, 1).wait_send()
            pltpu.make_async_copy(out.at[n], grad_ref.at[n], put.at[n]).wait()
        for m in range(PIECES):
            branch_y(m).wait_send()
            if m < PIECES // 2:
                branch_z(m).wait_send()


def backward_kernel(*refs):
    backward(*refs[:9], refs[9:11], refs[11:13], *refs[13:])


def run_backward(xdbl, xconv, dy, dtp, vec, rate, starts, mix, into, sent, kept, own, oth):
    w = xconv.shape[1]
    width = own.shape[1]
    _, _, tall, n = sent[0].shape
    at = lambda i: NCH - 1 - i
    dma = pltpu.SemaphoreType.DMA
    low = lambda *shape: pltpu.VMEM(shape, bf16)
    sums = pltpu.VMEM((NCH, XW, CH), f32)
    state = pltpu.VMEM((NSTATE, w), f32)
    return pl.pallas_call(
        backward_kernel,
        grid=(NCH,),
        in_specs=[
            chunk_of(XW, at),
            rows_of(w, at),
            rows_of(w, at),
            whole(RANK, w),
            whole(8, w),
            whole(NSTATE, w),
            pl.BlockSpec((1, NSTATE, w), lambda i: (at(i), 0, 0)),
            whole(8, w),
            whole(8, w),
        ]
        + [ANY] * 6,
        out_specs=(whole(NCH, XW, CH), rows_of(w, at), whole(NSTATE, w), whole(8, w), whole(RANK, w), ANY, ANY),
        out_shape=(
            shaped(NCH, XW, CH),
            shaped(SEQ, w),
            shaped(NSTATE, w),
            shaped(8, w),
            shaped(RANK, w),
            shaped(2, tall, n),
            shaped(SEQ // 2, width, dtype=bf16),
        ),
        scratch_shapes=[
            state,
            state,
            state,
            sums,
            sums,
            sums,
            sums,
            low(2, 2, 2, tall, n),
            pltpu.VMEM((2, 2, tall, n), f32),
            low(2, 2, tall, n),
            low(2, 2, tall, n),
            low(2, 2, tall, n),
            low(2, 2, tall, n),
            pltpu.VMEM((2, tall, n), f32),
            pltpu.VMEM((SEQ, width), f32),
            low(PIECES, PIECE, width),
            low(PIECES // 2, PIECE, width),
            low(PIECES // 2, PIECE, width),
            low(SEQ // 2, width),
            dma((NCH,)),
            dma((NCH,)),
            dma((NCH,)),
            dma((NCH,)),
            dma((1,)),
            dma((1,)),
            dma((2, 2)),
            dma((2, 2)),
            dma((2,)),
            dma((2,)),
            dma((2, 2)),
            dma((2, 2)),
            dma((PIECES,)),
            dma((PIECES,)),
            dma((PIECES // 2,)),
            dma((PIECES // 2,)),
            dma((1,)),
            dma((1,)),
            dma((2,)),
            dma((1,)),
            dma((2,)),
            dma((2,)),
            *backward_scratch(w),
        ],
        compiler_params=pltpu.CompilerParams(
            dimension_semantics=("arbitrary",), collective_id=3, has_side_effects=True, vmem_limit_bytes=61 * 1024 * 1024
        ),
        cost_estimate=pl.CostEstimate(flops=120 * 1000000000, bytes_accessed=1000000, transcendentals=0),
    )(xdbl, xconv, dy, dtp, vec, rate, starts, mix, into, *sent, *kept, own, oth)


def per_device(
    tokens,
    gain,
    in_proj,
    conv_weight,
    conv_bias,
    x_proj,
    dt_proj,
    dt_bias,
    a_log,
    d_skip,
    out_proj,
    table,
    cotangent,
):
    row = lax.axis_index("row")
    col = lax.axis_index("col")
    grp = lax.axis_index("grp")
    low_row = row == 0
    low_pair = col % 2 == 0
    half = col // 2
    places = [(r, c) for r in range(2) for c in range(4)]
    quick = lax.axis_size("grp") == 4

    def spot(r, c):
        return r * 4 + c

    def send(v, pairs):
        return lax.ppermute(v, ("row", "col"), [(spot(*a), spot(*b)) for a, b in pairs])

    def swap(v):
        return send(v, [((r, c), (1 - r, c)) for r, c in places])

    def pair(v):
        return send(v, [((r, c), (r, c ^ 1)) for r, c in places])

    def across(v):
        return send(v, [((r, c), (1 - r, c ^ 2)) for r, c in places])

    def quarter_spot(q, s):
        return ((q & 1) ^ s, 2 * s + (q >> 1))

    same = [((r, q), quarter_spot(q, r ^ (q & 1))) for r, q in places]
    other = [((r, q), quarter_spot(q, 1 ^ r ^ (q & 1))) for r, q in places]
    spread = [((r, q), quarter_spot(q, r)) for r, q in places]

    def back(pairs):
        return [(b, a) for a, b in pairs]

    def flip(v, bit):
        return lax.ppermute(v, "grp", [(g, g ^ bit) for g in range(4)])

    def scatter_grp(v, axis):
        return lax.psum_scatter(v, "grp", scatter_dimension=axis, tiled=True)

    def by_pair(own, paired):
        return jnp.where(low_pair, own, paired), jnp.where(low_pair, paired, own)

    local = tokens.shape[0]
    cut = local - LC
    tail_at = cut - LC

    def to_sequences(v):
        got = send(jnp.where(col == 3, v[tail_at:cut], v[cut:]), [((r, a), (r, b)) for r in range(2) for a, b in ((1, 2), (2, 3), (3, 1))])
        low = jnp.concatenate([v[:cut], jnp.where(col == 0, v[cut:], got)], axis=0)
        two = jnp.concatenate([got, v[:cut]], axis=0)
        three = jnp.concatenate([got, v[:tail_at], v[cut:]], axis=0)
        return jnp.where(col < 2, low, jnp.where(col == 2, two, three))

    def from_sequences(v):
        got = send(jnp.where(col == 1, v[cut:], v[:LC]), [((r, b), (r, a)) for r in range(2) for a, b in ((1, 2), (2, 3), (3, 1))])
        low = jnp.concatenate([v[:cut], jnp.where(col == 0, v[cut:], got)], axis=0)
        two = jnp.concatenate([v[LC:], got], axis=0)
        three = jnp.concatenate([v[LC:cut], got, v[cut:]], axis=0)
        return jnp.where(col < 2, low, jnp.where(col == 2, two, three))

    def gather_quad(v):
        swapped = swap(v)
        paired = pair(v)
        mid = v.shape[0] // 2
        diagonal = jnp.concatenate([pair(swapped[:mid]), swap(paired[mid:])], axis=0)
        first_own, second_own = by_pair(v, paired)
        first_oth, second_oth = by_pair(swapped, diagonal)
        return jnp.stack([jnp.concatenate([first_own, second_own], axis=0), jnp.concatenate([first_oth, second_oth], axis=0)])

    def scatter_quad(own, oth):
        v = own + swap(oth.astype(bf16)).astype(f32)
        first, second = v[:local], v[local:]
        kept, sent = jnp.where(low_pair, first, second), jnp.where(low_pair, second, first)
        return kept + pair(sent.astype(bf16)).astype(f32)

    own_table = jnp.where(half == 0, table[0], table[1])
    oth_table = jnp.where(half == 0, table[1], table[0])
    resumes_own = own_table == half
    resumed_by_other = oth_table == half

    small = jnp.concatenate([conv_weight, conv_bias[None], dt_bias[None], d_skip[None], a_log, dt_proj, x_proj.T], axis=0)
    lanes = small.shape[1]
    used = small.shape[0]
    gain_rows = gain.size // lanes
    width = tokens.shape[1]
    if quick:
        small = jnp.concatenate([small, gain.reshape(gain_rows, lanes)], axis=0)
        small = jnp.pad(small, ((0, -small.shape[0] % 16), (0, 0)))
        raw, wi, small = run_gather_start(tokens, in_proj[:, 0], small)
        gain_all = small[:, used : used + gain_rows].reshape(2, width).astype(f32)
        small = jnp.swapaxes(small, 0, 1).reshape(small.shape[1], 8 * lanes)
    else:
        raw = gather_quad(to_sequences(tokens))

        def weight(shard):
            v = lax.all_gather(jnp.stack([send(shard, same), send(shard, other)]), "grp", axis=2, tiled=True)
            v = v.reshape(2, v.shape[1], SLOTS, v.shape[2] // SLOTS)
            return jnp.transpose(v, (2, 0, 1, 3)).reshape(2 * SLOTS, v.shape[1], v.shape[3])

        wi = weight(in_proj[:, 0])
        small = send(lax.all_gather(small, ("row", "grp"), axis=1, tiled=True), spread)
        gain_all = lax.all_gather(gain, ("row", "grp"), axis=0, tiled=True).astype(f32).reshape(2, width)
    w = small.shape[1]
    zero_row = jnp.zeros((1, w), f32)
    conv = jnp.concatenate([small[0:5].astype(f32)] + [zero_row] * 3, axis=0)
    vec = jnp.concatenate([small[5:7].astype(f32)] + [zero_row] * 6, axis=0)
    rate = -jnp.exp(small[7 : 7 + NSTATE].astype(f32))
    dtp = small[7 + NSTATE : 7 + NSTATE + RANK]
    xproj = small[7 + NSTATE + RANK : 7 + NSTATE + RANK + XW]
    gain_own = jnp.where(low_row, gain_all[0], gain_all[1])
    gain_two = jnp.stack([gain_own, jnp.where(low_row, gain_all[1], gain_all[0])])

    normed, inv, inner = run_project_first(raw, gain_two, wi)
    zero_state = jnp.zeros((NSTATE, w), f32)
    if quick:
        mix = jnp.broadcast_to(resumes_own.astype(f32), (8, w))
        xconv, yfull, starts, xdbl, tail, wg, wo, cot = run_forward(inner, inv, mix, conv, xproj, dtp, vec, rate, in_proj[:, 1], out_proj, cotangent)
    else:
        tail_own = (inv * inner)[LP - 8 : LP]
        tail = jnp.where(resumes_own, tail_own, across(tail_own))
        xconv, xdbl = run_conv_forward(inner, inv, tail, conv, xproj)
        for move in (swap, pair):
            xdbl = xdbl + move(xdbl)
        xdbl = jnp.swapaxes(xdbl.reshape(XW, NCH, CH), 0, 1)
        *kept, final = run_scan_forward(0, PC, xdbl, xconv, dtp, vec, rate, zero_state)
        resumed = jnp.where(resumes_own, final, across(final))
        yfull, starts, _ = run_scan_forward(PC, NCH - PC, xdbl, xconv, dtp, vec, rate, resumed, kept)
        wg, wo = weight(in_proj[:, 1]), weight(out_proj)
        cot = gather_quad(to_sequences(cotangent))
    gated, d_yfull, d_gate_proj, gate_scale, branch_own, branch_oth = run_gate_backward(normed, wg, cot, wo, yfull, inv)

    def collect(v):
        return send(v[0].astype(bf16), back(same)).astype(f32) + send(v[1].astype(bf16), back(other)).astype(f32)

    def rows_product(a, b, out_dtype):
        return lax.dot_general(a, b, (((1,), (0,)), ((), ())), preferred_element_type=f32).astype(out_dtype)

    zero_head = jnp.zeros((8, w), f32)
    conv_back = functools.partial(run_conv_backward, inner=inner, inv=inv, tail=tail, conv=conv, xproj=xproj)
    if quick:
        x, core = grp // 2, grp % 2
        order = jnp.stack([2 * (1 - x) + 1 - core, 2 * x + 1 - core, 2 * (1 - x) + core, 2 * x + core]).astype(jnp.int32)
        gate_sent, out_sent, gate_kept, out_kept = run_late_parts(order, normed, d_gate_proj, gated, cot)
        sent, kept = (gate_sent, out_sent), (gate_kept, out_kept)
        into = jnp.broadcast_to(resumed_by_other.astype(f32), (8, w))
        dxdbl, dxc, alog_grad, scan_sums, dtp_grad, late_grads, branch = run_backward(
            xdbl, xconv, d_yfull, dtp, vec, rate, starts, mix, into, sent, kept, branch_own, branch_oth
        )
        gate_grad, out_grad = late_grads[0], late_grads[1]
    else:
        branch = from_sequences(scatter_quad(branch_own, branch_oth).astype(bf16))
        out_grad = collect([scatter_grp(dot_tn(gated, cot[d]), 1) for d in range(2)])
        gate_grad = collect([scatter_grp(dot_tn(normed[d], d_gate_proj), 1) for d in range(2)])
        sums = (zero_state, jnp.zeros((8, w), f32), jnp.zeros((RANK, w), f32))
        scan = functools.partial(run_scan_backward, xdbl=xdbl, xconv=xconv, dy=d_yfull, dtp=dtp, vec=vec, rate=rate, starts=starts)
        dx_c, dxc, *sums, g_first = scan(PC, NCH - PC, carry=zero_state, sums=sums)
        g_into = jnp.where(resumes_own, g_first, 0.0) + jnp.where(resumed_by_other, across(g_first), 0.0)
        dx_p, dxc, *sums, _ = scan(0, PC, carry=g_into, sums=sums, kept=(dxc,))
        alog_grad, scan_sums, dtp_grad = sums
        dxdbl = jnp.concatenate([dx_p, dx_c], axis=1)
        for move in (swap, pair):
            dxdbl = dxdbl + move(dxdbl)
        dxdbl = jnp.swapaxes(dxdbl.reshape(XW, NCH, CH), 0, 1)

    output = (tokens.astype(f32) + branch.astype(f32)).astype(bf16)
    sums = (jnp.zeros((8, w), f32), jnp.zeros((XW, w), f32))
    dp, ds, *sums, head = conv_back(PC, NCH - PC, dxc=dxc, dxdbl=dxdbl, follow=zero_head, sums=sums)
    follow = jnp.where(resumes_own, head, 0.0) + jnp.where(resumed_by_other, across(head), 0.0)
    d_inner_proj, inner_scale, conv_sums, xproj_grad, _ = conv_back(0, PC, dxc=dxc, dxdbl=dxdbl, follow=follow, sums=sums, kept=(dp, ds))

    scale = gate_scale + inner_scale
    scale = scale + swap(scale)
    first, second = scale[:local], scale[local:]
    scale_own = jnp.where(low_pair, first, second) + pair(jnp.where(low_pair, second, first))
    inv_own = jnp.where(low_pair, inv[:local], inv[local:])
    pull = from_sequences(scale_own * inv_own * inv_own * inv_own / D)
    if quick:
        d_normed, inner_grad, gain_sum = run_finish(d_inner_proj, d_gate_proj, normed, raw, wi, wg)
        gain_grad = jnp.sum(gain_sum, axis=0)
    else:
        inner_grad = collect([scatter_grp(dot_tn(normed[d], d_inner_proj), 1) for d in range(2)])
        d_normed = from_sequences(scatter_quad(*run_normed_backward(d_inner_proj, d_gate_proj, wi, wg)))
        gain_grad = jnp.sum(d_normed * tokens.astype(f32), axis=0)
        gain_grad = lax.psum_scatter(lax.psum(gain_grad, "col"), "grp", scatter_dimension=0, tiled=True)
    input_grad = (cotangent.astype(f32) + d_normed * gain_own - pull * tokens.astype(f32)).astype(bf16)
    in_grads = jnp.stack([inner_grad, gate_grad], axis=1)
    small_grad = jnp.concatenate([conv_sums[0:5], scan_sums[0:2], alog_grad * rate, dtp_grad, xproj_grad], axis=0)
    small_grad = jnp.pad(small_grad, ((0, -small_grad.shape[0] % 8), (0, 0)))
    small_grad = send(small_grad, back(spread))
    small_grad = lax.psum_scatter(small_grad, ("row", "grp"), scatter_dimension=1, tiled=True)
    return (
        output,
        input_grad,
        gain_grad,
        in_grads,
        small_grad[0:4],
        small_grad[4],
        small_grad[7 + NSTATE + RANK : 7 + NSTATE + RANK + XW].T,
        small_grad[7 + NSTATE : 7 + NSTATE + RANK],
        small_grad[5],
        small_grad[7 : 7 + NSTATE],
        small_grad[6],
        out_grad,
    )


def solution(mesh):
    placed = (
        P(("grp", "col"), "row"),
        P(("row", "grp")),
        P("row", None, ("col", "grp")),
        P(None, ("col", "row", "grp")),
        P(("col", "row", "grp")),
        P(("col", "row", "grp"), None),
        P(None, ("col", "row", "grp")),
        P(("col", "row", "grp")),
        P(None, ("col", "row", "grp")),
        P(("col", "row", "grp")),
        P("col", ("row", "grp")),
        P("grp"),
        P(("grp", "col"), "row"),
    )
    return jax.shard_map(
        per_device,
        mesh=mesh,
        in_specs=placed,
        out_specs=(
            P(("grp", "col"), "row"),
            P(("grp", "col"), "row"),
            P(("row", "grp")),
            P("row", None, ("col", "grp")),
            P(None, ("col", "row", "grp")),
            P(("col", "row", "grp")),
            P(("col", "row", "grp"), None),
            P(None, ("col", "row", "grp")),
            P(("col", "row", "grp")),
            P(None, ("col", "row", "grp")),
            P(("col", "row", "grp")),
            P("col", ("row", "grp")),
        ),
        check_vma=False,
    )
```

time: 760 us -> 680 us (0.89); the launches traced: 750 us -> 678 us
  Pallas kernels: 404 us -> 571 us
  waiting for transfers between devices: 124 us -> 32 us
  starting transfers between devices: 61.2 us -> 10.9 us
  other arithmetic: 57.6 us -> 13.1 us
  matrix products: 32.7 us -> 0 us
  blocking collectives: 12.7 us -> 0 us
    pallas_call x1 -> x5, Pallas kernels: 142 us -> 517 us  [the longest x1 169 us: run_forward(): pl.pallas_call(forward, grid=(2 * NCH,), in_specs=[rows_of(w, first), row...]
    pallas_call x14 -> x4, Pallas kernels: 262 us -> 53.8 us  [call(): pl.pallas_call(body, grid=(chunks,), in_specs=in_specs, out_specs=out_spe...]
    ppermute x32 -> x5, waiting for transfers between devices: 108 us -> 31.9 us  [send(): lax.ppermute(v, ('row', 'col'), [(spot(*a), spot(*b)) for a, b in pairs])]
    ppermute x32 -> x5, starting transfers between devices: 56.6 us -> 10.9 us  [send(): lax.ppermute(v, ('row', 'col'), [(spot(*a), spot(*b)) for a, b in pairs])]
    dot_general x8 -> x0, matrix products: 32.7 us -> none  [the longest x4 20.4 us: rows_product(): lax.dot_general(a, b, (((1,), (0,)), ((), ())), preferred_element_type=f32)]
    ppermute x8 -> x0, waiting for transfers between devices: 16 us -> none  [flip(): return lax.ppermute(v, 'grp', [(g, g ^ bit) for g in range(4)])]
    select_n x10 -> x1, other arithmetic: 12.1 us -> 0.08 us  [from_sequences(): return jnp.where(col < 2, low, jnp.where(col == 2, two, three))]
    add x10 -> x0, other arithmetic: 10.7 us -> none  [the longest x2 5.1 us: scatter_quad(): v = own + swap(oth.astype(bf16)).astype(f32)]
  transfers between devices with their start and end apart: 41 -> 6, of which waited for: 17 -> 4; matrix products, arithmetic and copies ran while one was open for 16% -> 2% of each run, Pallas kernels for 54% -> 15%
where the time goes in v2:
time: 680 us; the launch traced here: 678 us
  Pallas kernels  571 us (84%)
  local copies, waits for them, and re-layouts  34 us (5%)
  waiting for transfers between devices  32 us (5%)
  between operations  17 us (2%)
  other arithmetic  13.1 us (2%)
  starting transfers between devices  10.9 us (2%)
    pallas_call x1, Pallas kernels, run_forward(): pl.pallas_call(forward, grid=(2 * NCH,), in_specs=[rows_of(w, first), row...  169 us
    pallas_call x1, Pallas kernels, run_backward(): pl.pallas_call(backward_kernel, grid=(NCH,), in_specs=[chunk_of(XW, at),...  149 us
    pallas_call x1, Pallas kernels, run_finish(): pl.pallas_call(finish, in_specs=[ANY] * 6, out_specs=[ANY, vmem, vmem], o...  102 us
    pallas_call x1, Pallas kernels, run_gather_start(): pl.pallas_call(gather_start, in_specs=[ANY] * 3, out_specs=[ANY] * 3, out...  75.4 us
    pallas_call x4, Pallas kernels, call(): pl.pallas_call(body, grid=(chunks,), in_specs=in_specs, out_specs=out_spe...  53.8 us
    ppermute x5, waiting for transfers between devices, send(): lax.ppermute(v, ('row', 'col'), [(spot(*a), spot(*b)) for a, b in pairs])  31.9 us
    pallas_call x1, Pallas kernels, run_late_parts(): pl.pallas_call(late_parts, grid_spec=pltpu.PrefetchScalarGridSpec(num_sca...  21.2 us
  transfers between devices with their start and end apart: 6, of which 4 were waited for; matrix products, arithmetic and copies ran while one was open for 2% of the time, Pallas kernels for 15%

profile of v2, /device:TPU:14, one launch (start us, length us, event | category | flops | bytes accessed | tf_op | source)
XLA Modules:
  0.0 678.0 jit_solution(1705050243847081832)
XLA Ops:
  7.2 3.4 fusion.5
  10.8 1.2 copy_bitcast_fusion
  12.0 0.7 concatenate.54
  12.7 0.6 pad.12.small
  13.4 75.4 %shard_map.220 = (bf16[2,1152,1024]{2,1,0:T(8,128)(2,1)}, bf16[8,1024,256]{2,1,0:T(8,128)(2,1)}, bf16[8,320,128]{2,1,0:T(8,128)(2,1)}) custom-call(bf16[576,1024]{1,0:T(8,128)(2,1)} %tokens.1, bf16[1024,256]{1,0:T(8,128)(2,1)} %get-tuple-element.153.in_i, bf16[320,128]{1,0:T(8,128)(2,1)} %pad.12.small), custom_call_target="tpu_custom_call" | custom-call | tf_op jit(solution)/shard_map/pallas_call | solution.py:584
  88.7 0.8 slice_convert_fusion
  89.5 0.7 slice_bitcast_fusion.5
  90.2 1.8 copy_bitcast_fusion.2.xproj_ref
  92.0 1.7 copy_bitcast_fusion.3.dtp_ref.refs_3_
  93.8 0.7 slice_bitcast_fusion.6
  94.5 1.4 copy_bitcast_fusion.4.rate_ref.refs_5_
  99.1 0.6 pad_convert_fusion.1.conv_ref
  99.8 0.6 pad_convert_fusion.vec_ref.refs_4_
  101.6 10.8 %shard_map.221 = (bf16[2,1152,1024]{2,1,0:T(8,128)(2,1)}, f32[1152,1]{1,0:T(8,128)}, f32[1152,1024]{1,0:T(8,128)}) custom-call(bf16[2,1152,1024]{2,1,0:T(8,128)(2,1)} %get-tuple-element.55.raw_ref.raw_hbm, f32[2,1024]{1,0:T(2,128)} %pad_maximum_fusion.1.gain_ref, bf16[8,1024,256]{2,1,0:T(8,128)(2,1)} %get-tuple-element.57.w_ref.wi_hbm), custom_call_target="tpu_custom_call" | custom-call | flops 8999999488 | bytes 1000000 | tf_op jit(solution)/shard_map/pallas_call | solution.py:278
  113.6 169.1 %shard_map.222 = (bf16[1152,1024]{1,0:T(8,128)(2,1)}, bf16[1152,1024]{1,0:T(8,128)(2,1)}, f32[9,16,1024]{2,1,0:T(8,128)}, f32[9,160,128]{2,1,0:T(8,128)}, f32[8,...) custom-call(f32[1152,1024]{1,0:T(8,128)} %get-tuple-element.58.inner, ...), custom_call_target="tpu_custom_call" | custom-call | flops 60000002048 | bytes 1000000 | tf_op jit(solution)/shard_map/pallas_call | solution.py:723
  282.7 22.4 %shard_map.223 = (bf16[1152,1024]{1,0:T(8,128)(2,1)}, f32[1152,1024]{1,0:T(8,128)}, bf16[1152,1024]{1,0:T(8,128)(2,1)}, f32[1152,1]{1,0:T(8,128)}, f32[1152,1024]{1,0:T(8,128)}, /*index=5*/bf16[1152,1024]{1,0:T(8,128)(2,1)}) custom-call(bf16[2,1152,1024]{2,1,0:T(8,128)(2,1)} %get-tuple-element.62.normed_ref.normed_hbm, ...), custom_call_target="tpu_custom_call" | custom-call | flops 22000001024 | bytes 1000000 | tf_op jit(solution)/shard_map/pallas_call | solution.py:278
  305.1 21.2 %shard_map.224 = (bf16[2,2,1024,256]{3,2,1,0:T(8,128)(2,1)}, bf16[2,2,1024,256]{3,2,1,0:T(8,128)(2,1)}, f32[2,2,1024,256]{3,2,1,0:T(8,128)}, f32[2,2,1024,256]{3,2,1,0:T(8,128)}) custom-call(s32[4]{0:T(128)} %pad_add_fusion.order_ref, bf16[2,1152,1024]{2,1,0:T(8,128)(2,1)} %get-tuple-element.62.normed_ref.normed_hbm, ...), custom_call_target="tpu_custom_call" | custom-call | flops 14000000000 | bytes 1000000 | tf_op jit(solution)/shard_map/pallas_call | solution.py:1211
  327.0 149.4 %shard_map.225 = (f32[9,160,128]{2,1,0:T(8,128)}, f32[1152,1024]{1,0:T(8,128)}, f32[16,1024]{1,0:T(8,128)}, f32[8,1024]{1,0:T(8,128)}, f32[128,1024]{1,0:T(8,128...) custom-call(f32[9,160,128]{2,1,0:T(8,128)} %get-tuple-element.60.refs_0_, ...), custom_call_target="tpu_custom_call" | custom-call | flops 120000004096 | bytes 1000000 | tf_op jit(solution)/shard_map/pallas_call | solution.py:1472
  476.4 0.6 broadcast_1_follow_ref_sums0_ref.2.follow_ref.sums0_ref
  477.0 0.9 broadcast_in_dim.27.xprojg0_ref
  477.9 4.1 shard_map.226
  482.0 1.7 collective-permute-start
  483.7 0.8 fusion.4
  484.6 0.8 slice.138
  485.3 2.6 collective-permute-done
  487.9 1.4 select_add_fusion.follow_ref
  489.3 16.5 %shard_map.227 = (bf16[1152,1024]{1,0:T(8,128)(2,1)}, f32[1152,1]{1,0:T(8,128)}, f32[8,1024]{1,0:T(8,128)}, f32[160,1024]{1,0:T(8,128)}, f32[8,1024]{1,0:T(8,128)}) custom-call(f32[1152,1024]{1,0:T(8,128)} %get-tuple-element.58.inner_ref.tail_ref.halo_ref, ...), custom_call_target="tpu_custom_call", output_to_operand_aliasing={{0}: (12, {}), {1}: (13, {})} | custom-call | flops 16000000000 | bytes 1000000 | tf_op jit(solution)/shard_map/pallas_call | solution.py:278
  505.8 5.1 concatenate.68
  510.9 1.1 pad.13
  512.0 3.0 collective-permute-start.4
  515.1 1.5 slice_bitcast_fusion
  516.8 2.5 collective-permute-start.1
  519.3 22.8 %collective-permute-done.4 = f32[312,1024]{1,0:T(8,128)} collective-permute-done((f32[312,1024]{1,0:T(8,128)}, f32[312,1024]{1,0:T(8,128)}, u32[]{:S(2)}, u32[]{:S(2)}) %collective-permute-start.4) | collective-permute-done | bytes 1277984 | tf_op jit(solution)/shard_map/ppermute | solution.py:1576
  542.1 102.1 %shard_map.228 = (f32[576,1024]{1,0:T(8,128)}, f32[1024,256]{1,0:T(8,128)}, f32[8,256]{1,0:T(8,128)}) custom-call(bf16[1152,1024]{1,0:T(8,128)(2,1)} %get-tuple-element.86.inner_hbm, bf16[1152,1024]{1,0:T(8,128)(2,1)} %get-tuple-element.69.gate_ref.gate_hbm, bf16[2,1152,1024]{2,1,0:T(8,128)(2,1)} %get-tuple-element.62.normed_ref.normed_hbm, ...), custom_call_target="tpu_custom_call" | custom-call | flops 60000002048 | bytes 1000000 | tf_op jit(solution)/shard_map/pallas_call | solution.py:1141
  644.5 0.8 slice_select_fusion
  645.3 1.4 collective-permute-start.2
  646.6 1.4 pad_maximum_fusion
  648.6 2.9 copy.46
  651.6 3.1 collective-permute-done.2
  654.6 1.0 fusion.3
  655.7 2.3 collective-permute-start.3
  658.3 3.5 collective-permute-done.3
  662.1 2.1 fusion.2
  664.2 1.3 slice.161
  665.5 1.3 slice_bitcast_fusion.7
  666.8 1.5 slice_bitcast_fusion.4
  668.3 1.5 slice.164
  669.8 1.3 slice.166
  (64 shorter events, 5.5 us)
Async XLA Ops:
  7.2 657.0 %reduce-scatter.2.cloned.1.call-start = ((), (), s32[]{:S(2)}) async-start(), calls=%async_computation.1 | async-start | bytes 1437696 | tf_op jit(solution)/shard_map/reduce_scatter | solution.py:1753
  10.7 1.3 copy-start.10
  10.7 1.3 copy-start.13
  10.7 1.3 copy-start.15
  10.7 1.3 copy-start.17
  10.7 1.2 copy-start.18
  10.7 1.2 copy-start.19
  10.7 1.2 copy-start.20
  10.8 1.2 copy-start.21
  11.9 84.0 %copy-start.16 = (s32[2]{0:T(128)S(1)}, s32[2]{0:T(128)}, u32[]{:S(2)}) copy-start(s32[2]{0:T(128)} %param.24) | copy-start | bytes 28
  100.4 0.6 copy-start.11
  477.9 5.8 copy-start.9
  482.0 5.9 collective-permute-start
  505.8 9.2 %copy-start.3 = (f32[2,1024,256]{2,1,0:T(8,128)S(1)}, f32[2,1024,256]{2,1,0:T(8,128)}, u32[]{:S(2)}) copy-start(f32[2,1024,256]{2,1,0:T(8,128)} %get-tuple-element.92) | copy-start | bytes 6291460
  512.0 4.5 copy-start.7
  512.0 4.5 copy-start.8
  512.0 30.0 %collective-permute-start.4 = (f32[312,1024]{1,0:T(8,128)}, f32[312,1024]{1,0:T(8,128)}, u32[]{:S(2)}, u32[]{:S(2)}) collective-permute-start(f32[312,1024]{1,0:T(8,128)} %pad.13), channel_id=1, source_target_pairs={{0,0},{4,1},{1,2},{5,3},{6,4},{2,5},{7,6},{3,7},{8,8},{12,9},{9,10... | collective-permute-start | bytes 3833864 | tf_op jit(solution)/shard_map/ppermute | solution.py:1576
  516.8 127.4 %collective-permute-start.1 = (f32[1152,1]{0,1:T(1,128)S(1)}, f32[1152,1]{0,1:T(1,128)S(1)}, u32[]{:S(2)}, u32[]{:S(2)}) collective-permute-start(f32[1152,1]{0,1:T(1,128)S(1)} %copy.44), channel_id=1, source_target_pairs={{0,4},{1,5},{2,6},{3,7},{4,0},{5,1},{6,2},{7,3},{8,12},{9,13},{10,... | collective-permute-start | bytes 13832 | tf_op jit(solution)/shard_map/ppermute | solution.py:1576
  644.4 2.2 copy-start.6
  644.5 3.5 copy-start.14
  645.3 9.3 %collective-permute-start.2 = (f32[576,1]{1,0:T(8,128)}, f32[576,1]{1,0:T(8,128)}, u32[]{:S(2)}, u32[]{:S(2)}) collective-permute-start(f32[576,1]{1,0:T(8,128)} %slice_select_fusion), channel_id=1, source_target_pairs={{0,1},{1,0},{2,3},{3,2},{4,5},{5,4},{6,7},{7,6},{8,9},{9,8},{10,11... | collective-permute-start | bytes 6920 | tf_op jit(solution)/shard_map/ppermute | solution.py:1576
  648.0 6.6 copy-start
  648.6 13.5 %copy-start.2 = (f32[576,1024]{1,0:T(8,128)S(1)}, f32[576,1024]{1,0:T(8,128)}, u32[]{:S(2)}) copy-start(f32[576,1024]{1,0:T(8,128)} %get-tuple-element.87) | copy-start | bytes 7077892
  648.6 13.5 %copy-start.5 = (bf16[576,1024]{1,0:T(8,128)(2,1)S(1)}, bf16[576,1024]{1,0:T(8,128)(2,1)}, u32[]{:S(2)}) copy-start(bf16[576,1024]{1,0:T(8,128)(2,1)} %get-tuple-element.77) | copy-start | bytes 3538948
  651.6 10.5 %copy-start.1 = (bf16[576,1024]{1,0:T(8,128)(2,1)S(1)}, bf16[576,1024]{1,0:T(8,128)(2,1)}, u32[]{:S(2)}) copy-start(bf16[576,1024]{1,0:T(8,128)(2,1)} %tokens.1) | copy-start | bytes 3538948
  651.6 10.5 %copy-start.4 = (bf16[576,1024]{1,0:T(8,128)(2,1)S(1)}, bf16[576,1024]{1,0:T(8,128)(2,1)}, u32[]{:S(2)}) copy-start(bf16[576,1024]{1,0:T(8,128)(2,1)} %cot_in.1) | copy-start | bytes 3538948
  651.6 10.5 %copy-start.12 = (f32[4,2,128]{2,1,0:T(2,128)S(1)}, f32[4,2,128]{2,1,0:T(2,128)}, u32[]{:S(2)}) copy-start(f32[4,2,128]{2,1,0:T(2,128)} %copy-done.11) | copy-start | bytes 12292
  655.7 6.2 collective-permute-start.3
Sparse Core Ops, SparseCore 0:
  542.2 42.4 reduce-scatter.1

commit v3 on v2

--- a/solution.py
+++ b/solution.py
@@ -439,6 +439,7 @@
         self.alone = 2 * half + c // 2 == c
         self.ranks = (g, (1 - x) * 2 + core, x * 2 + 1 - core)
         self.x_dev, self.core_dev = (self.ranks[1], r, c), (self.ranks[2], r, c)
+        self.y_dev, self.z_dev = (g, 1 - r, c), (g, r, c + 1 - 2 * (c % 2))
         self.weights, self.tokens, self.raw = weights, tokens, raw
         self.w_send, self.w_recv, self.t_send, self.t_recv, self.here = w_send, w_recv, t_send, t_recv, here
 
@@ -520,48 +521,109 @@
 
         self.first_hop(n, 1).wait_send()
 
-    def token_copies(self, k):
-        copies, mine = [], []
-        for a, b, s, at in token_pieces(k, self.tokens.shape[0]):
-            for dr in range(2):
-                for dc in range(2):
-                    target = 2 * s + dc
-                    dst = self.raw.at[dr, pl.ds(at, b - a)]
-                    src = self.tokens.at[pl.ds(a, b - a)]
-                    if dr == 0 and target == k:
-                        mine.append(pltpu.make_async_copy(src, dst, self.here.at[2 + len(mine)]))
-                    else:
-                        device = (self.g, self.r if dr == 0 else 1 - self.r, target)
-                        copies.append(remote(src, dst, self.t_send.at[len(copies)], self.t_recv.at[dr], device))
-        return copies, mine
-
-    def begin_tokens(self):
+    def ranges(self, k):
+        local = self.tokens.shape[0]
+        held = {0: (0, local), 1: (local, LP), 2: (LC, LC + local), 3: (LC + local, SEQ)}
+        return held[k], held[k ^ 1], (LP, SEQ) if k < 2 else (0, LC)
+
+    def part(self, d, rows):
+        return self.raw.at[d, pl.ds(rows[0], rows[1] - rows[0])]
+
+    def on_col(self, act):
         for k in range(4):
 
             @pl.when(self.c == k)
             def _(k=k):
-                copies, mine = self.token_copies(k)
-                for copy in mine + copies:
-                    copy.start()
+                act(k)
+
+    def sources(self, k, lo, hi):
+        for a, b, s, at in token_pieces(k, self.tokens.shape[0]):
+            first, end = max(lo, at), min(hi, at + b - a)
+            if s == k // 2 and first < end:
+                yield a + first - at, first, end
+
+    def begin_half(self, h):
+        def act(k):
+            lo, hi = split(self.ranges(k)[0])[h]
+            for src, first, end in self.sources(k, lo, hi):
+                rows = self.tokens.at[pl.ds(src, end - first)]
+                pltpu.make_async_copy(rows, self.part(0, (first, end)), self.here.at[2 + h]).start()
+                remote(rows, self.part(1, (first, end)), self.t_send.at[h], self.t_recv.at[h], self.y_dev).start()
+                remote(rows, self.part(0, (first, end)), self.t_send.at[2 + h], self.t_recv.at[2 + h], self.z_dev).start()
+
+        self.on_col(act)
+
+    def foreign_copies(self, k):
+        copies = []
+        for a, b, s, at in token_pieces(k, self.tokens.shape[0]):
+            if s != k // 2:
+                for dr in range(2):
+                    for dc in range(2):
+                        device = (self.g, self.r if dr == 0 else 1 - self.r, 2 * s + dc)
+                        sems = self.t_send.at[6 + 2 * dr + dc], self.t_recv.at[6 + dr]
+                        copies.append(remote(self.tokens.at[pl.ds(a, b - a)], self.part(dr, (at, at + b - a)), *sems, device))
+        return copies
+
+    def begin_foreign(self):
+        def act(k):
+            for copy in self.foreign_copies(k):
+                copy.start()
+
+        self.on_col(act)
+
+    def relays(self, k):
+        own, paired, _ = self.ranges(k)
+        early, late = split(paired)[0], split(own)[1]
+        return (
+            remote(self.part(0, early), self.part(1, early), self.t_send.at[4], self.t_recv.at[4], self.y_dev),
+            remote(self.part(1, late), self.part(1, late), self.t_send.at[5], self.t_recv.at[5], self.z_dev),
+        )
+
+    def settle(self, d, rows, sem):
+        pltpu.make_async_copy(self.part(d, rows), self.part(d, rows), sem).wait()
+
+    def relay(self):
+        def act(k):
+            own, paired, _ = self.ranges(k)
+            by_y, by_z = self.relays(k)
+            self.settle(0, split(paired)[0], self.t_recv.at[2])
+            by_y.start()
+            self.settle(1, split(own)[1], self.t_recv.at[1])
+            by_z.start()
+
+        self.on_col(act)
 
     def end_tokens(self):
-        for k in range(4):
-
-            @pl.when(self.c == k)
-            def _(k=k):
-                copies, mine = self.token_copies(k)
-                held = sum(b - a for a, b, s, at in token_pieces(k, self.tokens.shape[0]) if s == k // 2)
-                rest = self.raw.at[0, pl.ds(0, SEQ - held)]
-                pltpu.make_async_copy(rest, rest, self.t_recv.at[0]).wait()
-                pltpu.make_async_copy(self.raw.at[1], self.raw.at[1], self.t_recv.at[1]).wait()
-                for copy in mine:
-                    copy.wait()
-                for copy in copies:
-                    copy.wait_send()
+        def act(k):
+            own, paired, foreign = self.ranges(k)
+            own, paired = split(own), split(paired)
+            by_y, by_z = self.relays(k)
+            self.settle(1, own[0], self.t_recv.at[0])
+            self.settle(0, paired[1], self.t_recv.at[3])
+            self.settle(1, paired[0], self.t_recv.at[4])
+            self.settle(1, paired[1], self.t_recv.at[5])
+            self.settle(0, foreign, self.t_recv.at[6])
+            self.settle(1, foreign, self.t_recv.at[7])
+            for h in range(2):
+                self.settle(0, own[h], self.here.at[2 + h])
+                self.settle(0, own[h], self.t_send.at[h])
+                self.settle(0, own[h], self.t_send.at[2 + h])
+            by_y.wait_send()
+            by_z.wait_send()
+            for copy in self.foreign_copies(k):
+                copy.wait_send()
+
+        self.on_col(act)
+
+
+def split(rows):
+    lo, hi = rows
+    mid = lo + (hi - lo) // 2
+    return (lo, mid), (mid, hi)
 
 
 def gather_semaphores():
-    return [pltpu.SemaphoreType.DMA(shape) for shape in ((2, 8), (2, 8), (12,), (2,), (4,))]
+    return [pltpu.SemaphoreType.DMA(shape) for shape in ((2, 8), (2, 8), (10,), (8,), (4,))]
 
 
 def gather_start(tokens, in_i, small, raw, wi, small_all, *sems):
@@ -569,9 +631,12 @@
     gather.greet()
     gather.begin(0)
     gather.begin(1)
-    gather.begin_tokens()
+    gather.begin_half(0)
+    gather.begin_half(1)
+    gather.begin_foreign()
     for n in range(2):
         gather.forward(n)
+    gather.relay()
     for n in range(2):
         gather.forward_again(n)
     gather.end_tokens()
@@ -595,23 +660,43 @@
     )(tokens, in_i, small)
 
 
-LAG = 2
-
-
-def forward(inner_ref, inv_ref, tail_ref, inv_tail_ref, mix_ref, conv_ref, xproj_ref, dtp_ref, vec_ref, rate_ref, in_g, out_w, cot_in,
-            xconv_ref, yfull_ref, starts_ref, xdbl_ref, joined_ref, wg, wo, cot,
-            buf, xc_s, part, yr, zs, zr, tail_s, tail_r, state, last, last_r,
+LAG = 4
+FIRST = BIG_STEPS
+SECOND = FIRST + NCH
+LAST = SECOND + NCH - 1
+BEGIN = (0, SECOND)
+FORWARD = (FIRST + 8, SECOND + 5)
+FORWARD_AGAIN = (SECOND + 3, LAST)
+HALVES = (FIRST + 6, SECOND + 1)
+FOREIGN = SECOND + 2
+RELAY = SECOND + 6
+
+
+def pack_sum(ref, k, v):
+    high = v[RANK:].astype(bf16)
+    ref[k, :RANK] = v[:RANK].astype(bf16)
+    ref[k, RANK:XW] = high
+    ref[k, XW:] = (v[RANK:] - high.astype(f32)).astype(bf16)
+
+
+def unpack_sum(ref, k):
+    return jnp.concatenate([ref[k, :RANK].astype(f32), ref[k, RANK:XW].astype(f32) + ref[k, XW:].astype(f32)], axis=0)
+
+
+def forward(raw_ref, gain_ref, wi_ref, mix_ref, conv_ref, xproj_ref, dtp_ref, vec_ref, rate_ref, in_g, out_w, cot_in,
+            normed_ref, inv_ref, inner_ref, xconv_ref, yfull_ref, starts_ref, xdbl_ref, joined_ref, wg, wo, cot,
+            inner_s, inv_s, buf, xc_s, part, ys, yr, zs, zr, tail_s, tail_r, state, last, last_r,
             dt_s, u_s, cb_s, h_s, y_s, y_send, y_recv, z_send, z_recv, e_send, e_recv, *sems):
     i = pl.program_id(0)
     gather = Gather([(in_g, wg, False), (out_w, wo, False)], cot_in, cot, *sems)
     g, r, c = gather.g, gather.r, gather.c
-    y_dev, z_dev = (g, 1 - r, c), (g, r, c + 1 - 2 * (c % 2))
+    y_dev, z_dev = gather.y_dev, gather.z_dev
     far_dev = (g, 1 - r, (c + 2) % 4)
     to_tail = remote(tail_s, tail_r, e_send.at[0], e_recv.at[0], far_dev)
     to_last = remote(last, last_r, e_send.at[1], e_recv.at[1], far_dev)
 
     def to_y(k):
-        return remote(part.at[k], yr.at[k], y_send.at[k], y_recv.at[k], y_dev)
+        return remote(ys.at[k], yr.at[k], y_send.at[k], y_recv.at[k], y_dev)
 
     def to_z(k):
         return remote(zs.at[k], zr.at[k], z_send.at[k], z_recv.at[k], z_dev)
@@ -619,88 +704,111 @@
     @pl.when(i == 0)
     def _():
         gather.greet()
-        tail_s[...] = inv_tail_ref[...] * tail_ref[...]
+
+    @pl.when(i < FIRST)
+    def _():
+        rows = pl.ds(pl.multiple_of(i * BIG, BIG), BIG)
+        project_first(raw_ref, gain_ref, wi_ref, normed_ref, inv_ref, inner_ref)
+        inner_s[rows, :] = inner_ref[...]
+        inv_s[rows, :] = inv_ref[...]
+
+    @pl.when(i == FIRST)
+    def _():
+        tail_s[...] = inv_s[LP - 8 : LP] * inner_s[LP - 8 : LP]
         to_tail.start()
-        gather.begin(0)
-        gather.begin(1)
         buf[0:8] = jnp.zeros_like(buf[0:8])
         state[...] = jnp.zeros_like(state)
 
     mix = mix_ref[...]
 
-    @pl.when(i == PC)
+    @pl.when(i == FIRST + PC)
     def _():
         to_tail.wait()
         joined = mix * tail_s[...] + (1.0 - mix) * tail_r[...]
         buf[0:8] = joined
         joined_ref[...] = joined
 
-    @pl.when((i > 0) & (i < PC))
+    @pl.when((i > FIRST) & (i < FIRST + PC))
     def _():
         buf[0:8] = buf[CH : CH + 8]
 
-    @pl.when(i < NCH)
-    def _():
-        buf[8 : CH + 8] = inv_ref[...] * inner_ref[...]
+    @pl.when((i >= FIRST) & (i < SECOND))
+    def _():
+        k = i - FIRST
+        rows = pl.ds(pl.multiple_of(k * CH, CH), CH)
+        buf[8 : CH + 8] = inv_s[rows, :] * inner_s[rows, :]
         out = conv_ref[4:5]
-        for k in range(KCONV):
-            out = out + conv_ref[k : k + 1] * buf[5 + k : 5 + k + CH]
+        for tap in range(KCONV):
+            out = out + conv_ref[tap : tap + 1] * buf[5 + tap : 5 + tap + CH]
         xconv = (out * jax.nn.sigmoid(out)).astype(bf16)
         xconv_ref[...] = xconv
-        xc_s[i] = xconv
-        part[i] = dot_nt(xproj_ref[...], xconv)
-        to_y(i).start()
-
-    @pl.when((i >= LAG) & (i < NCH + LAG))
-    def _():
-        k = i - LAG
+        xc_s[k] = xconv
+        part[k] = dot_nt(xproj_ref[...], xconv)
+        pack_sum(ys, k, part[k])
+        to_y(k).start()
+
+    @pl.when((i >= FIRST + LAG) & (i < SECOND + LAG))
+    def _():
+        k = i - FIRST - LAG
         to_y(k).wait_recv()
-        zs[k] = part[k] + yr[k]
+        part[k] = part[k] + unpack_sum(yr, k)
+        pack_sum(zs, k, part[k])
         to_z(k).start()
 
-    @pl.when((i >= 2 * LAG) & (i < NCH + 2 * LAG))
-    def _():
-        k = i - 2 * LAG
+    @pl.when((i >= FIRST + 2 * LAG) & (i < SECOND + 2 * LAG))
+    def _():
+        k = i - FIRST - 2 * LAG
         to_z(k).wait_recv()
-        xdbl_ref[k] = zs[k] + zr[k]
-
-    @pl.when(i == NCH)
-    def _():
-        gather.begin_tokens()
-
-    @pl.when(i == NCH + 2)
-    def _():
-        gather.forward(0)
-
-    @pl.when(i == NCH + 4)
-    def _():
-        gather.forward(1)
-
-    @pl.when(i == NCH + 6)
-    def _():
-        gather.forward_again(0)
-
-    @pl.when(i == 2 * NCH - 1)
+        xdbl_ref[k] = part[k] + unpack_sum(zr, k)
+
+    for n in range(2):
+
+        @pl.when(i == BEGIN[n])
+        def _(n=n):
+            gather.begin(n)
+
+        @pl.when(i == FORWARD[n])
+        def _(n=n):
+            gather.forward(n)
+
+        @pl.when(i == FORWARD_AGAIN[n])
+        def _(n=n):
+            gather.forward_again(n)
+
+    for h in range(2):
+
+        @pl.when(i == HALVES[h])
+        def _(h=h):
+            gather.begin_half(h)
+
+    @pl.when(i == FOREIGN)
+    def _():
+        gather.begin_foreign()
+
+    @pl.when(i == RELAY)
+    def _():
+        gather.relay()
+
+    @pl.when(i == LAST)
     def _():
         to_last.wait()
         state[...] = mix_ref[0:1] * last[...] + (1.0 - mix_ref[0:1]) * last_r[...]
 
-    @pl.when(i >= NCH)
-    def _():
-        k = i - NCH
+    @pl.when(i >= SECOND)
+    def _():
+        k = i - SECOND
         starts_ref[0] = state[...]
         h, yfull = scan_chunk(xdbl_ref.at[k], xc_s[k].astype(f32), dtp_ref, vec_ref, rate_ref, state[...], dt_s, u_s, cb_s, h_s, y_s)
         state[...] = h
         yfull_ref[...] = yfull.astype(bf16)
 
-    @pl.when(i == 2 * NCH - 2)
+    @pl.when(i == LAST - 1)
     def _():
         last[...] = state[...]
         to_last.start()
 
-    @pl.when(i == 2 * NCH - 1)
-    def _():
-        gather.forward_again(1)
+    @pl.when(i == LAST)
+    def _():
         gather.end_tokens()
         gather.end(0)
         gather.end(1)
@@ -713,21 +821,21 @@
         lax.fori_loop(0, NCH, sent, 0)
 
 
-def run_forward(inner, inv, mix, conv, xproj, dtp, vec, rate, in_g, out_w, cot):
-    w = inner.shape[1]
-    first = lambda i: jnp.minimum(i, NCH - 1)
-    second = lambda i: jnp.maximum(i - NCH, 0)
-    tail = lambda i: (LP // 8 - 1, 0)
+def run_forward(raw, gain, wi, mix, conv, xproj, dtp, vec, rate, in_g, out_w, cot):
+    w = SLOTS * wi.shape[2]
+    width = raw.shape[2]
+    zero = lambda i: jnp.minimum(i, FIRST - 1)
+    first = lambda i: jnp.clip(i - FIRST, 0, NCH - 1)
+    second = lambda i: jnp.maximum(i - SECOND, 0)
     dma = pltpu.SemaphoreType.DMA
-    sums = pltpu.VMEM((NCH, XW, CH), f32)
+    sums = pltpu.VMEM((NCH, XW + 2 * NSTATE, CH), bf16)
     return pl.pallas_call(
         forward,
-        grid=(2 * NCH,),
+        grid=(LAST + 1,),
         in_specs=[
-            rows_of(w, first),
-            rows_of(1, first),
-            pl.BlockSpec((8, w), tail),
-            pl.BlockSpec((8, 1), tail),
+            split_rows(width, zero, BIG),
+            whole(2, width),
+            whole(*wi.shape),
             whole(8, w),
             whole(8, w),
             whole(XW, w),
@@ -739,6 +847,9 @@
             ANY,
         ],
         out_specs=(
+            split_rows(width, zero, BIG),
+            rows_of(1, zero, BIG),
+            rows_of(w, zero, BIG),
             rows_of(w, first),
             rows_of(w, second),
             pl.BlockSpec((1, NSTATE, w), lambda i: (second(i), 0, 0)),
@@ -749,6 +860,9 @@
             ANY,
         ),
         out_shape=(
+            shaped(2, SEQ, width, dtype=bf16),
+            shaped(SEQ, 1),
+            shaped(SEQ, w),
             shaped(SEQ, w, dtype=bf16),
             shaped(SEQ, w, dtype=bf16),
             shaped(NCH, NSTATE, w),
@@ -759,8 +873,11 @@
             shaped(2, SEQ, cot.shape[1], dtype=bf16),
         ),
         scratch_shapes=[
+            pltpu.VMEM((SEQ, w), f32),
+            pltpu.VMEM((SEQ, 1), f32),
             pltpu.VMEM((CH + 8, w), f32),
             pltpu.VMEM((NCH, CH, w), bf16),
+            pltpu.VMEM((NCH, XW, CH), f32),
             sums,
             sums,
             sums,
@@ -783,7 +900,7 @@
             dimension_semantics=("arbitrary",), collective_id=2, has_side_effects=True, vmem_limit_bytes=VMEM_LIMIT
         ),
         cost_estimate=pl.CostEstimate(flops=60 * 1000000000, bytes_accessed=1000000, transcendentals=0),
-    )(inner, inv, inner, inv, mix, conv, xproj, dtp, vec, rate, in_g, out_w, cot)
+    )(raw, gain, wi, mix, conv, xproj, dtp, vec, rate, in_g, out_w, cot)
 
 
 def project_first(raw_ref, gain_ref, w_ref, normed_ref, inv_ref, out_ref):
@@ -888,13 +1005,13 @@
 
 
 def finish(inner_hbm, gate_hbm, normed_hbm, raw_hbm, wi_hbm, wg_hbm, dn_ref, grad_ref, gain_ref,
-           inner, gate, normed, raw, wi, wg, cs, cr, kept, xs, xr, fs, fr, ys, yr, zs, zr, own, gs, gr,
+           inner, gate, normed, raw, wi, wg, cs, cr, pairs, xs, xr, fs, fr, ys, yr, zs, zr, own, fin, gs, gr,
            loc, c_send, c_recv, x_send, x_recv, f_send, f_recv, y_send, y_recv, z_send, z_recv, b_send, b_recv, g_send, g_recv):
     g, r, c = lax.axis_index("grp"), lax.axis_index("row"), lax.axis_index("col")
     x, core, s, p = g // 2, g % 2, c // 2, c % 2
     tall, width = raw.shape
     part = tall // 2
-    n = wi.shape[2]
+    n = wi_hbm.shape[2]
     q = 2 * p + xor_bit(r, s)
     y_dev, z_dev = (g, 1 - r, c), (g, r, 2 * s + 1 - p)
     x_dev, core_dev = ((1 - x) * 2 + core, r, c), (2 * x + 1 - core, r, c)
@@ -904,12 +1021,16 @@
         pltpu.make_async_copy(normed_hbm, normed, loc.at[0]),
         pltpu.make_async_copy(inner_hbm, inner, loc.at[1]),
         pltpu.make_async_copy(gate_hbm, gate, loc.at[2]),
-        pltpu.make_async_copy(wi_hbm, wi, loc.at[3]),
-        pltpu.make_async_copy(wg_hbm, wg, loc.at[4]),
         pltpu.make_async_copy(raw_hbm.at[0, pl.ds(pl.multiple_of(p * tall, 64), tall)], raw, loc.at[5]),
     ]
-    for copy in loads:
+    for copy in loads[:3]:
         copy.start()
+    for k in range(SLOTS):
+        for d in range(2):
+            cols = pl.ds(k * n, n)
+            pltpu.make_async_copy(wi_hbm.at[2 * k + d], wi.at[d, :, cols], loc.at[3]).start()
+            pltpu.make_async_copy(wg_hbm.at[2 * k + d], wg.at[d, :, cols], loc.at[4]).start()
+    loads[3].start()
 
     barrier = pltpu.get_barrier_semaphore()
     for dg in range(4):
@@ -920,15 +1041,18 @@
         pl.semaphore_signal(barrier, inc=1, device_id=(g, 1 - r, (c + dc) % 4), device_id_type=MESH)
     pl.semaphore_wait(barrier, 19)
 
-    def weight_grad(d, block, store):
-        cols = pl.ds(pl.multiple_of(block * n, 128), n)
+    def weight_grad(at_x, d):
+        cols = pl.ds(pl.multiple_of(at_x * 2 * n, 128), 2 * n)
 
         def tile(t, _):
             rows = pl.ds(pl.multiple_of(t * n, 128), n)
-            store(rows, dot_tn(normed[d, :, rows], inner[:, cols]))
+            pairs[d, rows, :] = dot_tn(normed[d, :, rows], inner[:, cols])
             return 0
 
         lax.fori_loop(0, width // n, tile, 0)
+
+    def of_core(at_core):
+        return pl.ds(pl.multiple_of(at_core * n, 128), n)
 
     def to_core(i, d):
         return remote(cs.at[i, d], cr.at[i, d], c_send.at[2 * i + d], c_recv.at[2 * i + d], core_dev)
@@ -940,13 +1064,9 @@
         return remote(fs.at[d], fr.at[d], f_send.at[d], f_recv.at[d], (g, r if d == 0 else 1 - r, q))
 
     def grad_to_core(i):
-        block = 2 * (1 - x if i == 0 else x) + 1 - core
         for d in range(2):
-
-            def store(rows, v, d=d):
-                cs[i, d, rows, :] = v.astype(bf16)
-
-            weight_grad(d, block, store)
+            weight_grad(1 - x if i == 0 else x, d)
+            cs[i, d] = pairs[d, :, of_core(1 - core)].astype(bf16)
             to_core(i, d).start()
 
     def start_of(mine, h):
@@ -957,11 +1077,7 @@
 
         def tile(t, _):
             cols = pl.ds(pl.multiple_of(t * n, 128), n)
-            total = dot_nt(inner[rows, 0:n], wi[d, cols, :])
-            for j in range(1, SLOTS):
-                total = total + dot_nt(inner[rows, j * n : (j + 1) * n], wi[2 * j + d, cols, :])
-            for j in range(SLOTS):
-                total = total + dot_nt(gate[rows, j * n : (j + 1) * n], wg[2 * j + d, cols, :])
+            total = dot_nt(inner[rows, :], wi[d, cols, :]) + dot_nt(gate[rows, :], wg[d, cols, :])
             store(cols, total)
             return 0
 
@@ -984,29 +1100,23 @@
     loads[0].wait()
     loads[1].wait()
     grad_to_core(0)
-    for copy in loads[2:5]:
-        copy.wait()
+    loads[2].wait()
+    pltpu.make_async_copy(wi, wi, loc.at[3]).wait()
+    pltpu.make_async_copy(wg, wg, loc.at[4]).wait()
+    for d in range(2):
+        to_core(0, d).wait_recv()
+        xs[d] = (pairs[d, :, of_core(core)] + cr[0, d].astype(f32)).astype(bf16)
+        to_x(d).start()
+
     normed_part(False, 0, 1, into(ys, 0))
     to_y(0).start()
     normed_part(False, 1, 1, into(zs, 0))
     to_z(0).start()
-    grad_to_core(1)
-
-    for d in range(2):
-
-        def hold(rows, v, d=d):
-            kept[d, rows, :] = v
-
-        weight_grad(d, 2 * (1 - x) + core, hold)
-    for d in range(2):
-        to_core(0, d).wait_recv()
-        xs[d] = (kept[d] + cr[0, d].astype(f32)).astype(bf16)
-        to_x(d).start()
-
     normed_part(False, 1, 0, into(zs, 2))
     to_z(2).start()
     normed_part(True, 0, 1, into(ys, 1))
     to_y(1).start()
+    grad_to_core(1)
     to_y(0).wait_recv()
     normed_part(False, 0, 0, into(zs, 1, yr))
     to_z(1).start()
@@ -1015,15 +1125,9 @@
     to_y(2).start()
 
     for d in range(2):
-
-        def hold(rows, v, d=d):
-            kept[d, rows, :] = v
-
-        weight_grad(d, 2 * x + core, hold)
-    for d in range(2):
         to_core(1, d).wait_recv()
         to_x(d).wait_recv()
-        fs[d] = (kept[d] + cr[1, d].astype(f32) + xr[d].astype(f32)).astype(bf16)
+        fs[d] = (pairs[d, :, of_core(core)] + cr[1, d].astype(f32) + xr[d].astype(f32)).astype(bf16)
         if d == 0:
 
             @pl.when(alone)
@@ -1043,12 +1147,12 @@
 
         normed_part(True, h, 0, store)
 
-    loads[5].wait()
+    loads[3].wait()
     for h in range(2):
         to_y(1 + h).wait_recv()
         to_z(1 + h).wait_recv()
         total = own[h * part : (h + 1) * part, :] + yr[1 + h].astype(f32) + zr[1 + h].astype(f32)
-        own[h * part : (h + 1) * part, :] = total
+        fin[h * part : (h + 1) * part, :] = total.astype(bf16)
         product = total * raw[h * part : (h + 1) * part, :].astype(f32)
         folded = jnp.sum(product.reshape(part // 8, 8, width), axis=0)
         for b in range(SLOTS):
@@ -1068,11 +1172,11 @@
 
     def border(k):
         stays, leaves = moves[k]
-        mine = [pltpu.make_async_copy(own.at[a:b], dn_ref.at[at : at + b - a], loc.at[i]) for i, (a, b, at) in enumerate(stays)]
+        mine = [pltpu.make_async_copy(fin.at[a:b], dn_ref.at[at : at + b - a], loc.at[i]) for i, (a, b, at) in enumerate(stays)]
         if leaves is None:
             return mine, None
         a, to, at = leaves
-        return mine, remote(own.at[a : a + LC], dn_ref.at[at : at + LC], b_send.at[0], b_recv.at[0], (g, r, to))
+        return mine, remote(fin.at[a : a + LC], dn_ref.at[at : at + LC], b_send.at[0], b_recv.at[0], (g, r, to))
 
     for k in range(4):
 
@@ -1142,17 +1246,17 @@
         finish,
         in_specs=[ANY] * 6,
         out_specs=[ANY, vmem, vmem],
-        out_shape=(shaped(tall, width), shaped(width, n), shaped(8, n)),
+        out_shape=(shaped(tall, width, dtype=bf16), shaped(width, n), shaped(8, n)),
         scratch_shapes=[
             low(SEQ, w),
             low(SEQ, w),
             low(2, SEQ, width),
             low(tall, width),
-            low(2 * SLOTS, width, n),
-            low(2 * SLOTS, width, n),
+            low(2, width, w),
+            low(2, width, w),
             low(2, 2, width, n),
             low(2, 2, width, n),
-            pltpu.VMEM((2, width, n), f32),
+            pltpu.VMEM((2, width, 2 * n), f32),
             low(2, width, n),
             low(2, width, n),
             low(2, width, n),
@@ -1162,6 +1266,7 @@
             low(3, part, width),
             low(3, part, width),
             pltpu.VMEM((tall, width), f32),
+            low(tall, width),
             pltpu.VMEM((SLOTS, 8, n), f32),
             pltpu.VMEM((15, 8, n), f32),
             dma((6,)),
@@ -1227,9 +1332,16 @@
     )(order, normed, d_gate, gated, cot)
 
 
-PIECES = 8
-PIECE = SEQ // PIECES
-PIECE_STEP = (0, 0, 1, 1, 2, 3, 4, 5)
+QUARTERS = 4
+SUM_LAG = 3
+PIECE = SEQ // 2 // QUARTERS
+OTHER_STEP = (1, 2, 3, 4)
+PAIR_STEP = (3, 4, 1, 2)
+FINAL_STEP = (7, 7, 7, 7)
+X_STEP = (0, 1)
+OWNER_STEP = (2, 4)
+DONE_STEP = (8, 8)
+QUARTER_STEP = ((2, 3, 4, 5), (4, 5, 6, 7))
 
 
 def border_moves(tall):
@@ -1245,7 +1357,7 @@
 
 def backward(xdbl_ref, xconv_ref, dy_ref, dtp_ref, vec_ref, rate_ref, starts_ref, mix_ref, into_ref, sent_hbm, kept_hbm, own_hbm, oth_hbm,
              dxdbl_ref, dxc_ref, alog_ref, sums_ref, dtpg_ref, grad_ref, branch_ref,
-             first, first_s, first_r, part, yr, zs, zr, cr, kp, xs, xr, fs, fr, out, own, by, bz_s, bz, fin,
+             first, first_s, first_r, part, ys, yr, zs, zr, cr, kp, xs, xr, fs, fr, out, own, oth, by_s, by, bz_s, bz, fin,
              y_send, y_recv, z_send, z_recv, e_send, e_recv, c_send, c_recv, x_send, x_recv, f_send, f_recv,
              p_send, p_recv, q_send, q_recv, b_send, b_recv, load_k, load_o, stay, put, *scratch):
     i = pl.program_id(0)
@@ -1259,7 +1371,7 @@
     to_first = remote(first_s, first_r, e_send.at[0], e_recv.at[0], far_dev)
 
     def to_y(k):
-        return remote(part.at[k], yr.at[k], y_send.at[k], y_recv.at[k], y_dev)
+        return remote(ys.at[k], yr.at[k], y_send.at[k], y_recv.at[k], y_dev)
 
     def to_z(k):
         return remote(zs.at[k], zr.at[k], z_send.at[k], z_recv.at[k], z_dev)
@@ -1273,18 +1385,32 @@
     def to_x(n):
         return remote(xs.at[n], xr.at[n], x_send.at[n], x_recv.at[n], x_dev)
 
-    def to_owner(n, d):
-        return remote(fs.at[n, d], fr.at[n, d], f_send.at[n, d], f_recv.at[n, d], (g, r if d == 0 else 1 - r, q))
-
-    def rows_at(m):
-        base = (1 - p) if m < PIECES // 2 else p
-        return pl.ds(pl.multiple_of(base * tall + (m % (PIECES // 2)) * PIECE, 16), PIECE)
+    def to_owner(n, d, at=None):
+        device = (g, r if d == 0 else 1 - r, q)
+        if at is None:
+            return remote(fs.at[n, d], fr.at[n, d], f_send.at[n, d], f_recv.at[n, d], device)
+        tall = fs.shape[2] // QUARTERS
+        rows = pl.ds(at * tall, tall)
+        return remote(fs.at[n, d, rows], fr.at[n, d, rows], f_send.at[n, d], f_recv.at[n, d], device)
+
+    def rows_at(mine, j):
+        return pl.ds(pl.multiple_of((p if mine else 1 - p) * tall + j * PIECE, 16), PIECE)
 
     def branch_y(m):
-        return remote(oth_hbm.at[rows_at(m)], by.at[m], p_send.at[m], p_recv.at[m], y_dev)
+        if m >= QUARTERS:
+            src = oth_hbm.at[rows_at(False, m - QUARTERS)]
+        elif m < 2:
+            src = oth_hbm.at[rows_at(True, m)]
+        else:
+            src = by_s.at[m - 2]
+        return remote(src, by.at[m], p_send.at[m], p_recv.at[m], y_dev)
 
     def branch_z(m):
-        return remote(bz_s.at[m], bz.at[m], q_send.at[m], q_recv.at[m], z_dev)
+        src = bz_s.at[m] if m < QUARTERS else oth_hbm.at[rows_at(False, m - 2)]
+        return remote(src, bz.at[m], q_send.at[m], q_recv.at[m], z_dev)
+
+    load_own = pltpu.make_async_copy(own_hbm, own, load_o.at[0])
+    load_oth = pltpu.make_async_copy(oth_hbm.at[pl.ds(pl.multiple_of(p * tall + 2 * PIECE, 16), 2 * PIECE)], oth, load_o.at[1])
 
     def border(k):
         stays, leaves = border_moves(tall)[k]
@@ -1300,6 +1426,16 @@
             @pl.when(c == k)
             def _(k=k):
                 act(*border(k))
+
+    def pass_on(k):
+        to_y(k).wait_recv()
+        part[k] = part[k] + yr[k].astype(f32)
+        zs[k] = part[k].astype(bf16)
+        to_z(k).start()
+
+    def settle(k):
+        to_z(k).wait_recv()
+        dxdbl_ref[NCH - 1 - k] = part[k] + zr[k].astype(f32)
 
     @pl.when(i == 0)
     def _():
@@ -1311,11 +1447,16 @@
         for device in (x_dev, core_dev):
             pl.semaphore_signal(barrier, inc=1, device_id=device, device_id_type=MESH)
         pl.semaphore_wait(barrier, 9)
+        for j in range(2):
+            for n in range(2):
+                to_core(n, j).start()
         for n in range(2):
-            for j in range(2):
-                to_core(n, j).start()
             load(n, 0).start()
-        pltpu.make_async_copy(own_hbm, own, load_o.at[0]).start()
+        load_own.start()
+        load_oth.start()
+        for m in (QUARTERS, QUARTERS + 1):
+            branch_y(m).start()
+            branch_z(m).start()
         first[...] = jnp.zeros_like(first)
         alog_ref[...] = jnp.zeros_like(alog_ref)
         sums_ref[...] = jnp.zeros_like(sums_ref)
@@ -1335,17 +1476,20 @@
 
     @pl.when(i == 1)
     def _():
-        pltpu.make_async_copy(own_hbm, own, load_o.at[0]).wait()
-        for n in range(2):
+        load_own.wait()
+        load_oth.wait()
+
+    for n in range(2):
+
+        @pl.when(i == X_STEP[n])
+        def _(n=n):
             to_core(n, 0).wait_recv()
             load(n, 0).wait()
             xs[n] = (kp[n] + cr[n, 0].astype(f32)).astype(bf16)
             to_x(n).start()
             load(n, 1).start()
 
-    for n in range(2):
-
-        @pl.when(i == 3 + n)
+        @pl.when(i == OWNER_STEP[n])
         def _(n=n):
             load(n, 1).wait()
             to_core(n, 1).wait_recv()
@@ -1356,13 +1500,17 @@
             def _():
                 fr[n, 0] = fs[n, 0]
 
-            @pl.when(jnp.logical_not(alone))
-            def _():
-                to_owner(n, 0).start()
-
-            to_owner(n, 1).start()
-
-        @pl.when(i == 6 + n)
+        for k in range(QUARTERS):
+
+            @pl.when(i == QUARTER_STEP[n][k])
+            def _(n=n, k=k):
+                @pl.when(jnp.logical_not(alone))
+                def _():
+                    to_owner(n, 0, k).start()
+
+                to_owner(n, 1, k).start()
+
+        @pl.when(i == DONE_STEP[n])
         def _(n=n):
             @pl.when(jnp.logical_not(alone))
             def _():
@@ -1372,19 +1520,30 @@
             out[n] = fr[n, 0].astype(f32) + fr[n, 1].astype(f32)
             pltpu.make_async_copy(out.at[n], grad_ref.at[n], put.at[n]).start()
 
-    for m in range(PIECES):
-
-        @pl.when(i == PIECE_STEP[m] + 1)
-        def _(m=m):
-            branch_y(m).wait_recv()
-            total = own[rows_at(m), :] + by[m].astype(f32)
-            if m < PIECES // 2:
-                bz_s[m] = total.astype(bf16)
-                branch_z(m).start()
-            else:
-                j = m - PIECES // 2
-                branch_z(j).wait_recv()
-                fin[j * PIECE : (j + 1) * PIECE, :] = (total + bz[j].astype(f32)).astype(bf16)
+    for j in range(QUARTERS):
+
+        @pl.when(i == OTHER_STEP[j])
+        def _(j=j):
+            if j >= 2:
+                branch_z(QUARTERS + j - 2).wait_recv()
+                mine = oth[(j - 2) * PIECE : (j - 1) * PIECE, :].astype(f32)
+                by_s[j - 2] = (mine + bz[QUARTERS + j - 2].astype(f32)).astype(bf16)
+            branch_y(j).start()
+
+        @pl.when(i == PAIR_STEP[j])
+        def _(j=j):
+            total = own[rows_at(False, j), :]
+            if j < 2:
+                branch_y(QUARTERS + j).wait_recv()
+                total = total + by[QUARTERS + j].astype(f32)
+            bz_s[j] = total.astype(bf16)
+            branch_z(j).start()
+
+        @pl.when(i == FINAL_STEP[j])
+        def _(j=j):
+            branch_y(j).wait_recv()
+            branch_z(j).wait_recv()
+            fin[j * PIECE : (j + 1) * PIECE, :] = (own[rows_at(True, j), :] + by[j].astype(f32) + bz[j].astype(f32)).astype(bf16)
 
     @pl.when(i == 7)
     def _():
@@ -1396,34 +1555,18 @@
 
         at_border(begin)
 
-    @pl.when((i >= 1) & (i <= NCH - 1))
-    def _():
-        k = i - 1
-        to_y(k).wait_recv()
-        zs[k] = part[k] + yr[k]
-        to_z(k).start()
-
-    @pl.when(i >= 3)
-    def _():
-        k = i - 3
-        to_z(k).wait_recv()
-        dxdbl_ref[NCH - 1 - k] = zs[k] + zr[k]
-
+    @pl.when(i >= SUM_LAG)
+    def _():
+        pass_on(i - SUM_LAG)
+
+    ys[i] = part[i].astype(bf16)
     to_y(i).start()
-    for m in range(PIECES):
-
-        @pl.when(i == PIECE_STEP[m])
-        def _(m=m):
-            branch_y(m).start()
-
     @pl.when(i == NCH - 1)
     def _():
-        to_y(NCH - 1).wait_recv()
-        zs[NCH - 1] = part[NCH - 1] + yr[NCH - 1]
-        to_z(NCH - 1).start()
-        for k in (NCH - 3, NCH - 2, NCH - 1):
-            to_z(k).wait_recv()
-            dxdbl_ref[NCH - 1 - k] = zs[k] + zr[k]
+        for k in range(NCH - SUM_LAG, NCH):
+            pass_on(k)
+        for k in range(NCH):
+            settle(k)
 
         def finish_border(mine, gone):
             for copy in mine:
@@ -1450,10 +1593,9 @@
 
             to_owner(n, 1).wait_send()
             pltpu.make_async_copy(out.at[n], grad_ref.at[n], put.at[n]).wait()
-        for m in range(PIECES):
+        for m in range(QUARTERS + 2):
             branch_y(m).wait_send()
-            if m < PIECES // 2:
-                branch_z(m).wait_send()
+            branch_z(m).wait_send()
 
 
 def backward_kernel(*refs):
@@ -1467,7 +1609,7 @@
     at = lambda i: NCH - 1 - i
     dma = pltpu.SemaphoreType.DMA
     low = lambda *shape: pltpu.VMEM(shape, bf16)
-    sums = pltpu.VMEM((NCH, XW, CH), f32)
+    sums = low(NCH, XW, CH)
     state = pltpu.VMEM((NSTATE, w), f32)
     return pl.pallas_call(
         backward_kernel,
@@ -1498,6 +1640,7 @@
             state,
             state,
             state,
+            pltpu.VMEM((NCH, XW, CH), f32),
             sums,
             sums,
             sums,
@@ -1510,9 +1653,11 @@
             low(2, 2, tall, n),
             pltpu.VMEM((2, tall, n), f32),
             pltpu.VMEM((SEQ, width), f32),
-            low(PIECES, PIECE, width),
-            low(PIECES // 2, PIECE, width),
-            low(PIECES // 2, PIECE, width),
+            low(2 * PIECE, width),
+            low(2, PIECE, width),
+            low(QUARTERS + 2, PIECE, width),
+            low(QUARTERS, PIECE, width),
+            low(QUARTERS + 2, PIECE, width),
             low(SEQ // 2, width),
             dma((NCH,)),
             dma((NCH,)),
@@ -1526,14 +1671,14 @@
             dma((2,)),
             dma((2, 2)),
             dma((2, 2)),
-            dma((PIECES,)),
-            dma((PIECES,)),
-            dma((PIECES // 2,)),
-            dma((PIECES // 2,)),
+            dma((QUARTERS + 2,)),
+            dma((QUARTERS + 2,)),
+            dma((QUARTERS + 2,)),
+            dma((QUARTERS + 2,)),
             dma((1,)),
             dma((1,)),
             dma((2,)),
-            dma((1,)),
+            dma((2,)),
             dma((2,)),
             dma((2,)),
             *backward_scratch(w),
@@ -1673,12 +1818,12 @@
     gain_own = jnp.where(low_row, gain_all[0], gain_all[1])
     gain_two = jnp.stack([gain_own, jnp.where(low_row, gain_all[1], gain_all[0])])
 
-    normed, inv, inner = run_project_first(raw, gain_two, wi)
     zero_state = jnp.zeros((NSTATE, w), f32)
     if quick:
         mix = jnp.broadcast_to(resumes_own.astype(f32), (8, w))
-        xconv, yfull, starts, xdbl, tail, wg, wo, cot = run_forward(inner, inv, mix, conv, xproj, dtp, vec, rate, in_proj[:, 1], out_proj, cotangent)
+        normed, inv, inner, xconv, yfull, starts, xdbl, tail, wg, wo, cot = run_forward(raw, gain_two, wi, mix, conv, xproj, dtp, vec, rate, in_proj[:, 1], out_proj, cotangent)
     else:
+        normed, inv, inner = run_project_first(raw, gain_two, wi)
         tail_own = (inv * inner)[LP - 8 : LP]
         tail = jnp.where(resumes_own, tail_own, across(tail_own))
         xconv, xdbl = run_conv_forward(inner, inv, tail, conv, xproj)
@@ -1745,7 +1890,7 @@
         d_normed = from_sequences(scatter_quad(*run_normed_backward(d_inner_proj, d_gate_proj, wi, wg)))
         gain_grad = jnp.sum(d_normed * tokens.astype(f32), axis=0)
         gain_grad = lax.psum_scatter(lax.psum(gain_grad, "col"), "grp", scatter_dimension=0, tiled=True)
-    input_grad = (cotangent.astype(f32) + d_normed * gain_own - pull * tokens.astype(f32)).astype(bf16)
+    input_grad = (cotangent.astype(f32) + d_normed.astype(f32) * gain_own - pull * tokens.astype(f32)).astype(bf16)
     in_grads = jnp.stack([inner_grad, gate_grad], axis=1)
     small_grad = jnp.concatenate([conv_sums[0:5], scan_sums[0:2], alog_grad * rate, dtp_grad, xproj_grad], axis=0)
     small_grad = jnp.pad(small_grad, ((0, -small_grad.shape[0] % 8), (0, 0)))

time: 680 us -> 570 us (0.84)
  Pallas kernels: 571 us -> 456 us
  starting transfers between devices: 10.9 us -> 18.5 us
    pallas_call x1, Pallas kernels: 169 us -> 111 us  [run_forward(): pl.pallas_call(forward, grid=(LAST + 1,), in_specs=[split_rows(width, zer...]
    pallas_call x1, Pallas kernels: 149 us -> 126 us  [run_backward(): pl.pallas_call(backward_kernel, grid=(NCH,), in_specs=[chunk_of(XW, at),...]
    pallas_call x1, Pallas kernels: 75.4 us -> 61.7 us  [run_gather_start(): pl.pallas_call(gather_start, in_specs=[ANY] * 3, out_specs=[ANY] * 3, out...]
    pallas_call x4 -> x3, Pallas kernels: 53.8 us -> 43.2 us  [call(): pl.pallas_call(body, grid=(chunks,), in_specs=in_specs, out_specs=out_spe...]
    pallas_call x1, Pallas kernels: 102 us -> 93.5 us  [run_finish(): pl.pallas_call(finish, in_specs=[ANY] * 6, out_specs=[ANY, vmem, vmem], o...]
    ppermute x5, starting transfers between devices: 10.9 us -> 18.5 us  [send(): lax.ppermute(v, ('row', 'col'), [(spot(*a), spot(*b)) for a, b in pairs])]
  transfers between devices with their start and end apart: 6 -> 6, of which waited for: 4 -> 4; matrix products, arithmetic and copies ran while one was open for 2% -> 2% of each run, Pallas kernels for 15% -> 16%
where the time goes in v3:
time: 570 us; the launch traced here: 568 us
  Pallas kernels  456 us (80%)
  local copies, waits for them, and re-layouts  34 us (6%)
  waiting for transfers between devices  29.6 us (5%)
  starting transfers between devices  18.5 us (3%)
  between operations  17 us (3%)
  other arithmetic  12.4 us (2%)
    pallas_call x1, Pallas kernels, run_backward(): pl.pallas_call(backward_kernel, grid=(NCH,), in_specs=[chunk_of(XW, at),...  126 us
    pallas_call x1, Pallas kernels, run_forward(): pl.pallas_call(forward, grid=(LAST + 1,), in_specs=[split_rows(width, zer...  111 us
    pallas_call x1, Pallas kernels, run_finish(): pl.pallas_call(finish, in_specs=[ANY] * 6, out_specs=[ANY, vmem, vmem], o...  93.5 us
    pallas_call x1, Pallas kernels, run_gather_start(): pl.pallas_call(gather_start, in_specs=[ANY] * 3, out_specs=[ANY] * 3, out...  61.7 us
    pallas_call x3, Pallas kernels, call(): pl.pallas_call(body, grid=(chunks,), in_specs=in_specs, out_specs=out_spe...  43.2 us
    ppermute x5, waiting for transfers between devices, send(): lax.ppermute(v, ('row', 'col'), [(spot(*a), spot(*b)) for a, b in pairs])  29.6 us
    pallas_call x1, Pallas kernels, run_late_parts(): pl.pallas_call(late_parts, grid_spec=pltpu.PrefetchScalarGridSpec(num_sca...  21.4 us
    ppermute x5, starting transfers between devices, send(): lax.ppermute(v, ('row', 'col'), [(spot(*a), spot(*b)) for a, b in pairs])  18.5 us
  transfers between devices with their start and end apart: 6, of which 4 were waited for; matrix products, arithmetic and copies ran while one was open for 2% of the time, Pallas kernels for 16%

profile of v3, /device:TPU:14, one launch (start us, length us, event | category | flops | bytes accessed | tf_op | source)
XLA Modules:
  0.0 567.7 jit_solution(2379064265070272131)
XLA Ops:
  7.2 3.4 fusion.5
  10.8 1.2 copy_bitcast_fusion
  12.0 0.7 concatenate.54
  12.7 0.6 pad.12.small
  13.4 61.7 %shard_map.220 = (bf16[2,1152,1024]{2,1,0:T(8,128)(2,1)}, bf16[8,1024,256]{2,1,0:T(8,128)(2,1)}, bf16[8,320,128]{2,1,0:T(8,128)(2,1)}) custom-call(bf16[576,1024]{1,0:T(8,128)(2,1)} %tokens.1, bf16[1024,256]{1,0:T(8,128)(2,1)} %get-tuple-element.153.in_i, bf16[320,128]{1,0:T(8,128)(2,1)} %pad.12.small), custom_call_target="tpu_custom_call" | custom-call | tf_op jit(solution)/shard_map/pallas_call | solution.py:649
  75.1 0.8 slice_convert_fusion
  75.8 0.7 slice_bitcast_fusion.5
  76.5 1.8 copy_bitcast_fusion.2.xproj_ref
  78.3 1.7 copy_bitcast_fusion.3.dtp_ref.refs_3_
  80.1 0.7 slice_bitcast_fusion.6
  80.8 1.4 copy_bitcast_fusion.4.rate_ref.refs_5_
  85.4 0.6 pad_convert_fusion.1.conv_ref
  86.1 0.6 pad_convert_fusion.vec_ref.refs_4_
  88.5 0.6 broadcast_in_dim.25.mix_ref.refs_7_
  89.1 110.5 %shard_map.221 = (bf16[2,1152,1024]{2,1,0:T(8,128)(2,1)}, f32[1152,1]{1,0:T(8,128)}, f32[1152,1024]{1,0:T(8,128)}, bf16[1152,1024]{1,0:T(8,128)(2,1)}, bf16[1152...) custom-call(bf16[2,1152,1024]{2,1,0:T(8,128)(2,1)} %get-tuple-elemen, ...), custom_call_target="tpu_custom_call" | custom-call | flops 60000002048 | bytes 1000000 | tf_op jit(solution)/shard_map/pallas_call | solution.py:832
  199.6 22.4 %shard_map.222 = (bf16[1152,1024]{1,0:T(8,128)(2,1)}, f32[1152,1024]{1,0:T(8,128)}, bf16[1152,1024]{1,0:T(8,128)(2,1)}, f32[1152,1]{1,0:T(8,128)}, f32[1152,1024]{1,0:T(8,128)}, /*index=5*/bf16[1152,1024]{1,0:T(8,128)(2,1)}) custom-call(bf16[2,1152,1024]{2,1,0:T(8,128)(2,1)} %get-tuple-element.60.normed_ref.normed_hbm, ...), custom_call_target="tpu_custom_call" | custom-call | flops 22000001024 | bytes 1000000 | tf_op jit(solution)/shard_map/pallas_call | solution.py:278
  222.0 21.4 %shard_map.223 = (bf16[2,2,1024,256]{3,2,1,0:T(8,128)(2,1)}, bf16[2,2,1024,256]{3,2,1,0:T(8,128)(2,1)}, f32[2,2,1024,256]{3,2,1,0:T(8,128)}, f32[2,2,1024,256]{3,2,1,0:T(8,128)}) custom-call(s32[4]{0:T(128)} %pad_add_fusion.order_ref, bf16[2,1152,1024]{2,1,0:T(8,128)(2,1)} %get-tuple-element.60.normed_ref.normed_hbm, ...), custom_call_target="tpu_custom_call" | custom-call | flops 14000000000 | bytes 1000000 | tf_op jit(solution)/shard_map/pallas_call | solution.py:1316
  243.4 0.6 broadcast_in_dim.26.refs_8_
  244.0 125.9 %shard_map.224 = (f32[9,160,128]{2,1,0:T(8,128)}, f32[1152,1024]{1,0:T(8,128)}, f32[16,1024]{1,0:T(8,128)}, f32[8,1024]{1,0:T(8,128)}, f32[128,1024]{1,0:T(8,128...) custom-call(f32[9,160,128]{2,1,0:T(8,128)} %get-tuple-element.58.refs_0_, ...), custom_call_target="tpu_custom_call" | custom-call | flops 120000004096 | bytes 1000000 | tf_op jit(solution)/shard_map/pallas_call | solution.py:1614
  369.9 0.6 broadcast_1_follow_ref_sums0_ref.2.follow_ref.sums0_ref
  370.5 0.9 broadcast_in_dim.27.xprojg0_ref
  371.4 4.1 shard_map.225
  375.5 7.4 %collective-permute-start = (f32[8,1024]{1,0:T(8,128)}, f32[8,1024]{1,0:T(8,128)S(1)}, u32[]{:S(2)}, u32[]{:S(2)}) collective-permute-start(f32[8,1024]{1,0:T(8,128)} %get-tuple-element.81), channel_id=1, source_target_pairs={{0,6},{1,7},{2,4},{3,5},{4,2},{5,3},{6,0},{7,1},{8,14},{9,15},{10,... | collective-permute-start | bytes 98312 | tf_op jit(solution)/shard_map/ppermute | solution.py:1721
  382.9 0.8 fusion.4
  383.7 0.8 slice.138
  385.0 0.6 select_add_fusion.follow_ref
  385.6 16.7 %shard_map.226 = (bf16[1152,1024]{1,0:T(8,128)(2,1)}, f32[1152,1]{1,0:T(8,128)}, f32[8,1024]{1,0:T(8,128)}, f32[160,1024]{1,0:T(8,128)}, f32[8,1024]{1,0:T(8,128)}) custom-call(f32[1152,1024]{1,0:T(8,128)} %get-tuple-element.77.inner_ref.halo_ref, f32[1152,1024]{1,0:T(8,128)} %get-tuple-element.77.inner_ref.halo_ref, ...), custom_call_target="tpu_custom_call", output_to_operand_aliasing={{0}: (12, {}), {1}: (13, {})} | custom-call | flops 16000000000 | bytes 1000000 | tf_op jit(solution)/shard_map/pallas_call | solution.py:278
  402.3 5.1 concatenate.68
  407.4 1.1 pad.13
  408.5 5.9 %collective-permute-start.4 = (f32[312,1024]{1,0:T(8,128)}, f32[312,1024]{1,0:T(8,128)}, u32[]{:S(2)}, u32[]{:S(2)}) collective-permute-start(f32[312,1024]{1,0:T(8,128)} %pad.13), channel_id=1, source_target_pairs={{0,0},{4,1},{1,2},{5,3},{6,4},{2,5},{7,6},{3,7},{8,8},{12,9},{9,10... | collective-permute-start | bytes 3833864 | tf_op jit(solution)/shard_map/ppermute | solution.py:1721
  414.4 1.5 slice_bitcast_fusion
  416.2 1.6 collective-permute-start.1
  417.7 22.5 %collective-permute-done.4 = f32[312,1024]{1,0:T(8,128)} collective-permute-done((f32[312,1024]{1,0:T(8,128)}, f32[312,1024]{1,0:T(8,128)}, u32[]{:S(2)}, u32[]{:S(2)}) %collective-permute-start.4) | collective-permute-done | bytes 1277984 | tf_op jit(solution)/shard_map/ppermute | solution.py:1721
  440.3 93.5 %shard_map.227 = (bf16[576,1024]{1,0:T(8,128)(2,1)}, f32[1024,256]{1,0:T(8,128)}, f32[8,256]{1,0:T(8,128)}) custom-call(bf16[1152,1024]{1,0:T(8,128)(2,1)} %get-tuple-element.86.inner_hbm, bf16[1152,1024]{1,0:T(8,128)(2,1)} %get-tuple-element.68.gate_ref.gate_hbm, bf16[2,1152,1024]{2,1,0:T(8,128)(2,1)} %get-tuple-element.60.normed_ref.normed_hbm, ...), custom_call_target="tpu_custom_call" | custom-call | flops 60000002048 | bytes 1000000 | tf_op jit(solution)/shard_map/pallas_call | solution.py:1245
  534.2 0.7 slice_select_fusion
  534.9 1.4 collective-permute-start.2
  536.3 1.4 pad_maximum_fusion
  538.3 2.9 copy.46
  541.2 3.1 collective-permute-done.2
  544.3 1.0 fusion.3
  545.3 2.3 collective-permute-start.3
  548.0 3.5 collective-permute-done.3
  551.8 2.2 fusion.2
  554.0 1.3 slice.161
  555.2 1.3 slice_bitcast_fusion.7
  556.5 1.5 slice_bitcast_fusion.4
  558.1 1.5 slice.164
  559.6 1.3 slice.166
  (63 shorter events, 4.8 us)
Async XLA Ops:
  7.2 546.8 %reduce-scatter.2.cloned.1.call-start = ((), (), s32[]{:S(2)}) async-start(), calls=%async_computation.1 | async-start | bytes 1437696 | tf_op jit(solution)/shard_map/reduce_scatter | solution.py:1898
  10.7 1.3 copy-start.10
  10.7 1.3 copy-start.13
  10.7 1.3 copy-start.15
  10.7 1.3 copy-start.17
  10.7 1.2 copy-start.18
  10.7 1.2 copy-start.19
  10.7 1.2 copy-start.20
  10.8 1.2 copy-start.21
  11.9 70.3 %copy-start.16 = (s32[2]{0:T(128)S(1)}, s32[2]{0:T(128)}, u32[]{:S(2)}) copy-start(s32[2]{0:T(128)} %param.24) | copy-start | bytes 28
  86.7 0.6 copy-start.11
  371.4 11.5 %copy-start.9 = (f32[16,1024]{1,0:T(8,128)S(1)}, f32[16,1024]{1,0:T(8,128)}, u32[]{:S(2)}) copy-start(f32[16,1024]{1,0:T(8,128)} %get-tuple-element.95) | copy-start | bytes 196612
  375.5 9.5 %collective-permute-start = (f32[8,1024]{1,0:T(8,128)}, f32[8,1024]{1,0:T(8,128)S(1)}, u32[]{:S(2)}, u32[]{:S(2)}) collective-permute-start(f32[8,1024]{1,0:T(8,128)} %get-tuple-element.81), channel_id=1, source_target_pairs={{0,6},{1,7},{2,4},{3,5},{4,2},{5,3},{6,0},{7,1},{8,14},{9,15},{10,... | collective-permute-start | bytes 98312 | tf_op jit(solution)/shard_map/ppermute | solution.py:1721
  402.3 12.1 %copy-start.2 = (f32[2,1024,256]{2,1,0:T(8,128)S(1)}, f32[2,1024,256]{2,1,0:T(8,128)}, u32[]{:S(2)}) copy-start(f32[2,1024,256]{2,1,0:T(8,128)} %get-tuple-element.92) | copy-start | bytes 6291460
  408.5 7.4 %copy-start.7 = (f32[1152,1]{1,0:T(8,128)S(1)}, f32[1152,1]{1,0:T(8,128)}, u32[]{:S(2)}) copy-start(f32[1152,1]{1,0:T(8,128)} %get-tuple-element.88) | copy-start | bytes 13828
  408.5 7.4 %copy-start.8 = (f32[1152,1]{1,0:T(8,128)S(1)}, f32[1152,1]{1,0:T(8,128)}, u32[]{:S(2)}) copy-start(f32[1152,1]{1,0:T(8,128)} %get-tuple-element.89) | copy-start | bytes 13828
  408.5 31.7 %collective-permute-start.4 = (f32[312,1024]{1,0:T(8,128)}, f32[312,1024]{1,0:T(8,128)}, u32[]{:S(2)}, u32[]{:S(2)}) collective-permute-start(f32[312,1024]{1,0:T(8,128)} %pad.13), channel_id=1, source_target_pairs={{0,0},{4,1},{1,2},{5,3},{6,4},{2,5},{7,6},{3,7},{8,8},{12,9},{9,10... | collective-permute-start | bytes 3833864 | tf_op jit(solution)/shard_map/ppermute | solution.py:1721
  416.2 117.7 %collective-permute-start.1 = (f32[1152,1]{0,1:T(1,128)S(1)}, f32[1152,1]{0,1:T(1,128)S(1)}, u32[]{:S(2)}, u32[]{:S(2)}) collective-permute-start(f32[1152,1]{0,1:T(1,128)S(1)} %copy.44), channel_id=1, source_target_pairs={{0,4},{1,5},{2,6},{3,7},{4,0},{5,1},{6,2},{7,3},{8,12},{9,13},{10,... | collective-permute-start | bytes 13832 | tf_op jit(solution)/shard_map/ppermute | solution.py:1721
  534.1 2.2 copy-start.6
  534.2 3.5 copy-start.14
  534.9 9.3 %collective-permute-start.2 = (f32[576,1]{1,0:T(8,128)}, f32[576,1]{1,0:T(8,128)}, u32[]{:S(2)}, u32[]{:S(2)}) collective-permute-start(f32[576,1]{1,0:T(8,128)} %slice_select_fusion), channel_id=1, source_target_pairs={{0,1},{1,0},{2,3},{3,2},{4,5},{5,4},{6,7},{7,6},{8,9},{9,8},{10,11... | collective-permute-start | bytes 6920 | tf_op jit(solution)/shard_map/ppermute | solution.py:1721
  537.7 6.6 %copy-start = (f32[1152,1]{1,0:T(8,128)S(1)}, f32[1152,1]{1,0:T(8,128)}, u32[]{:S(2)}) copy-start(f32[1152,1]{1,0:T(8,128)} %get-tuple-element.65.inv_ref.halo_inv_ref) | copy-start | bytes 13828
  538.3 13.5 %copy-start.4 = (bf16[576,1024]{1,0:T(8,128)(2,1)S(1)}, bf16[576,1024]{1,0:T(8,128)(2,1)}, u32[]{:S(2)}) copy-start(bf16[576,1024]{1,0:T(8,128)(2,1)} %get-tuple-element.76) | copy-start | bytes 3538948
  538.3 13.5 %copy-start.5 = (bf16[576,1024]{1,0:T(8,128)(2,1)S(1)}, bf16[576,1024]{1,0:T(8,128)(2,1)}, u32[]{:S(2)}) copy-start(bf16[576,1024]{1,0:T(8,128)(2,1)} %get-tuple-element.87) | copy-start | bytes 3538948
  541.2 10.5 %copy-start.1 = (bf16[576,1024]{1,0:T(8,128)(2,1)S(1)}, bf16[576,1024]{1,0:T(8,128)(2,1)}, u32[]{:S(2)}) copy-start(bf16[576,1024]{1,0:T(8,128)(2,1)} %tokens.1) | copy-start | bytes 3538948
  541.2 10.5 %copy-start.3 = (bf16[576,1024]{1,0:T(8,128)(2,1)S(1)}, bf16[576,1024]{1,0:T(8,128)(2,1)}, u32[]{:S(2)}) copy-start(bf16[576,1024]{1,0:T(8,128)(2,1)} %cot_in.1) | copy-start | bytes 3538948
  541.2 10.5 %copy-start.12 = (f32[4,2,128]{2,1,0:T(2,128)S(1)}, f32[4,2,128]{2,1,0:T(2,128)}, u32[]{:S(2)}) copy-start(f32[4,2,128]{2,1,0:T(2,128)} %copy-done.11) | copy-start | bytes 12292
  545.3 6.2 %collective-permute-start.3 = (f32[128,1]{1,0:T(8,128)S(1)}, f32[128,1]{1,0:T(8,128)S(1)}, u32[]{:S(2)}, u32[]{:S(2)}) collective-permute-start(f32[128,1]{1,0:T(8,128)S(1)} %slice_select_fusion.1), channel_id=1, source_target_pairs={{2,1},{3,2},{1,3},{6,5},{7,6},{5,7},{10,9},{11,10},{9,11},{14,13},... | collective-permute-start | bytes 1544 | tf_op jit(solution)/shard_map/ppermute | solution.py:1721
Sparse Core Ops, SparseCore 0:
  440.4 42.8 reduce-scatter.1

commit v4 on v3

--- a/solution.py
+++ b/solution.py
@@ -235,17 +235,7 @@
     ]
 
 
-def conv_backward(kept, chunks, first, inner_ref, halo_ref, inv_ref, halo_inv_ref, tail_ref, conv_ref, xproj_ref, dxc_ref, dxdbl_ref, follow_ref, sums0_ref, xprojg0_ref, *refs):
-    dproj_ref, dscale_ref, sums_ref, xprojg_ref, head_ref, buf, dbuf = refs[kept:]
-    i = pl.program_id(0)
-    chunk = first + chunks - 1 - i
-
-    @pl.when(i == 0)
-    def _():
-        sums_ref[...] = sums0_ref[...]
-        xprojg_ref[...] = xprojg0_ref[...]
-        head_ref[...] = follow_ref[...]
-
+def conv_chunk(chunk, inner_ref, halo_ref, inv_ref, halo_inv_ref, tail_ref, conv_ref, xproj_ref, dxc_ref, dxdbl_ref, dproj_ref, dscale_ref, sums_ref, xprojg_ref, head_ref, buf, dbuf):
     projected = inner_ref[...]
     inv = inv_ref[...]
     before = halo_inv_ref[...] * halo_ref[...]
@@ -272,6 +262,20 @@
     dproj_ref[...] = (inv * d_inner).astype(bf16)
     dscale_ref[...] = jnp.sum(d_inner * projected, axis=1, keepdims=True)
     head_ref[...] = d_conv[0:8]
+
+
+def conv_backward(kept, chunks, first, *refs):
+    given, init, out = refs[:9], refs[9:12], refs[12 + kept :]
+    dproj_ref, dscale_ref, sums_ref, xprojg_ref, head_ref, buf, dbuf = out
+    i = pl.program_id(0)
+
+    @pl.when(i == 0)
+    def _():
+        head_ref[...] = init[0][...]
+        sums_ref[...] = init[1][...]
+        xprojg_ref[...] = init[2][...]
+
+    conv_chunk(first + chunks - 1 - i, *given, *out)
 
 
 def call(body, chunks, args, in_specs, outs, out_specs, scratch, micros, aliases=None):
@@ -1004,9 +1008,10 @@
     )
 
 
-def finish(inner_hbm, gate_hbm, normed_hbm, raw_hbm, wi_hbm, wg_hbm, dn_ref, grad_ref, gain_ref,
-           inner, gate, normed, raw, wi, wg, cs, cr, pairs, xs, xr, fs, fr, ys, yr, zs, zr, own, fin, gs, gr,
-           loc, c_send, c_recv, x_send, x_recv, f_send, f_recv, y_send, y_recv, z_send, z_recv, b_send, b_recv, g_send, g_recv):
+def finish(inner_hbm, gate_hbm, normed_hbm, raw_hbm, wi_hbm, wg_hbm, gain_in_ref, pull_ref, conv_hbm, scan_hbm, alog_hbm, dtp_hbm, xproj_hbm,
+           dn_ref, grad_ref, gain_ref, small_ref,
+           inner, gate, normed, raw, wi, wg, cs, cr, pairs, xs, xr, fs, fr, ys, yr, zs, zr, own, fin, gs, gr, sv, sr,
+           loc, c_send, c_recv, x_send, x_recv, f_send, f_recv, y_send, y_recv, z_send, z_recv, b_send, b_recv, g_send, g_recv, s_send, s_recv, s_load):
     g, r, c = lax.axis_index("grp"), lax.axis_index("row"), lax.axis_index("col")
     x, core, s, p = g // 2, g % 2, c // 2, c % 2
     tall, width = raw.shape
@@ -1034,12 +1039,28 @@
 
     barrier = pltpu.get_barrier_semaphore()
     for dg in range(4):
-        for dc in range(4):
-            if dg or dc:
-                pl.semaphore_signal(barrier, inc=1, device_id=((g + dg) % 4, r, (c + dc) % 4), device_id_type=MESH)
-    for dc in range(4):
-        pl.semaphore_signal(barrier, inc=1, device_id=(g, 1 - r, (c + dc) % 4), device_id_type=MESH)
-    pl.semaphore_wait(barrier, 19)
+        for dr in range(2):
+            for dc in range(4):
+                if dg or dr or dc:
+                    device = ((g + dg) % 4, (r + dr) % 2, (c + dc) % 4)
+                    pl.semaphore_signal(barrier, inc=1, device_id=device, device_id_type=MESH)
+    pl.semaphore_wait(barrier, 31)
+
+    def small_loads():
+        at = 0
+        for ref in (conv_hbm, scan_hbm, alog_hbm, dtp_hbm, xproj_hbm):
+            yield pltpu.make_async_copy(ref, sv.at[pl.ds(at, ref.shape[0])], s_load.at[0])
+            at += ref.shape[0]
+
+    def to_small(dg, dr):
+        to_g, to_r = (g + dg) % 4, (r + dr) % 2
+        cols = pl.ds(pl.multiple_of((to_r * 4 + to_g) * 128, 128), 128)
+        src, dst = sv.at[:, cols], sr.at[g * 2 + s]
+        return src, dst, remote(src, dst, s_send.at[2 * dg + dr], s_recv.at[0], (to_g, to_r, q))
+
+    owners = [(dg, dr) for dg in range(4) for dr in range(2)]
+    for copy in small_loads():
+        copy.start()
 
     def weight_grad(at_x, d):
         cols = pl.ds(pl.multiple_of(at_x * 2 * n, 128), 2 * n)
@@ -1107,6 +1128,21 @@
         to_core(0, d).wait_recv()
         xs[d] = (pairs[d, :, of_core(core)] + cr[0, d].astype(f32)).astype(bf16)
         to_x(d).start()
+
+    pltpu.make_async_copy(sv, sv, s_load.at[0]).wait()
+    for dg, dr in owners:
+        src, dst, copy = to_small(dg, dr)
+        if dg or dr:
+            copy.start()
+        else:
+
+            @pl.when(alone)
+            def _(src=src, dst=dst):
+                pltpu.make_async_copy(src, dst, s_load.at[1]).start()
+
+            @pl.when(jnp.logical_not(alone))
+            def _(copy=copy):
+                copy.start()
 
     normed_part(False, 0, 1, into(ys, 0))
     to_y(0).start()
@@ -1152,8 +1188,10 @@
         to_y(1 + h).wait_recv()
         to_z(1 + h).wait_recv()
         total = own[h * part : (h + 1) * part, :] + yr[1 + h].astype(f32) + zr[1 + h].astype(f32)
-        fin[h * part : (h + 1) * part, :] = total.astype(bf16)
-        product = total * raw[h * part : (h + 1) * part, :].astype(f32)
+        tokens = raw[h * part : (h + 1) * part, :].astype(f32)
+        pulled = total * gain_in_ref[0:1] - pull_ref[h * part : (h + 1) * part, :] * tokens
+        fin[h * part : (h + 1) * part, :] = pulled.astype(bf16)
+        product = total * tokens
         folded = jnp.sum(product.reshape(part // 8, 8, width), axis=0)
         for b in range(SLOTS):
             if h == 0:
@@ -1216,6 +1254,27 @@
                 copy.wait()
             if gone is not None:
                 gone.wait()
+
+    @pl.when(alone)
+    def _():
+        src, dst, _ = to_small(0, 0)
+        pltpu.make_async_copy(src, dst, s_load.at[1]).wait()
+        most = sr.at[pl.ds(0, 7)]
+        pltpu.make_async_copy(most, most, s_recv.at[0]).wait()
+
+    @pl.when(jnp.logical_not(alone))
+    def _():
+        pltpu.make_async_copy(sr, sr, s_recv.at[0]).wait()
+
+    small_ref[...] = jnp.sum(sr[...], axis=0)
+    for dg, dr in owners:
+        if dg or dr:
+            to_small(dg, dr)[2].wait_send()
+        else:
+
+            @pl.when(jnp.logical_not(alone))
+            def _():
+                to_small(0, 0)[2].wait_send()
 
     for dg, dc in pairs:
         gain_copy(dg, dc).wait_send()
@@ -1234,7 +1293,7 @@
     to_owner(1).wait_send()
 
 
-def run_finish(d_inner, d_gate, normed, raw, wi, wg):
+def run_finish(d_inner, d_gate, normed, raw, wi, wg, gain, pull, small):
     w = d_inner.shape[1]
     width, n = wi.shape[1], wi.shape[2]
     tall = SEQ // 2
@@ -1242,11 +1301,12 @@
     dma = pltpu.SemaphoreType.DMA
     low = lambda *shape: pltpu.VMEM(shape, bf16)
     vmem = pl.BlockSpec(memory_space=pltpu.VMEM)
+    rows = sum(v.shape[0] for v in small)
     return pl.pallas_call(
         finish,
-        in_specs=[ANY] * 6,
-        out_specs=[ANY, vmem, vmem],
-        out_shape=(shaped(tall, width, dtype=bf16), shaped(width, n), shaped(8, n)),
+        in_specs=[ANY] * 6 + [vmem, vmem] + [ANY] * 5,
+        out_specs=[ANY, vmem, vmem, vmem],
+        out_shape=(shaped(tall, width, dtype=bf16), shaped(width, n), shaped(8, n), shaped(rows, 128)),
         scratch_shapes=[
             low(SEQ, w),
             low(SEQ, w),
@@ -1269,6 +1329,8 @@
             low(tall, width),
             pltpu.VMEM((SLOTS, 8, n), f32),
             pltpu.VMEM((15, 8, n), f32),
+            pltpu.VMEM((rows, w), f32),
+            pltpu.VMEM((8, rows, 128), f32),
             dma((6,)),
             dma((4,)),
             dma((4,)),
@@ -1284,10 +1346,13 @@
             dma((1,)),
             dma((15,)),
             dma((1,)),
+            dma((8,)),
+            dma((1,)),
+            dma((2,)),
         ],
         compiler_params=pltpu.CompilerParams(collective_id=1, has_side_effects=True, vmem_limit_bytes=VMEM_LIMIT),
         cost_estimate=pl.CostEstimate(flops=60 * 1000000000, bytes_accessed=1000000, transcendentals=0),
-    )(d_inner, d_gate, normed, raw, wi, wg)
+    )(d_inner, d_gate, normed, raw, wi, wg, gain, pull, *small)
 
 
 def late_parts(order_ref, normed_ref, gate_ref, gated_ref, cot_ref, gate_sent, out_sent, gate_kept, out_kept):
@@ -1690,6 +1755,75 @@
     )(xdbl, xconv, dy, dtp, vec, rate, starts, mix, into, *sent, *kept, own, oth)
 
 
+def conv_backward_far(inner_ref, halo_ref, inv_ref, halo_inv_ref, tail_ref, conv_ref, xproj_ref, dxc_ref, dxdbl_ref, mix_ref, into_ref,
+                      dproj_ref, dscale_ref, sums_ref, xprojg_ref, head, sent, got, buf, dbuf, send_sem, recv_sem):
+    i = pl.program_id(0)
+    g, r, c = lax.axis_index("grp"), lax.axis_index("row"), lax.axis_index("col")
+    far_dev = (g, 1 - r, (c + 2) % 4)
+    to_far = remote(sent, got, send_sem.at[0], recv_sem.at[0], far_dev)
+
+    @pl.when(i == 0)
+    def _():
+        barrier = pltpu.get_barrier_semaphore()
+        pl.semaphore_signal(barrier, inc=1, device_id=far_dev, device_id_type=MESH)
+        pl.semaphore_wait(barrier, 1)
+        head[...] = jnp.zeros_like(head)
+        sums_ref[...] = jnp.zeros_like(sums_ref)
+        xprojg_ref[...] = jnp.zeros_like(xprojg_ref)
+
+    @pl.when(i == 1)
+    def _():
+        to_far.wait()
+        head[...] = mix_ref[...] * sent[...] + into_ref[...] * got[...]
+
+    conv_chunk(NCH - 1 - i, inner_ref, halo_ref, inv_ref, halo_inv_ref, tail_ref, conv_ref, xproj_ref, dxc_ref, dxdbl_ref,
+               dproj_ref, dscale_ref, sums_ref, xprojg_ref, head, buf, dbuf)
+
+    @pl.when(i == 0)
+    def _():
+        sent[...] = head[...]
+        to_far.start()
+
+
+def run_conv_backward_far(inner, inv, tail, conv, xproj, dxc, dxdbl, mix, into):
+    w = inner.shape[1]
+    at = lambda i: NCH - 1 - i
+    before = lambda i: (jnp.maximum(at(i) * (CH // 8) - 1, 0), 0)
+    rows = pltpu.VMEM((8, w), f32)
+    return pl.pallas_call(
+        conv_backward_far,
+        grid=(NCH,),
+        in_specs=[
+            rows_of(w, at),
+            pl.BlockSpec((8, w), before),
+            rows_of(1, at),
+            pl.BlockSpec((8, 1), before),
+            whole(8, w),
+            whole(8, w),
+            whole(XW, w),
+            rows_of(w, at),
+            chunk_of(XW, at),
+            whole(8, w),
+            whole(8, w),
+        ],
+        out_specs=(rows_of(w, at), rows_of(1, at), whole(8, w), whole(XW, w)),
+        out_shape=(shaped(SEQ, w, dtype=bf16), shaped(SEQ, 1), shaped(8, w), shaped(XW, w)),
+        scratch_shapes=[
+            rows,
+            rows,
+            rows,
+            pltpu.VMEM((CH + 8, w), f32),
+            pltpu.VMEM((CH + 8, w), f32),
+            pltpu.SemaphoreType.DMA((1,)),
+            pltpu.SemaphoreType.DMA((1,)),
+        ],
+        compiler_params=pltpu.CompilerParams(
+            dimension_semantics=("arbitrary",), collective_id=4, has_side_effects=True, vmem_limit_bytes=VMEM_LIMIT
+        ),
+        cost_estimate=pl.CostEstimate(flops=20 * 1000000000, bytes_accessed=1000000, transcendentals=0),
+    )(inner, inner, inv, inv, tail, conv, xproj, dxc, dxdbl, mix, into)
+
+
 def per_device(
     tokens,
     gain,
@@ -1871,31 +2005,44 @@
         dxdbl = jnp.swapaxes(dxdbl.reshape(XW, NCH, CH), 0, 1)
 
     output = (tokens.astype(f32) + branch.astype(f32)).astype(bf16)
-    sums = (jnp.zeros((8, w), f32), jnp.zeros((XW, w), f32))
-    dp, ds, *sums, head = conv_back(PC, NCH - PC, dxc=dxc, dxdbl=dxdbl, follow=zero_head, sums=sums)
-    follow = jnp.where(resumes_own, head, 0.0) + jnp.where(resumed_by_other, across(head), 0.0)
-    d_inner_proj, inner_scale, conv_sums, xproj_grad, _ = conv_back(0, PC, dxc=dxc, dxdbl=dxdbl, follow=follow, sums=sums, kept=(dp, ds))
+    if quick:
+        d_inner_proj, inner_scale, conv_sums, xproj_grad = run_conv_backward_far(inner, inv, tail, conv, xproj, dxc, dxdbl, mix, into)
+    else:
+        sums = (jnp.zeros((8, w), f32), jnp.zeros((XW, w), f32))
+        dp, ds, *sums, head = conv_back(PC, NCH - PC, dxc=dxc, dxdbl=dxdbl, follow=zero_head, sums=sums)
+        follow = jnp.where(resumes_own, head, 0.0) + jnp.where(resumed_by_other, across(head), 0.0)
+        d_inner_proj, inner_scale, conv_sums, xproj_grad, _ = conv_back(0, PC, dxc=dxc, dxdbl=dxdbl, follow=follow, sums=sums, kept=(dp, ds))
 
     scale = gate_scale + inner_scale
-    scale = scale + swap(scale)
-    first, second = scale[:local], scale[local:]
-    scale_own = jnp.where(low_pair, first, second) + pair(jnp.where(low_pair, second, first))
-    inv_own = jnp.where(low_pair, inv[:local], inv[local:])
-    pull = from_sequences(scale_own * inv_own * inv_own * inv_own / D)
+
+    def own_rows(v):
+        return jnp.where(low_pair, v[:local], v[local:])
+
+    def pair_rows(v):
+        return jnp.where(low_pair, v[local:], v[:local])
+
+    diagonal = send(pair_rows(scale), [((r, c), (1 - r, c ^ 1)) for r, c in places])
+    scale = own_rows(scale) + swap(own_rows(scale)) + pair(pair_rows(scale)) + diagonal
+    inv_own = own_rows(inv)
+    pull = scale * inv_own * inv_own * inv_own / D
+    small_parts = (conv_sums, scan_sums, alog_grad * rate, dtp_grad, xproj_grad)
     if quick:
-        d_normed, inner_grad, gain_sum = run_finish(d_inner_proj, d_gate_proj, normed, raw, wi, wg)
+        pulled, inner_grad, gain_sum, small_grad = run_finish(
+            d_inner_proj, d_gate_proj, normed, raw, wi, wg, jnp.broadcast_to(gain_own[None], (8, width)), pull, small_parts
+        )
         gain_grad = jnp.sum(gain_sum, axis=0)
     else:
         inner_grad = collect([scatter_grp(dot_tn(normed[d], d_inner_proj), 1) for d in range(2)])
-        d_normed = from_sequences(scatter_quad(*run_normed_backward(d_inner_proj, d_gate_proj, wi, wg)))
-        gain_grad = jnp.sum(d_normed * tokens.astype(f32), axis=0)
+        d_normed = scatter_quad(*run_normed_backward(d_inner_proj, d_gate_proj, wi, wg))
+        fixed = own_rows(raw[0]).astype(f32)
+        gain_grad = jnp.sum(d_normed * fixed, axis=0)
         gain_grad = lax.psum_scatter(lax.psum(gain_grad, "col"), "grp", scatter_dimension=0, tiled=True)
-    input_grad = (cotangent.astype(f32) + d_normed.astype(f32) * gain_own - pull * tokens.astype(f32)).astype(bf16)
+        pulled = from_sequences((d_normed * gain_own - pull * fixed).astype(bf16))
+        small_grad = send(jnp.concatenate(small_parts, axis=0), back(spread))
+        small_grad = lax.psum_scatter(small_grad, ("row", "grp"), scatter_dimension=1, tiled=True)
+    input_grad = (cotangent.astype(f32) + pulled.astype(f32)).astype(bf16)
     in_grads = jnp.stack([inner_grad, gate_grad], axis=1)
-    small_grad = jnp.concatenate([conv_sums[0:5], scan_sums[0:2], alog_grad * rate, dtp_grad, xproj_grad], axis=0)
-    small_grad = jnp.pad(small_grad, ((0, -small_grad.shape[0] % 8), (0, 0)))
-    small_grad = send(small_grad, back(spread))
-    small_grad = lax.psum_scatter(small_grad, ("row", "grp"), scatter_dimension=1, tiled=True)
+    rank_at = 16 + NSTATE
     return (
         output,
         input_grad,
@@ -1903,11 +2050,11 @@
         in_grads,
         small_grad[0:4],
         small_grad[4],
-        small_grad[7 + NSTATE + RANK : 7 + NSTATE + RANK + XW].T,
-        small_grad[7 + NSTATE : 7 + NSTATE + RANK],
-        small_grad[5],
-        small_grad[7 : 7 + NSTATE],
-        small_grad[6],
+        small_grad[rank_at + RANK :].T,
+        small_grad[rank_at : rank_at + RANK],
+        small_grad[8],
+        small_grad[16 : 16 + NSTATE],
+        small_grad[9],
         out_grad,
     )
 

time: 570 us -> 546 us (0.958)
  Pallas kernels: 456 us -> 493 us
  waiting for transfers between devices: 29.6 us -> 5.12 us
  starting transfers between devices: 18.5 us -> 4.01 us
  between operations: 17 us -> 3.54 us
  local copies, waits for them, and re-layouts: 34 us -> 24.8 us
    pallas_call x1 -> x2, Pallas kernels: 93.5 us -> 151 us  [the longest x1 123 us: run_finish(): pl.pallas_call(finish, in_specs=[ANY] * 6 + [vmem, vmem] + [ANY] * 5, out...]
    ppermute x5 -> x3, waiting for transfers between devices: 29.6 us -> 5.12 us  [send(): lax.ppermute(v, ('row', 'col'), [(spot(*a), spot(*b)) for a, b in pairs])]
    pallas_call x3 -> x1, Pallas kernels: 43.2 us -> 22.4 us  [call(): pl.pallas_call(body, grid=(chunks,), in_specs=in_specs, out_specs=out_spe...]
    ppermute x5 -> x3, starting transfers between devices: 18.5 us -> 4.01 us  [send(): lax.ppermute(v, ('row', 'col'), [(spot(*a), spot(*b)) for a, b in pairs])]
  transfers between devices with their start and end apart: 6 -> 3, of which waited for: 4 -> 1; matrix products, arithmetic and copies ran while one was open for 2% -> 1% of each run, Pallas kernels for 16% -> 0%
where the time goes in v4:
time: 546 us; the launch traced here: 543 us
  Pallas kernels  493 us (90%)
  local copies, waits for them, and re-layouts  24.8 us (5%)
  other arithmetic  13.1 us (2%)
    pallas_call x1, Pallas kernels, run_backward(): pl.pallas_call(backward_kernel, grid=(NCH,), in_specs=[chunk_of(XW, at),...  126 us
    pallas_call x1, Pallas kernels, run_finish(): pl.pallas_call(finish, in_specs=[ANY] * 6 + [vmem, vmem] + [ANY] * 5, out...  123 us
    pallas_call x1, Pallas kernels, run_forward(): pl.pallas_call(forward, grid=(LAST + 1,), in_specs=[split_rows(width, zer...  110 us
    pallas_call x1, Pallas kernels, run_gather_start(): pl.pallas_call(gather_start, in_specs=[ANY] * 3, out_specs=[ANY] * 3, out...  61.7 us
    pallas_call x1, Pallas kernels, run_conv_backward_far(): pl.pallas_call(conv_backward_far, grid=(NCH,), in_specs=[rows_of(w, at),...  28.1 us
    pallas_call x1, Pallas kernels, call(): pl.pallas_call(body, grid=(chunks,), in_specs=in_specs, out_specs=out_spe...  22.4 us
    pallas_call x1, Pallas kernels, run_late_parts(): pl.pallas_call(late_parts, grid_spec=pltpu.PrefetchScalarGridSpec(num_sca...  21.3 us
  transfers between devices with their start and end apart: 3, of which 1 were waited for; matrix products, arithmetic and copies ran while one was open for 1% of the time, Pallas kernels for 0%

profile of v4, /device:TPU:14, one launch (start us, length us, event | category | flops | bytes accessed | tf_op | source)
XLA Modules:
  0.0 543.4 jit_solution(181490743257270019)
XLA Ops:
  0.7 3.3 fusion.2
  4.0 0.0 copy-start.8
  4.0 0.0 copy-start.11
  4.0 0.0 copy-start.15
  4.1 0.0 copy-start.16
  4.1 0.0 copy-start.19
  4.1 1.2 copy_bitcast_fusion
  5.3 0.7 concatenate.15
  6.1 0.6 pad.8.small
  6.7 61.7 %shard_map.220 = (bf16[2,1152,1024]{2,1,0:T(8,128)(2,1)}, bf16[8,1024,256]{2,1,0:T(8,128)(2,1)}, bf16[8,320,128]{2,1,0:T(8,128)(2,1)}) custom-call(bf16[576,1024]{1,0:T(8,128)(2,1)} %tokens.1, bf16[1024,256]{1,0:T(8,128)(2,1)} %get-tuple-element.128.in_i, bf16[320,128]{1,0:T(8,128)(2,1)} %pad.8.small), custom_call_target="tpu_custom_call" | custom-call | tf_op jit(solution)/shard_map/pallas_call | solution.py:653
  68.4 0.8 slice_convert_fusion
  69.2 1.8 copy_bitcast_fusion.2.xproj_ref
  71.0 1.7 copy_bitcast_fusion.3.dtp_ref.refs_3_
  72.7 1.4 copy_bitcast_fusion.4.rate_ref.refs_5_
  74.1 0.7 slice_bitcast_fusion.5
  74.8 0.7 slice_bitcast_fusion.6
  75.6 0.6 fusion.3
  78.8 0.6 pad_convert_fusion.1.conv_ref
  79.4 0.6 pad_convert_fusion.vec_ref.refs_4_
  80.0 0.6 copy-done.9
  80.6 0.6 pad_maximum_fusion.1.gain_ref
  81.2 0.6 pad_add_fusion.order_ref
  81.8 0.6 broadcast_in_dim.26.mix_ref.refs_7_
  82.4 110.5 %shard_map.221 = (bf16[2,1152,1024]{2,1,0:T(8,128)(2,1)}, f32[1152,1]{1,0:T(8,128)}, f32[1152,1024]{1,0:T(8,128)}, bf16[1152,1024]{1,0:T(8,128)(2,1)}, bf16[1152...) custom-call(bf16[2,1152,1024]{2,1,0:T(8,128)(2,1)} %get-tuple-elemen, ...), custom_call_target="tpu_custom_call" | custom-call | flops 60000002048 | bytes 1000000 | tf_op jit(solution)/shard_map/pallas_call | solution.py:836
  192.9 22.4 %shard_map.222 = (bf16[1152,1024]{1,0:T(8,128)(2,1)}, f32[1152,1024]{1,0:T(8,128)}, bf16[1152,1024]{1,0:T(8,128)(2,1)}, f32[1152,1]{1,0:T(8,128)}, f32[1152,1024]{1,0:T(8,128)}, /*index=5*/bf16[1152,1024]{1,0:T(8,128)(2,1)}) custom-call(bf16[2,1152,1024]{2,1,0:T(8,128)(2,1)} %get-tuple-element.56.normed_ref.normed_hbm, ...), custom_call_target="tpu_custom_call" | custom-call | flops 22000001024 | bytes 1000000 | tf_op jit(solution)/shard_map/pallas_call | solution.py:282
  215.3 21.3 %shard_map.223 = (bf16[2,2,1024,256]{3,2,1,0:T(8,128)(2,1)}, bf16[2,2,1024,256]{3,2,1,0:T(8,128)(2,1)}, f32[2,2,1024,256]{3,2,1,0:T(8,128)}, f32[2,2,1024,256]{3,2,1,0:T(8,128)}) custom-call(s32[4]{0:T(128)} %pad_add_fusion.order_ref, bf16[2,1152,1024]{2,1,0:T(8,128)(2,1)} %get-tuple-element.56.normed_ref.normed_hbm, ...), custom_call_target="tpu_custom_call" | custom-call | flops 14000000000 | bytes 1000000 | tf_op jit(solution)/shard_map/pallas_call | solution.py:1381
  236.6 0.6 broadcast_in_dim.27.refs_8_.into_ref
  237.3 125.9 %shard_map.224 = (f32[9,160,128]{2,1,0:T(8,128)}, f32[1152,1024]{1,0:T(8,128)}, f32[16,1024]{1,0:T(8,128)}, f32[8,1024]{1,0:T(8,128)}, f32[128,1024]{1,0:T(8,128...) custom-call(f32[9,160,128]{2,1,0:T(8,128)} %get-tuple-element.54.refs_0_, ...), custom_call_target="tpu_custom_call" | custom-call | flops 120000004096 | bytes 1000000 | tf_op jit(solution)/shard_map/pallas_call | solution.py:1679
  363.2 28.1 %shard_map.225 = (bf16[1152,1024]{1,0:T(8,128)(2,1)}, f32[1152,1]{1,0:T(8,128)}, f32[8,1024]{1,0:T(8,128)}, f32[160,1024]{1,0:T(8,128)}) custom-call(f32[1152,1024]{1,0:T(8,128)} %get-tuple-element.73.inner_ref.halo_ref, f32[1152,1024]{1,0:T(8,128)} %get-tuple-element.73.inner_ref.halo_ref, f32[1152,1]{1,0:T(8,128)} %get-tuple-element.61.inv_ref.halo_inv_ref, ...), custom_call_target="tpu_custom_call" | custom-call | flops 20000000000 | bytes 1000000 | tf_op jit(solution)/shard_map/pallas_call | solution.py:1793
  391.4 1.3 add.52
  392.7 2.5 collective-permute-start.1
  395.2 1.5 collective-permute-start
  396.7 1.1 slice_bitcast_fusion
  397.9 1.5 add_convert_fusion.1
  399.4 1.5 fusion.1.alog_hbm
  400.8 5.1 collective-permute-done
  406.0 0.8 fusion.pull_ref
  406.8 0.6 broadcast_in_dim.29.gain_in_ref
  407.4 122.8 %shard_map.226 = (bf16[576,1024]{1,0:T(8,128)(2,1)}, f32[1024,256]{1,0:T(8,128)}, f32[8,256]{1,0:T(8,128)}, f32[320,128]{1,0:T(8,128)}) custom-call(bf16[1152,1024]{1,0:T(8,128)(2,1)} %get-tuple-element.77.inner_hbm, bf16[1152,1024]{1,0:T(8,128)(2,1)} %get-tuple-element.64.gate_ref.gate_hbm, bf16[2,1152,1024]{2,1,0:T(8,128)(2,1)} %get-tuple-element.56.normed_ref.normed_hbm, ...), custom_call_target="tpu_custom_call" | custom-call | flops 60000002048 | bytes 1000000 | tf_op jit(solution)/shard_map/pallas_call | solution.py:1305
  530.1 1.5 slice_bitcast_fusion.4
  531.7 1.5 slice.118
  533.1 1.3 slice.120
  534.4 1.3 slice.115
  535.7 1.3 slice_bitcast_fusion.7
  537.0 1.4 pad_maximum_fusion
  538.4 2.9 copy.36
  541.3 1.5 add_convert_fusion
  542.8 0.6 reduce_sum.9
  (39 shorter events, 0.1 us)
Async XLA Ops:
  4.0 1.3 copy-start.8
  4.0 1.3 copy-start.11
  4.0 1.3 copy-start.13
  4.0 1.3 copy-start.15
  4.1 1.2 copy-start.16
  4.1 1.2 copy-start.17
  4.1 1.2 copy-start.18
  4.1 1.2 copy-start.19
  5.3 70.3 %copy-start.14 = (s32[2]{0:T(128)S(1)}, s32[2]{0:T(128)}, u32[]{:S(2)}) copy-start(s32[2]{0:T(128)} %param.24) | copy-start | bytes 28
  80.0 0.6 copy-start.9
  363.2 28.2 %copy-start.6 = (f32[1152,1]{1,0:T(8,128)S(1)}, f32[1152,1]{1,0:T(8,128)}, u32[]{:S(2)}) copy-start(f32[1152,1]{1,0:T(8,128)} %get-tuple-element.78) | copy-start | bytes 13828
  391.4 5.4 copy-start.1
  392.7 5.2 copy-start
  392.7 5.1 copy-start.3
  392.7 13.2 %collective-permute-start.1 = (f32[576,1]{1,0:T(8,128)S(1)}, f32[576,1]{1,0:T(8,128)S(1)}, u32[]{:S(2)}, u32[]{:S(2)}) collective-permute-start(f32[576,1]{1,0:T(8,128)S(1)} %get-tuple-element.119), channel_id=1, source_target_pairs={{0,1},{1,0},{2,3},{3,2},{4,5},{5,4},{6,7},{7,6},{8,9},{9,8},{10,11... | collective-permute-start | bytes 6920 | tf_op jit(solution)/shard_map/ppermute | solution.py:1855
  395.2 10.7 %collective-permute-start.2 = (f32[576,1]{1,0:T(8,128)S(1)}, f32[576,1]{1,0:T(8,128)S(1)}, u32[]{:S(2)}, u32[]{:S(2)}) collective-permute-start(f32[576,1]{1,0:T(8,128)S(1)} %get-tuple-element.119), channel_id=1, source_target_pairs={{0,5},{1,4},{2,7},{3,6},{4,1},{5,0},{6,3},{7,2},{8,13},{9,12},{10,... | collective-permute-start | bytes 6920 | tf_op jit(solution)/shard_map/ppermute | solution.py:1855
  395.2 10.7 %collective-permute-start = (f32[576,1]{1,0:T(8,128)S(1)}, f32[576,1]{1,0:T(8,128)S(1)}, u32[]{:S(2)}, u32[]{:S(2)}) collective-permute-start(f32[576,1]{1,0:T(8,128)S(1)} %get-tuple-element.118), channel_id=1, source_target_pairs={{0,4},{1,5},{2,6},{3,7},{4,0},{5,1},{6,2},{7,3},{8,12},{9,13},{10,... | collective-permute-start | bytes 6920 | tf_op jit(solution)/shard_map/ppermute | solution.py:1855
  397.9 1.5 copy-start.7
  397.9 8.1 %copy-start.5 = (f32[1152,1]{1,0:T(8,128)S(1)}, f32[1152,1]{1,0:T(8,128)}, u32[]{:S(2)}) copy-start(f32[1152,1]{1,0:T(8,128)} %get-tuple-element.61.inv_ref.halo_inv_ref) | copy-start | bytes 13828
  397.9 8.9 %copy-start.10 = (f32[4,2,128]{2,1,0:T(2,128)S(1)}, f32[4,2,128]{2,1,0:T(2,128)}, u32[]{:S(2)}) copy-start(f32[4,2,128]{2,1,0:T(2,128)} %copy-done.9) | copy-start | bytes 12292
  538.3 3.0 copy-start.2
  538.4 3.0 copy-start.4
  541.3 1.5 copy-start.12

commit v5 on v4

--- a/solution.py
+++ b/solution.py
@@ -1009,8 +1009,8 @@
 
 
 def finish(inner_hbm, gate_hbm, normed_hbm, raw_hbm, wi_hbm, wg_hbm, gain_in_ref, pull_ref, conv_hbm, scan_hbm, alog_hbm, dtp_hbm, xproj_hbm,
-           dn_ref, grad_ref, gain_ref, small_ref,
-           inner, gate, normed, raw, wi, wg, cs, cr, pairs, xs, xr, fs, fr, ys, yr, zs, zr, own, fin, gs, gr, sv, sr,
+           dn_ref, grad_ref, gain_ref, small_refs,
+           inner, gate, normed, raw, wi, wg, cs, cr, pairs, xs, xr, fs, fr, ys, yr, zs, zr, own, fin, gs, gr, sv, kr, ks, kx, kf, kg,
            loc, c_send, c_recv, x_send, x_recv, f_send, f_recv, y_send, y_recv, z_send, z_recv, b_send, b_recv, g_send, g_recv, s_send, s_recv, s_load):
     g, r, c = lax.axis_index("grp"), lax.axis_index("row"), lax.axis_index("col")
     x, core, s, p = g // 2, g % 2, c // 2, c % 2
@@ -1039,12 +1039,12 @@
 
     barrier = pltpu.get_barrier_semaphore()
     for dg in range(4):
-        for dr in range(2):
-            for dc in range(4):
-                if dg or dr or dc:
-                    device = ((g + dg) % 4, (r + dr) % 2, (c + dc) % 4)
-                    pl.semaphore_signal(barrier, inc=1, device_id=device, device_id_type=MESH)
-    pl.semaphore_wait(barrier, 31)
+        for dc in range(4):
+            if dg or dc:
+                pl.semaphore_signal(barrier, inc=1, device_id=((g + dg) % 4, r, (c + dc) % 4), device_id_type=MESH)
+    for dc in range(4):
+        pl.semaphore_signal(barrier, inc=1, device_id=(g, 1 - r, (c + dc) % 4), device_id_type=MESH)
+    pl.semaphore_wait(barrier, 19)
 
     def small_loads():
         at = 0
@@ -1052,13 +1052,20 @@
             yield pltpu.make_async_copy(ref, sv.at[pl.ds(at, ref.shape[0])], s_load.at[0])
             at += ref.shape[0]
 
-    def to_small(dg, dr):
-        to_g, to_r = (g + dg) % 4, (r + dr) % 2
-        cols = pl.ds(pl.multiple_of((to_r * 4 + to_g) * 128, 128), 128)
-        src, dst = sv.at[:, cols], sr.at[g * 2 + s]
-        return src, dst, remote(src, dst, s_send.at[2 * dg + dr], s_recv.at[0], (to_g, to_r, q))
-
-    owners = [(dg, dr) for dg in range(4) for dr in range(2)]
+    def channels(d, at_x, at_core):
+        to_r = r if d == 0 else 1 - r
+        return pl.ds(pl.multiple_of((to_r * 4 + 2 * at_x + at_core) * 128, 128), 128)
+
+    def small_core(j, d):
+        src = sv.at[:, channels(d, 1 - x if j == 0 else x, 1 - core)]
+        return remote(src, kr.at[j, d], s_send.at[2 * j + d], s_recv.at[2 * j + d], core_dev)
+
+    def small_x(d):
+        return remote(ks.at[d], kx.at[d], s_send.at[4 + d], s_recv.at[4 + d], x_dev)
+
+    def small_owner(d):
+        return remote(kf.at[d], kg.at[d], s_send.at[6 + d], s_recv.at[6 + d], (g, r if d == 0 else 1 - r, q))
+
     for copy in small_loads():
         copy.start()
 
@@ -1118,6 +1125,10 @@
 
         return store
 
+    pltpu.make_async_copy(sv, sv, s_load.at[0]).wait()
+    for j in range(2):
+        for d in range(2):
+            small_core(j, d).start()
     loads[0].wait()
     loads[1].wait()
     grad_to_core(0)
@@ -1129,20 +1140,10 @@
         xs[d] = (pairs[d, :, of_core(core)] + cr[0, d].astype(f32)).astype(bf16)
         to_x(d).start()
 
-    pltpu.make_async_copy(sv, sv, s_load.at[0]).wait()
-    for dg, dr in owners:
-        src, dst, copy = to_small(dg, dr)
-        if dg or dr:
-            copy.start()
-        else:
-
-            @pl.when(alone)
-            def _(src=src, dst=dst):
-                pltpu.make_async_copy(src, dst, s_load.at[1]).start()
-
-            @pl.when(jnp.logical_not(alone))
-            def _(copy=copy):
-                copy.start()
+    for d in range(2):
+        small_core(0, d).wait_recv()
+        ks[d] = sv[:, channels(d, 1 - x, core)] + kr[0, d]
+        small_x(d).start()
 
     normed_part(False, 0, 1, into(ys, 0))
     to_y(0).start()
@@ -1175,6 +1176,20 @@
                 to_owner(0).start()
         else:
             to_owner(1).start()
+    for d in range(2):
+        small_core(1, d).wait_recv()
+        small_x(d).wait_recv()
+        kf[d] = sv[:, channels(d, x, core)] + kr[1, d] + kx[d]
+
+    @pl.when(alone)
+    def _():
+        kg[0] = kf[0]
+
+    @pl.when(jnp.logical_not(alone))
+    def _():
+        small_owner(0).start()
+
+    small_owner(1).start()
 
     for h in range(2):
 
@@ -1255,26 +1270,19 @@
             if gone is not None:
                 gone.wait()
 
-    @pl.when(alone)
-    def _():
-        src, dst, _ = to_small(0, 0)
-        pltpu.make_async_copy(src, dst, s_load.at[1]).wait()
-        most = sr.at[pl.ds(0, 7)]
-        pltpu.make_async_copy(most, most, s_recv.at[0]).wait()
-
     @pl.when(jnp.logical_not(alone))
     def _():
-        pltpu.make_async_copy(sr, sr, s_recv.at[0]).wait()
-
-    small_ref[...] = jnp.sum(sr[...], axis=0)
-    for dg, dr in owners:
-        if dg or dr:
-            to_small(dg, dr)[2].wait_send()
-        else:
-
-            @pl.when(jnp.logical_not(alone))
-            def _():
-                to_small(0, 0)[2].wait_send()
+        small_owner(0).wait()
+
+    small_owner(1).wait()
+    at = 0
+    for ref in small_refs:
+        ref[...] = kg[0, at : at + ref.shape[0], :] + kg[1, at : at + ref.shape[0], :]
+        at += ref.shape[0]
+    for d in range(2):
+        for j in range(2):
+            small_core(j, d).wait_send()
+        small_x(d).wait_send()
 
     for dg, dc in pairs:
         gain_copy(dg, dc).wait_send()
@@ -1291,6 +1299,14 @@
         to_owner(0).wait_send()
 
     to_owner(1).wait_send()
+
+
+SMALL_ROWS = (KCONV, 1, 3, 1, 1, 6, NSTATE, RANK, XW)
+
+
+def finish_kernel(*refs):
+    n = len(SMALL_ROWS)
+    finish(*refs[:16], refs[16 : 16 + n], *refs[16 + n :])
 
 
 def run_finish(d_inner, d_gate, normed, raw, wi, wg, gain, pull, small):
@@ -1303,10 +1319,10 @@
     vmem = pl.BlockSpec(memory_space=pltpu.VMEM)
     rows = sum(v.shape[0] for v in small)
     return pl.pallas_call(
-        finish,
+        finish_kernel,
         in_specs=[ANY] * 6 + [vmem, vmem] + [ANY] * 5,
-        out_specs=[ANY, vmem, vmem, vmem],
-        out_shape=(shaped(tall, width, dtype=bf16), shaped(width, n), shaped(8, n), shaped(rows, 128)),
+        out_specs=[ANY, vmem, vmem] + [vmem] * len(SMALL_ROWS),
+        out_shape=(shaped(tall, width, dtype=bf16), shaped(width, n), shaped(8, n), *[shaped(v, 128) for v in SMALL_ROWS]),
         scratch_shapes=[
             low(SEQ, w),
             low(SEQ, w),
@@ -1330,7 +1346,11 @@
             pltpu.VMEM((SLOTS, 8, n), f32),
             pltpu.VMEM((15, 8, n), f32),
             pltpu.VMEM((rows, w), f32),
-            pltpu.VMEM((8, rows, 128), f32),
+            pltpu.VMEM((2, 2, rows, 128), f32),
+            pltpu.VMEM((2, rows, 128), f32),
+            pltpu.VMEM((2, rows, 128), f32),
+            pltpu.VMEM((2, rows, 128), f32),
+            pltpu.VMEM((2, rows, 128), f32),
             dma((6,)),
             dma((4,)),
             dma((4,)),
@@ -1347,8 +1367,8 @@
             dma((15,)),
             dma((1,)),
             dma((8,)),
+            dma((8,)),
             dma((1,)),
-            dma((2,)),
         ],
         compiler_params=pltpu.CompilerParams(collective_id=1, has_side_effects=True, vmem_limit_bytes=VMEM_LIMIT),
         cost_estimate=pl.CostEstimate(flops=60 * 1000000000, bytes_accessed=1000000, transcendentals=0),
@@ -2027,7 +2047,7 @@
     pull = scale * inv_own * inv_own * inv_own / D
     small_parts = (conv_sums, scan_sums, alog_grad * rate, dtp_grad, xproj_grad)
     if quick:
-        pulled, inner_grad, gain_sum, small_grad = run_finish(
+        pulled, inner_grad, gain_sum, *small_grads = run_finish(
             d_inner_proj, d_gate_proj, normed, raw, wi, wg, jnp.broadcast_to(gain_own[None], (8, width)), pull, small_parts
         )
         gain_grad = jnp.sum(gain_sum, axis=0)
@@ -2040,21 +2060,21 @@
         pulled = from_sequences((d_normed * gain_own - pull * fixed).astype(bf16))
         small_grad = send(jnp.concatenate(small_parts, axis=0), back(spread))
         small_grad = lax.psum_scatter(small_grad, ("row", "grp"), scatter_dimension=1, tiled=True)
+        small_grads = jnp.split(small_grad, [sum(SMALL_ROWS[: k + 1]) for k in range(len(SMALL_ROWS) - 1)], axis=0)
     input_grad = (cotangent.astype(f32) + pulled.astype(f32)).astype(bf16)
     in_grads = jnp.stack([inner_grad, gate_grad], axis=1)
-    rank_at = 16 + NSTATE
     return (
         output,
         input_grad,
         gain_grad,
         in_grads,
-        small_grad[0:4],
-        small_grad[4],
-        small_grad[rank_at + RANK :].T,
-        small_grad[rank_at : rank_at + RANK],
-        small_grad[8],
-        small_grad[16 : 16 + NSTATE],
-        small_grad[9],
+        small_grads[0],
+        small_grads[1][0],
+        small_grads[8].T,
+        small_grads[7],
+        small_grads[3][0],
+        small_grads[6],
+        small_grads[4][0],
         out_grad,
     )
 

time: 546 us -> 529 us (0.969)
  Pallas kernels: 493 us -> 479 us
    pallas_call x1, Pallas kernels: 123 us -> 109 us  [run_finish(): pl.pallas_call(finish_kernel, in_specs=[ANY] * 6 + [vmem, vmem] + [ANY] *...]
where the time goes in v5:
time: 529 us; the launch traced here: 526 us
  Pallas kernels  479 us (91%)
  local copies, waits for them, and re-layouts  22 us (4%)
  other arithmetic  13.1 us (2%)
    pallas_call x1, Pallas kernels, run_backward(): pl.pallas_call(backward_kernel, grid=(NCH,), in_specs=[chunk_of(XW, at),...  126 us
    pallas_call x1, Pallas kernels, run_forward(): pl.pallas_call(forward, grid=(LAST + 1,), in_specs=[split_rows(width, zer...  110 us
    pallas_call x1, Pallas kernels, run_finish(): pl.pallas_call(finish_kernel, in_specs=[ANY] * 6 + [vmem, vmem] + [ANY] *...  109 us
    pallas_call x1, Pallas kernels, run_gather_start(): pl.pallas_call(gather_start, in_specs=[ANY] * 3, out_specs=[ANY] * 3, out...  61.7 us
    pallas_call x1, Pallas kernels, run_conv_backward_far(): pl.pallas_call(conv_backward_far, grid=(NCH,), in_specs=[rows_of(w, at),...  28.1 us
    pallas_call x1, Pallas kernels, call(): pl.pallas_call(body, grid=(chunks,), in_specs=in_specs, out_specs=out_spe...  22.4 us
    pallas_call x1, Pallas kernels, run_late_parts(): pl.pallas_call(late_parts, grid_spec=pltpu.PrefetchScalarGridSpec(num_sca...  21.3 us
  transfers between devices with their start and end apart: 3, of which 1 were waited for; matrix products, arithmetic and copies ran while one was open for 1% of the time, Pallas kernels for 0%

profile of v5, /device:TPU:14, one launch (start us, length us, event | category | flops | bytes accessed | tf_op | source)
XLA Modules:
  0.0 526.4 jit_solution(13048460819979940008)
XLA Ops:
  0.7 3.3 fusion.2
  4.0 0.0 copy-start.16
  4.0 0.0 copy-start.19
  4.1 0.0 copy-start.21
  4.1 1.2 copy_bitcast_fusion
  5.3 0.7 concatenate.15
  6.1 0.6 pad.8.small
  6.7 61.7 %shard_map.220 = (bf16[2,1152,1024]{2,1,0:T(8,128)(2,1)}, bf16[8,1024,256]{2,1,0:T(8,128)(2,1)}, bf16[8,320,128]{2,1,0:T(8,128)(2,1)}) custom-call(bf16[576,1024]{1,0:T(8,128)(2,1)} %tokens.1, bf16[1024,256]{1,0:T(8,128)(2,1)} %get-tuple-element.137.in_i, bf16[320,128]{1,0:T(8,128)(2,1)} %pad.8.small), custom_call_target="tpu_custom_call" | custom-call | tf_op jit(solution)/shard_map/pallas_call | solution.py:653
  68.4 0.8 slice_convert_fusion
  69.2 1.8 copy_bitcast_fusion.2.xproj_ref
  71.0 1.7 copy_bitcast_fusion.3.dtp_ref.refs_3_
  72.7 1.4 copy_bitcast_fusion.4.rate_ref.refs_5_
  74.1 0.7 slice_bitcast_fusion.4
  74.8 0.7 slice_bitcast_fusion.5
  75.6 0.6 fusion.3
  78.8 0.6 pad_convert_fusion.1.conv_ref
  79.4 0.6 pad_convert_fusion.vec_ref.refs_4_
  80.0 0.6 copy-done.11
  80.6 0.6 pad_maximum_fusion.1.gain_ref
  81.2 0.6 pad_add_fusion.order_ref
  81.8 0.6 broadcast_in_dim.26.mix_ref.refs_7_
  82.4 110.5 %shard_map.221 = (bf16[2,1152,1024]{2,1,0:T(8,128)(2,1)}, f32[1152,1]{1,0:T(8,128)}, f32[1152,1024]{1,0:T(8,128)}, bf16[1152,1024]{1,0:T(8,128)(2,1)}, bf16[1152...) custom-call(bf16[2,1152,1024]{2,1,0:T(8,128)(2,1)} %get-tuple-elemen, ...), custom_call_target="tpu_custom_call" | custom-call | flops 60000002048 | bytes 1000000 | tf_op jit(solution)/shard_map/pallas_call | solution.py:836
  192.9 22.4 %shard_map.222 = (bf16[1152,1024]{1,0:T(8,128)(2,1)}, f32[1152,1024]{1,0:T(8,128)}, bf16[1152,1024]{1,0:T(8,128)(2,1)}, f32[1152,1]{1,0:T(8,128)}, f32[1152,1024]{1,0:T(8,128)}, /*index=5*/bf16[1152,1024]{1,0:T(8,128)(2,1)}) custom-call(bf16[2,1152,1024]{2,1,0:T(8,128)(2,1)} %get-tuple-element.62.normed_ref.refs_2_, ...), custom_call_target="tpu_custom_call" | custom-call | flops 22000001024 | bytes 1000000 | tf_op jit(solution)/shard_map/pallas_call | solution.py:282
  215.3 21.3 %shard_map.223 = (bf16[2,2,1024,256]{3,2,1,0:T(8,128)(2,1)}, bf16[2,2,1024,256]{3,2,1,0:T(8,128)(2,1)}, f32[2,2,1024,256]{3,2,1,0:T(8,128)}, f32[2,2,1024,256]{3,2,1,0:T(8,128)}) custom-call(s32[4]{0:T(128)} %pad_add_fusion.order_ref, bf16[2,1152,1024]{2,1,0:T(8,128)(2,1)} %get-tuple-element.62.normed_ref.refs_2_, ...), custom_call_target="tpu_custom_call" | custom-call | flops 14000000000 | bytes 1000000 | tf_op jit(solution)/shard_map/pallas_call | solution.py:1401
  236.6 0.6 broadcast_in_dim.27.refs_8_.into_ref
  237.2 125.9 %shard_map.224 = (f32[9,160,128]{2,1,0:T(8,128)}, f32[1152,1024]{1,0:T(8,128)}, f32[16,1024]{1,0:T(8,128)}, f32[8,1024]{1,0:T(8,128)}, f32[128,1024]{1,0:T(8,128...) custom-call(f32[9,160,128]{2,1,0:T(8,128)} %get-tuple-element.60.refs_0_, ...), custom_call_target="tpu_custom_call" | custom-call | flops 120000004096 | bytes 1000000 | tf_op jit(solution)/shard_map/pallas_call | solution.py:1699
  363.2 28.1 %shard_map.225 = (bf16[1152,1024]{1,0:T(8,128)(2,1)}, f32[1152,1]{1,0:T(8,128)}, f32[8,1024]{1,0:T(8,128)}, f32[160,1024]{1,0:T(8,128)}) custom-call(f32[1152,1024]{1,0:T(8,128)} %get-tuple-element.79.inner_ref.halo_ref, f32[1152,1024]{1,0:T(8,128)} %get-tuple-element.79.inner_ref.halo_ref, f32[1152,1]{1,0:T(8,128)} %get-tuple-element.67.inv_ref.halo_inv_ref, ...), custom_call_target="tpu_custom_call" | custom-call | flops 20000000000 | bytes 1000000 | tf_op jit(solution)/shard_map/pallas_call | solution.py:1813
  391.3 1.3 add.52
  392.7 2.5 collective-permute-start.1
  395.2 1.5 collective-permute-start
  396.7 1.1 slice_bitcast_fusion
  397.8 1.5 add_convert_fusion.1
  399.3 1.5 fusion.1.refs_10_
  400.8 5.1 collective-permute-done
  405.9 0.8 fusion.refs_7_
  406.7 0.6 broadcast_in_dim.29.refs_6_
  407.3 108.6 %shard_map.226 = (bf16[576,1024]{1,0:T(8,128)(2,1)}, f32[1024,256]{1,0:T(8,128)}, f32[8,256]{1,0:T(8,128)}, f32[4,128]{1,0:T(4,128)}, f32[1,128]{1,0:T(1,128)}, ...) custom-call(bf16[1152,1024]{1,0:T(8,128)(2,1)} %get-tuple-element.83, ...), custom_call_target="tpu_custom_call" | custom-call | flops 60000002048 | bytes 1000000 | tf_op jit(solution)/shard_map/pallas_call | solution.py:1321
  516.0 1.4 pad_maximum_fusion
  517.3 2.9 copy.36
  520.4 1.5 add_convert_fusion
  521.8 0.6 reduce_sum.9
  522.4 0.6 copy.56
  523.0 0.5 copy.57
  523.5 0.6 copy.58
  524.2 0.6 copy.59
  524.8 0.5 copy.60
  525.3 0.6 copy.61
  525.9 0.5 copy.62
  (55 shorter events, 0.2 us)
Async XLA Ops:
  4.0 1.3 copy-start.10
  4.0 1.3 copy-start.13
  4.0 1.3 copy-start.16
  4.0 1.3 copy-start.19
  4.1 1.2 copy-start.20
  4.1 1.2 copy-start.21
  4.1 1.2 copy-start.22
  4.1 1.2 copy-start.23
  5.3 70.3 %copy-start.18 = (s32[2]{0:T(128)S(1)}, s32[2]{0:T(128)}, u32[]{:S(2)}) copy-start(s32[2]{0:T(128)} %param.24) | copy-start | bytes 28
  80.0 0.6 copy-start.11
  363.2 28.2 %copy-start.6 = (f32[1152,1]{1,0:T(8,128)S(1)}, f32[1152,1]{1,0:T(8,128)}, u32[]{:S(2)}) copy-start(f32[1152,1]{1,0:T(8,128)} %get-tuple-element.84) | copy-start | bytes 13828
  391.3 5.4 %copy-start.1 = (f32[2,1024,256]{2,1,0:T(8,128)S(1)}, f32[2,1024,256]{2,1,0:T(8,128)}, u32[]{:S(2)}) copy-start(f32[2,1024,256]{2,1,0:T(8,128)} %get-tuple-element.94) | copy-start | bytes 6291460
  392.7 5.2 copy-start
  392.7 5.2 copy-start.3
  392.7 13.2 %collective-permute-start.1 = (f32[576,1]{1,0:T(8,128)S(1)}, f32[576,1]{1,0:T(8,128)S(1)}, u32[]{:S(2)}, u32[]{:S(2)}) collective-permute-start(f32[576,1]{1,0:T(8,128)S(1)} %get-tuple-element.131), channel_id=1, source_target_pairs={{0,1},{1,0},{2,3},{3,2},{4,5},{5,4},{6,7},{7,6},{8,9},{9,8},{10,11... | collective-permute-start | bytes 6920 | tf_op jit(solution)/shard_map/ppermute | solution.py:1875
  395.2 10.7 %collective-permute-start.2 = (f32[576,1]{1,0:T(8,128)S(1)}, f32[576,1]{1,0:T(8,128)S(1)}, u32[]{:S(2)}, u32[]{:S(2)}) collective-permute-start(f32[576,1]{1,0:T(8,128)S(1)} %get-tuple-element.131), channel_id=1, source_target_pairs={{0,5},{1,4},{2,7},{3,6},{4,1},{5,0},{6,3},{7,2},{8,13},{9,12},{10,... | collective-permute-start | bytes 6920 | tf_op jit(solution)/shard_map/ppermute | solution.py:1875
  395.2 10.7 %collective-permute-start = (f32[576,1]{1,0:T(8,128)S(1)}, f32[576,1]{1,0:T(8,128)S(1)}, u32[]{:S(2)}, u32[]{:S(2)}) collective-permute-start(f32[576,1]{1,0:T(8,128)S(1)} %get-tuple-element.130), channel_id=1, source_target_pairs={{0,4},{1,5},{2,6},{3,7},{4,0},{5,1},{6,2},{7,3},{8,12},{9,13},{10,... | collective-permute-start | bytes 6920 | tf_op jit(solution)/shard_map/ppermute | solution.py:1875
  397.8 1.5 copy-start.8
  397.8 8.1 %copy-start.5 = (f32[1152,1]{1,0:T(8,128)S(1)}, f32[1152,1]{1,0:T(8,128)}, u32[]{:S(2)}) copy-start(f32[1152,1]{1,0:T(8,128)} %get-tuple-element.67.inv_ref.halo_inv_ref) | copy-start | bytes 13828
  397.8 8.9 %copy-start.12 = (f32[4,2,128]{2,1,0:T(2,128)S(1)}, f32[4,2,128]{2,1,0:T(2,128)}, u32[]{:S(2)}) copy-start(f32[4,2,128]{2,1,0:T(2,128)} %copy-done.11) | copy-start | bytes 12292
  517.3 3.0 copy-start.2
  517.3 3.0 copy-start.4
  520.3 1.6 copy-start.14
  520.3 2.1 copy-start.17
  520.3 2.7 copy-start.26
  520.3 3.2 copy-start.7
  520.3 3.9 copy-start.9
  520.3 4.5 copy-start.25
  520.3 5.0 copy-start.15
  520.3 5.6 %copy-start.24 = (f32[1,128]{1,0:T(1,128)S(1)}, f32[1,128]{1,0:T(1,128)}, u32[]{:S(2)}) copy-start(f32[1,128]{1,0:T(1,128)} %get-tuple-element.101) | copy-start | bytes 1540

commit v6 on v5

--- a/solution.py
+++ b/solution.py
@@ -1010,8 +1010,8 @@
 
 def finish(inner_hbm, gate_hbm, normed_hbm, raw_hbm, wi_hbm, wg_hbm, gain_in_ref, pull_ref, conv_hbm, scan_hbm, alog_hbm, dtp_hbm, xproj_hbm,
            dn_ref, grad_ref, gain_ref, small_refs,
-           inner, gate, normed, raw, wi, wg, cs, cr, pairs, xs, xr, fs, fr, ys, yr, zs, zr, own, fin, gs, gr, sv, kr, ks, kx, kf, kg,
-           loc, c_send, c_recv, x_send, x_recv, f_send, f_recv, y_send, y_recv, z_send, z_recv, b_send, b_recv, g_send, g_recv, s_send, s_recv, s_load):
+           inner, gate, normed, raw, wi, wg, cs, cr, pairs, xs, xr, fs, fr, fq, ys, yr, zs, zr, own, fin, gs, gr, sv, kr, ks, kx, kf, kg,
+           loc, c_send, c_recv, x_send, x_recv, f_send, f_recv, r_send, r_recv, y_send, y_recv, z_send, z_recv, b_send, b_recv, g_send, g_recv, s_send, s_recv, s_load):
     g, r, c = lax.axis_index("grp"), lax.axis_index("row"), lax.axis_index("col")
     x, core, s, p = g // 2, g % 2, c // 2, c % 2
     tall, width = raw.shape
@@ -1021,6 +1021,8 @@
     y_dev, z_dev = (g, 1 - r, c), (g, r, 2 * s + 1 - p)
     x_dev, core_dev = ((1 - x) * 2 + core, r, c), (2 * x + 1 - core, r, c)
     alone = q == c
+    passed = 2 * p + xor_bit(1 - r, s)
+    stays_here = passed == c
 
     loads = [
         pltpu.make_async_copy(normed_hbm, normed, loc.at[0]),
@@ -1088,8 +1090,14 @@
     def to_x(d):
         return remote(xs.at[d], xr.at[d], x_send.at[d], x_recv.at[d], x_dev)
 
-    def to_owner(d):
-        return remote(fs.at[d], fr.at[d], f_send.at[d], f_recv.at[d], (g, r if d == 0 else 1 - r, q))
+    def to_owner():
+        return remote(fs.at[0], fr.at[0], f_send.at[0], f_recv.at[0], (g, r, q))
+
+    def to_passer():
+        return remote(fs.at[1], fq, r_send.at[0], r_recv.at[0], y_dev)
+
+    def pass_owner():
+        return remote(fq, fr.at[1], f_send.at[1], f_recv.at[1], (g, r, passed))
 
     def grad_to_core(i):
         for d in range(2):
@@ -1173,9 +1181,9 @@
 
             @pl.when(jnp.logical_not(alone))
             def _():
-                to_owner(0).start()
+                to_owner().start()
         else:
-            to_owner(1).start()
+            to_passer().start()
     for d in range(2):
         small_core(1, d).wait_recv()
         small_x(d).wait_recv()
@@ -1197,6 +1205,16 @@
             own[h * part : (h + 1) * part, cols] = v
 
         normed_part(True, h, 0, store)
+
+    to_passer().wait_recv()
+
+    @pl.when(stays_here)
+    def _():
+        fr[1] = fq[...]
+
+    @pl.when(jnp.logical_not(stays_here))
+    def _():
+        pass_owner().start()
 
     loads[3].wait()
     for h in range(2):
@@ -1252,9 +1270,12 @@
 
     @pl.when(jnp.logical_not(alone))
     def _():
-        to_owner(0).wait_recv()
-
-    to_owner(1).wait_recv()
+        to_owner().wait_recv()
+
+    @pl.when(jnp.logical_not(stays_here))
+    def _():
+        pass_owner().wait_recv()
+
     grad_ref[...] = fr[0].astype(f32) + fr[1].astype(f32)
 
     pltpu.make_async_copy(gr, gr, g_recv.at[0]).wait()
@@ -1296,9 +1317,13 @@
 
     @pl.when(jnp.logical_not(alone))
     def _():
-        to_owner(0).wait_send()
-
-    to_owner(1).wait_send()
+        to_owner().wait_send()
+
+    @pl.when(jnp.logical_not(stays_here))
+    def _():
+        pass_owner().wait_send()
+
+    to_passer().wait_send()
 
 
 SMALL_ROWS = (KCONV, 1, 3, 1, 1, 6, NSTATE, RANK, XW)
@@ -1337,6 +1362,7 @@
             low(2, width, n),
             low(2, width, n),
             low(2, width, n),
+            low(width, n),
             low(3, part, width),
             low(3, part, width),
             low(3, part, width),
@@ -1358,6 +1384,8 @@
             dma((2,)),
             dma((2,)),
             dma((2,)),
+            dma((1,)),
+            dma((1,)),
             dma((3,)),
             dma((3,)),
             dma((3,)),
@@ -1426,7 +1454,8 @@
 X_STEP = (0, 1)
 OWNER_STEP = (2, 4)
 DONE_STEP = (8, 8)
-QUARTER_STEP = ((2, 3, 4, 5), (4, 5, 6, 7))
+QUARTER_STEP = ((2, 2, 3, 3), (4, 4, 5, 5))
+PASS_STEP = ((4, 4, 5, 5), (6, 6, 6, 6))
 
 
 def border_moves(tall):
@@ -1442,8 +1471,8 @@
 
 def backward(xdbl_ref, xconv_ref, dy_ref, dtp_ref, vec_ref, rate_ref, starts_ref, mix_ref, into_ref, sent_hbm, kept_hbm, own_hbm, oth_hbm,
              dxdbl_ref, dxc_ref, alog_ref, sums_ref, dtpg_ref, grad_ref, branch_ref,
-             first, first_s, first_r, part, ys, yr, zs, zr, cr, kp, xs, xr, fs, fr, out, own, oth, by_s, by, bz_s, bz, fin,
-             y_send, y_recv, z_send, z_recv, e_send, e_recv, c_send, c_recv, x_send, x_recv, f_send, f_recv,
+             first, first_s, first_r, part, ys, yr, zs, zr, cr, kp, xs, xr, fs, fr, fq, out, own, oth, by_s, by, bz_s, bz, fin,
+             y_send, y_recv, z_send, z_recv, e_send, e_recv, c_send, c_recv, x_send, x_recv, f_send, f_recv, r_send, r_recv,
              p_send, p_recv, q_send, q_recv, b_send, b_recv, load_k, load_o, stay, put, *scratch):
     i = pl.program_id(0)
     g, r, c = lax.axis_index("grp"), lax.axis_index("row"), lax.axis_index("col")
@@ -1451,6 +1480,8 @@
     q = 2 * p + xor_bit(r, s)
     tall = SEQ // 2
     alone = q == c
+    passed = 2 * p + xor_bit(1 - r, s)
+    stays_here = passed == c
     y_dev, z_dev, far_dev = (g, 1 - r, c), (g, r, 2 * s + 1 - p), (g, 1 - r, (c + 2) % 4)
     x_dev, core_dev = ((1 - x) * 2 + core, r, c), (2 * x + 1 - core, r, c)
     to_first = remote(first_s, first_r, e_send.at[0], e_recv.at[0], far_dev)
@@ -1470,13 +1501,18 @@
     def to_x(n):
         return remote(xs.at[n], xr.at[n], x_send.at[n], x_recv.at[n], x_dev)
 
-    def to_owner(n, d, at=None):
-        device = (g, r if d == 0 else 1 - r, q)
-        if at is None:
-            return remote(fs.at[n, d], fr.at[n, d], f_send.at[n, d], f_recv.at[n, d], device)
-        tall = fs.shape[2] // QUARTERS
-        rows = pl.ds(at * tall, tall)
-        return remote(fs.at[n, d, rows], fr.at[n, d, rows], f_send.at[n, d], f_recv.at[n, d], device)
+    def quarter(ref, at):
+        rows = ref.shape[0] // QUARTERS
+        return ref if at is None else ref.at[pl.ds(at * rows, rows)]
+
+    def to_owner(n, at=None):
+        return remote(quarter(fs.at[n, 0], at), quarter(fr.at[n, 0], at), f_send.at[n, 0], f_recv.at[n, 0], (g, r, q))
+
+    def to_passer(n):
+        return remote(fs.at[n, 1], fq.at[n], r_send.at[n], r_recv.at[n], y_dev)
+
+    def pass_owner(n, at=None):
+        return remote(quarter(fq.at[n], at), quarter(fr.at[n, 1], at), f_send.at[n, 1], f_recv.at[n, 1], (g, r, passed))
 
     def rows_at(mine, j):
         return pl.ds(pl.multiple_of((p if mine else 1 - p) * tall + j * PIECE, 16), PIECE)
@@ -1581,27 +1617,40 @@
             to_x(n).wait_recv()
             fs[n] = (kp[n] + cr[n, 1].astype(f32) + xr[n].astype(f32)).astype(bf16)
 
+            to_passer(n).start()
+
             @pl.when(alone)
             def _():
                 fr[n, 0] = fs[n, 0]
 
+        @pl.when(i == OWNER_STEP[n] + 2)
+        def _(n=n):
+            to_passer(n).wait_recv()
+
+            @pl.when(stays_here)
+            def _():
+                fr[n, 1] = fq[n]
+
         for k in range(QUARTERS):
 
-            @pl.when(i == QUARTER_STEP[n][k])
+            @pl.when(jnp.logical_not(alone) & (i == QUARTER_STEP[n][k]))
             def _(n=n, k=k):
-                @pl.when(jnp.logical_not(alone))
-                def _():
-                    to_owner(n, 0, k).start()
-
-                to_owner(n, 1, k).start()
+                to_owner(n, k).start()
+
+            @pl.when(jnp.logical_not(stays_here) & (i == PASS_STEP[n][k]))
+            def _(n=n, k=k):
+                pass_owner(n, k).start()
 
         @pl.when(i == DONE_STEP[n])
         def _(n=n):
             @pl.when(jnp.logical_not(alone))
             def _():
-                to_owner(n, 0).wait_recv()
-
-            to_owner(n, 1).wait_recv()
+                to_owner(n).wait_recv()
+
+            @pl.when(jnp.logical_not(stays_here))
+            def _():
+                pass_owner(n).wait_recv()
+
             out[n] = fr[n, 0].astype(f32) + fr[n, 1].astype(f32)
             pltpu.make_async_copy(out.at[n], grad_ref.at[n], put.at[n]).start()
 
@@ -1672,11 +1721,16 @@
                 to_core(n, j).wait_send()
             to_x(n).wait_send()
 
+            to_passer(n).wait_send()
+
             @pl.when(jnp.logical_not(alone))
             def _(n=n):
-                to_owner(n, 0).wait_send()
-
-            to_owner(n, 1).wait_send()
+                to_owner(n).wait_send()
+
+            @pl.when(jnp.logical_not(stays_here))
+            def _(n=n):
+                pass_owner(n).wait_send()
+
             pltpu.make_async_copy(out.at[n], grad_ref.at[n], put.at[n]).wait()
         for m in range(QUARTERS + 2):
             branch_y(m).wait_send()
@@ -1736,6 +1790,7 @@
             low(2, 2, tall, n),
             low(2, 2, tall, n),
             low(2, 2, tall, n),
+            low(2, tall, n),
             pltpu.VMEM((2, tall, n), f32),
             pltpu.VMEM((SEQ, width), f32),
             low(2 * PIECE, width),
@@ -1756,6 +1811,8 @@
             dma((2,)),
             dma((2, 2)),
             dma((2, 2)),
+            dma((2,)),
+            dma((2,)),
             dma((QUARTERS + 2,)),
             dma((QUARTERS + 2,)),
             dma((QUARTERS + 2,)),

time: 529 us -> 502 us (0.949)
  Pallas kernels: 479 us -> 452 us
    pallas_call x1, Pallas kernels: 109 us -> 94.1 us  [run_finish(): pl.pallas_call(finish_kernel, in_specs=[ANY] * 6 + [vmem, vmem] + [ANY] *...]
    pallas_call x1, Pallas kernels: 126 us -> 117 us  [run_backward(): pl.pallas_call(backward_kernel, grid=(NCH,), in_specs=[chunk_of(XW, at),...]
where the time goes in v6:
time: 502 us; the launch traced here: 499 us
  Pallas kernels  452 us (90%)
  local copies, waits for them, and re-layouts  22 us (4%)
  other arithmetic  13.1 us (3%)
    pallas_call x1, Pallas kernels, run_backward(): pl.pallas_call(backward_kernel, grid=(NCH,), in_specs=[chunk_of(XW, at),...  117 us
    pallas_call x1, Pallas kernels, run_forward(): pl.pallas_call(forward, grid=(LAST + 1,), in_specs=[split_rows(width, zer...  110 us
    pallas_call x1, Pallas kernels, run_finish(): pl.pallas_call(finish_kernel, in_specs=[ANY] * 6 + [vmem, vmem] + [ANY] *...  94.1 us
    pallas_call x1, Pallas kernels, run_gather_start(): pl.pallas_call(gather_start, in_specs=[ANY] * 3, out_specs=[ANY] * 3, out...  61.7 us
    pallas_call x1, Pallas kernels, run_conv_backward_far(): pl.pallas_call(conv_backward_far, grid=(NCH,), in_specs=[rows_of(w, at),...  24.5 us
    pallas_call x1, Pallas kernels, call(): pl.pallas_call(body, grid=(chunks,), in_specs=in_specs, out_specs=out_spe...  22.4 us
    pallas_call x1, Pallas kernels, run_late_parts(): pl.pallas_call(late_parts, grid_spec=pltpu.PrefetchScalarGridSpec(num_sca...  21.3 us
  transfers between devices with their start and end apart: 3, of which 1 were waited for; matrix products, arithmetic and copies ran while one was open for 1% of the time, Pallas kernels for 0%

profile of v6, /device:TPU:14, one launch (start us, length us, event | category | flops | bytes accessed | tf_op | source)
XLA Modules:
  0.0 498.9 jit_solution(645066563564906492)
XLA Ops:
  0.7 3.3 fusion.2
  4.0 0.0 copy-start.13
  4.0 0.0 copy-start.16
  4.1 1.2 copy_bitcast_fusion
  5.3 0.7 concatenate.15
  6.1 0.6 pad.8.small
  6.7 61.7 %shard_map.220 = (bf16[2,1152,1024]{2,1,0:T(8,128)(2,1)}, bf16[8,1024,256]{2,1,0:T(8,128)(2,1)}, bf16[8,320,128]{2,1,0:T(8,128)(2,1)}) custom-call(bf16[576,1024]{1,0:T(8,128)(2,1)} %tokens.1, bf16[1024,256]{1,0:T(8,128)(2,1)} %get-tuple-element.137.in_i, bf16[320,128]{1,0:T(8,128)(2,1)} %pad.8.small), custom_call_target="tpu_custom_call" | custom-call | tf_op jit(solution)/shard_map/pallas_call | solution.py:653
  68.4 0.8 slice_convert_fusion
  69.2 1.8 copy_bitcast_fusion.2.xproj_ref
  71.0 1.7 copy_bitcast_fusion.3.dtp_ref.refs_3_
  72.7 1.4 copy_bitcast_fusion.4.rate_ref.refs_5_
  74.1 0.7 slice_bitcast_fusion.4
  74.8 0.7 slice_bitcast_fusion.5
  75.6 0.6 fusion.3
  78.8 0.6 pad_convert_fusion.1.conv_ref
  79.4 0.6 pad_convert_fusion.vec_ref.refs_4_
  80.0 0.6 copy-done.11
  80.6 0.6 pad_maximum_fusion.1.gain_ref
  81.2 0.6 pad_add_fusion.order_ref
  81.8 0.6 broadcast_in_dim.26.mix_ref.refs_7_
  82.4 110.5 %shard_map.221 = (bf16[2,1152,1024]{2,1,0:T(8,128)(2,1)}, f32[1152,1]{1,0:T(8,128)}, f32[1152,1024]{1,0:T(8,128)}, bf16[1152,1024]{1,0:T(8,128)(2,1)}, bf16[1152...) custom-call(bf16[2,1152,1024]{2,1,0:T(8,128)(2,1)} %get-tuple-elemen, ...), custom_call_target="tpu_custom_call" | custom-call | flops 60000002048 | bytes 1000000 | tf_op jit(solution)/shard_map/pallas_call | solution.py:836
  192.9 22.4 %shard_map.222 = (bf16[1152,1024]{1,0:T(8,128)(2,1)}, f32[1152,1024]{1,0:T(8,128)}, bf16[1152,1024]{1,0:T(8,128)(2,1)}, f32[1152,1]{1,0:T(8,128)}, f32[1152,1024]{1,0:T(8,128)}, /*index=5*/bf16[1152,1024]{1,0:T(8,128)(2,1)}) custom-call(bf16[2,1152,1024]{2,1,0:T(8,128)(2,1)} %get-tuple-element.62.normed_ref.refs_2_, ...), custom_call_target="tpu_custom_call" | custom-call | flops 22000001024 | bytes 1000000 | tf_op jit(solution)/shard_map/pallas_call | solution.py:282
  215.3 21.3 %shard_map.223 = (bf16[2,2,1024,256]{3,2,1,0:T(8,128)(2,1)}, bf16[2,2,1024,256]{3,2,1,0:T(8,128)(2,1)}, f32[2,2,1024,256]{3,2,1,0:T(8,128)}, f32[2,2,1024,256]{3,2,1,0:T(8,128)}) custom-call(s32[4]{0:T(128)} %pad_add_fusion.order_ref, bf16[2,1152,1024]{2,1,0:T(8,128)(2,1)} %get-tuple-element.62.normed_ref.refs_2_, ...), custom_call_target="tpu_custom_call" | custom-call | flops 14000000000 | bytes 1000000 | tf_op jit(solution)/shard_map/pallas_call | solution.py:1429
  236.6 0.6 broadcast_in_dim.27.refs_8_.into_ref
  237.2 117.3 %shard_map.224 = (f32[9,160,128]{2,1,0:T(8,128)}, f32[1152,1024]{1,0:T(8,128)}, f32[16,1024]{1,0:T(8,128)}, f32[8,1024]{1,0:T(8,128)}, f32[128,1024]{1,0:T(8,128...) custom-call(f32[9,160,128]{2,1,0:T(8,128)} %get-tuple-element.60.refs_0_, ...), custom_call_target="tpu_custom_call" | custom-call | flops 120000004096 | bytes 1000000 | tf_op jit(solution)/shard_map/pallas_call | solution.py:1753
  354.6 24.5 %shard_map.225 = (bf16[1152,1024]{1,0:T(8,128)(2,1)}, f32[1152,1]{1,0:T(8,128)}, f32[8,1024]{1,0:T(8,128)}, f32[160,1024]{1,0:T(8,128)}) custom-call(f32[1152,1024]{1,0:T(8,128)} %get-tuple-element.79.inner_ref.halo_ref, f32[1152,1024]{1,0:T(8,128)} %get-tuple-element.79.inner_ref.halo_ref, f32[1152,1]{1,0:T(8,128)} %get-tuple-element.67.inv_ref.halo_inv_ref, ...), custom_call_target="tpu_custom_call" | custom-call | flops 20000000000 | bytes 1000000 | tf_op jit(solution)/shard_map/pallas_call | solution.py:1870
  379.1 1.3 add.52
  380.5 2.1 collective-permute-start.1
  382.6 0.2 collective-permute-start.2
  382.7 1.4 collective-permute-start
  384.1 1.1 slice_bitcast_fusion
  385.2 1.5 add_convert_fusion.1
  386.7 1.5 fusion.1.refs_10_
  388.2 4.7 collective-permute-done
  392.9 0.8 fusion.refs_7_
  393.7 0.6 broadcast_in_dim.29.refs_6_
  394.3 94.1 %shard_map.226 = (bf16[576,1024]{1,0:T(8,128)(2,1)}, f32[1024,256]{1,0:T(8,128)}, f32[8,256]{1,0:T(8,128)}, f32[4,128]{1,0:T(4,128)}, f32[1,128]{1,0:T(1,128)}, ...) custom-call(bf16[1152,1024]{1,0:T(8,128)(2,1)} %get-tuple-element.83, ...), custom_call_target="tpu_custom_call" | custom-call | flops 60000002048 | bytes 1000000 | tf_op jit(solution)/shard_map/pallas_call | solution.py:1346
  488.4 1.4 pad_maximum_fusion
  489.8 2.9 copy.36
  492.8 1.5 add_convert_fusion
  494.3 0.6 reduce_sum.9
  494.9 0.6 copy.56
  495.4 0.5 copy.57
  496.0 0.6 copy.58
  496.6 0.6 copy.59
  497.2 0.5 copy.60
  497.7 0.6 copy.61
  498.3 0.5 copy.62
  (55 shorter events, 0.2 us)
Async XLA Ops:
  4.0 1.3 copy-start.10
  4.0 1.3 copy-start.13
  4.0 1.3 copy-start.16
  4.0 1.3 copy-start.19
  4.1 1.2 copy-start.20
  4.1 1.2 copy-start.21
  4.1 1.2 copy-start.22
  4.1 1.2 copy-start.23
  5.3 70.3 %copy-start.18 = (s32[2]{0:T(128)S(1)}, s32[2]{0:T(128)}, u32[]{:S(2)}) copy-start(s32[2]{0:T(128)} %param.24) | copy-start | bytes 28
  80.0 0.6 copy-start.11
  354.6 24.6 %copy-start.6 = (f32[1152,1]{1,0:T(8,128)S(1)}, f32[1152,1]{1,0:T(8,128)}, u32[]{:S(2)}) copy-start(f32[1152,1]{1,0:T(8,128)} %get-tuple-element.84) | copy-start | bytes 13828
  379.1 5.0 copy-start.1
  380.5 4.7 copy-start
  380.5 4.7 copy-start.3
  380.5 12.4 %collective-permute-start.1 = (f32[576,1]{1,0:T(8,128)S(1)}, f32[576,1]{1,0:T(8,128)S(1)}, u32[]{:S(2)}, u32[]{:S(2)}) collective-permute-start(f32[576,1]{1,0:T(8,128)S(1)} %get-tuple-element.131), channel_id=1, source_target_pairs={{0,1},{1,0},{2,3},{3,2},{4,5},{5,4},{6,7},{7,6},{8,9},{9,8},{10,11... | collective-permute-start | bytes 6920 | tf_op jit(solution)/shard_map/ppermute | solution.py:1932
  382.6 10.3 %collective-permute-start.2 = (f32[576,1]{1,0:T(8,128)S(1)}, f32[576,1]{1,0:T(8,128)S(1)}, u32[]{:S(2)}, u32[]{:S(2)}) collective-permute-start(f32[576,1]{1,0:T(8,128)S(1)} %get-tuple-element.131), channel_id=1, source_target_pairs={{0,5},{1,4},{2,7},{3,6},{4,1},{5,0},{6,3},{7,2},{8,13},{9,12},{10,... | collective-permute-start | bytes 6920 | tf_op jit(solution)/shard_map/ppermute | solution.py:1932
  382.7 10.1 %collective-permute-start = (f32[576,1]{1,0:T(8,128)S(1)}, f32[576,1]{1,0:T(8,128)S(1)}, u32[]{:S(2)}, u32[]{:S(2)}) collective-permute-start(f32[576,1]{1,0:T(8,128)S(1)} %get-tuple-element.130), channel_id=1, source_target_pairs={{0,4},{1,5},{2,6},{3,7},{4,0},{5,1},{6,2},{7,3},{8,12},{9,13},{10,... | collective-permute-start | bytes 6920 | tf_op jit(solution)/shard_map/ppermute | solution.py:1932
  385.2 1.5 copy-start.8
  385.2 7.7 %copy-start.5 = (f32[1152,1]{1,0:T(8,128)S(1)}, f32[1152,1]{1,0:T(8,128)}, u32[]{:S(2)}) copy-start(f32[1152,1]{1,0:T(8,128)} %get-tuple-element.67.inv_ref.halo_inv_ref) | copy-start | bytes 13828
  385.2 8.5 %copy-start.12 = (f32[4,2,128]{2,1,0:T(2,128)S(1)}, f32[4,2,128]{2,1,0:T(2,128)}, u32[]{:S(2)}) copy-start(f32[4,2,128]{2,1,0:T(2,128)} %copy-done.11) | copy-start | bytes 12292
  489.8 3.0 copy-start.2
  489.8 3.0 copy-start.4
  492.7 1.6 copy-start.14
  492.7 2.1 copy-start.17
  492.7 2.7 copy-start.26
  492.7 3.2 copy-start.7
  492.7 3.9 copy-start.9
  492.7 4.5 copy-start.25
  492.8 5.0 %copy-start.15 = (f32[16,128]{1,0:T(8,128)S(1)}, f32[16,128]{1,0:T(8,128)}, u32[]{:S(2)}) copy-start(f32[16,128]{1,0:T(8,128)} %get-tuple-element.159) | copy-start | bytes 24580
  492.8 5.6 %copy-start.24 = (f32[1,128]{1,0:T(1,128)S(1)}, f32[1,128]{1,0:T(1,128)}, u32[]{:S(2)}) copy-start(f32[1,128]{1,0:T(1,128)} %get-tuple-element.101) | copy-start | bytes 1540

commit v7 on v6

--- a/solution.py
+++ b/solution.py
@@ -1470,7 +1470,7 @@
 
 
 def backward(xdbl_ref, xconv_ref, dy_ref, dtp_ref, vec_ref, rate_ref, starts_ref, mix_ref, into_ref, sent_hbm, kept_hbm, own_hbm, oth_hbm,
-             dxdbl_ref, dxc_ref, alog_ref, sums_ref, dtpg_ref, grad_ref, branch_ref,
+             dxdbl_ref, dxc_ref, alog_ref, sums_ref, dtpg_ref, grad_refs, branch_ref,
              first, first_s, first_r, part, ys, yr, zs, zr, cr, kp, xs, xr, fs, fr, fq, out, own, oth, by_s, by, bz_s, bz, fin,
              y_send, y_recv, z_send, z_recv, e_send, e_recv, c_send, c_recv, x_send, x_recv, f_send, f_recv, r_send, r_recv,
              p_send, p_recv, q_send, q_recv, b_send, b_recv, load_k, load_o, stay, put, *scratch):
@@ -1652,7 +1652,7 @@
                 pass_owner(n).wait_recv()
 
             out[n] = fr[n, 0].astype(f32) + fr[n, 1].astype(f32)
-            pltpu.make_async_copy(out.at[n], grad_ref.at[n], put.at[n]).start()
+            pltpu.make_async_copy(out.at[n], grad_refs[n], put.at[n]).start()
 
     for j in range(QUARTERS):
 
@@ -1697,6 +1697,7 @@
     to_y(i).start()
     @pl.when(i == NCH - 1)
     def _():
+        alog_ref[...] = alog_ref[...] * rate_ref[...]
         for k in range(NCH - SUM_LAG, NCH):
             pass_on(k)
         for k in range(NCH):
@@ -1731,14 +1732,14 @@
             def _(n=n):
                 pass_owner(n).wait_send()
 
-            pltpu.make_async_copy(out.at[n], grad_ref.at[n], put.at[n]).wait()
+            pltpu.make_async_copy(out.at[n], grad_refs[n], put.at[n]).wait()
         for m in range(QUARTERS + 2):
             branch_y(m).wait_send()
             branch_z(m).wait_send()
 
 
 def backward_kernel(*refs):
-    backward(*refs[:9], refs[9:11], refs[11:13], *refs[13:])
+    backward(*refs[:9], refs[9:11], refs[11:13], *refs[13:20], refs[20:22], *refs[22:])
 
 
 def run_backward(xdbl, xconv, dy, dtp, vec, rate, starts, mix, into, sent, kept, own, oth):
@@ -1765,14 +1766,15 @@
             whole(8, w),
         ]
         + [ANY] * 6,
-        out_specs=(whole(NCH, XW, CH), rows_of(w, at), whole(NSTATE, w), whole(8, w), whole(RANK, w), ANY, ANY),
+        out_specs=(whole(NCH, XW, CH), rows_of(w, at), whole(NSTATE, w), whole(8, w), whole(RANK, w), ANY, ANY, ANY),
         out_shape=(
             shaped(NCH, XW, CH),
             shaped(SEQ, w),
             shaped(NSTATE, w),
             shaped(8, w),
             shaped(RANK, w),
-            shaped(2, tall, n),
+            shaped(tall, n),
+            shaped(tall, n),
             shaped(SEQ // 2, width, dtype=bf16),
         ),
         scratch_shapes=[
@@ -2062,10 +2064,9 @@
         gate_sent, out_sent, gate_kept, out_kept = run_late_parts(order, normed, d_gate_proj, gated, cot)
         sent, kept = (gate_sent, out_sent), (gate_kept, out_kept)
         into = jnp.broadcast_to(resumed_by_other.astype(f32), (8, w))
-        dxdbl, dxc, alog_grad, scan_sums, dtp_grad, late_grads, branch = run_backward(
+        dxdbl, dxc, alog_grad, scan_sums, dtp_grad, gate_grad, out_grad, branch = run_backward(
             xdbl, xconv, d_yfull, dtp, vec, rate, starts, mix, into, sent, kept, branch_own, branch_oth
         )
-        gate_grad, out_grad = late_grads[0], late_grads[1]
     else:
         branch = from_sequences(scatter_quad(branch_own, branch_oth).astype(bf16))
         out_grad = collect([scatter_grp(dot_tn(gated, cot[d]), 1) for d in range(2)])
@@ -2076,6 +2077,7 @@
         g_into = jnp.where(resumes_own, g_first, 0.0) + jnp.where(resumed_by_other, across(g_first), 0.0)
         dx_p, dxc, *sums, _ = scan(0, PC, carry=g_into, sums=sums, kept=(dxc,))
         alog_grad, scan_sums, dtp_grad = sums
+        alog_grad = alog_grad * rate
         dxdbl = jnp.concatenate([dx_p, dx_c], axis=1)
         for move in (swap, pair):
             dxdbl = dxdbl + move(dxdbl)
@@ -2102,10 +2104,10 @@
     scale = own_rows(scale) + swap(own_rows(scale)) + pair(pair_rows(scale)) + diagonal
     inv_own = own_rows(inv)
     pull = scale * inv_own * inv_own * inv_own / D
-    small_parts = (conv_sums, scan_sums, alog_grad * rate, dtp_grad, xproj_grad)
+    small_parts = (conv_sums, scan_sums, alog_grad, dtp_grad, xproj_grad)
     if quick:
         pulled, inner_grad, gain_sum, *small_grads = run_finish(
-            d_inner_proj, d_gate_proj, normed, raw, wi, wg, jnp.broadcast_to(gain_own[None], (8, width)), pull, small_parts
+            d_inner_proj, d_gate_proj, normed, raw, wi, wg, gain_two, pull, small_parts
         )
         gain_grad = jnp.sum(gain_sum, axis=0)
     else:

time: 502 us -> 502 us (level)
  transfers between devices with their start and end apart: 3 -> 3, of which waited for: 1 -> 1; matrix products, arithmetic and copies ran while one was open for 1% -> 0% of each run, Pallas kernels for 0% -> 0%
where the time goes in v7:
time: 502 us; the launch traced here: 499 us
  Pallas kernels  453 us (90%)
  local copies, waits for them, and re-layouts  21.3 us (4%)
  other arithmetic  11.9 us (2%)
  waiting for transfers between devices  6.02 us (1%)
    pallas_call x1, Pallas kernels, run_backward(): pl.pallas_call(backward_kernel, grid=(NCH,), in_specs=[chunk_of(XW, at),...  117 us
    pallas_call x1, Pallas kernels, run_forward(): pl.pallas_call(forward, grid=(LAST + 1,), in_specs=[split_rows(width, zer...  110 us
    pallas_call x1, Pallas kernels, run_finish(): pl.pallas_call(finish_kernel, in_specs=[ANY] * 6 + [vmem, vmem] + [ANY] *...  94.8 us
    pallas_call x1, Pallas kernels, run_gather_start(): pl.pallas_call(gather_start, in_specs=[ANY] * 3, out_specs=[ANY] * 3, out...  61.7 us
    pallas_call x1, Pallas kernels, run_conv_backward_far(): pl.pallas_call(conv_backward_far, grid=(NCH,), in_specs=[rows_of(w, at),...  24.5 us
    pallas_call x1, Pallas kernels, call(): pl.pallas_call(body, grid=(chunks,), in_specs=in_specs, out_specs=out_spe...  22.4 us
    pallas_call x1, Pallas kernels, run_late_parts(): pl.pallas_call(late_parts, grid_spec=pltpu.PrefetchScalarGridSpec(num_sca...  21.3 us
  transfers between devices with their start and end apart: 3, of which 1 were waited for; matrix products, arithmetic and copies ran while one was open for 0% of the time, Pallas kernels for 0%

profile of v7, /device:TPU:14, one launch (start us, length us, event | category | flops | bytes accessed | tf_op | source)
XLA Modules:
  0.0 498.9 jit_solution(5783583454200698060)
XLA Ops:
  0.8 1.3 fusion.2
  4.7 3.4 fusion.1
  8.1 0.7 concatenate.15
  8.8 0.6 pad.8.small
  9.5 1.1 copy_bitcast_fusion
  10.6 61.7 %shard_map.220 = (bf16[2,1152,1024]{2,1,0:T(8,128)(2,1)}, bf16[8,1024,256]{2,1,0:T(8,128)(2,1)}, bf16[8,320,128]{2,1,0:T(8,128)(2,1)}) custom-call(bf16[576,1024]{1,0:T(8,128)(2,1)} %tokens.1, bf16[1024,256]{1,0:T(8,128)(2,1)} %get-tuple-element.137.in_i, bf16[320,128]{1,0:T(8,128)(2,1)} %pad.8.small), custom_call_target="tpu_custom_call" | custom-call | tf_op jit(solution)/shard_map/pallas_call | solution.py:653
  72.3 0.8 slice_convert_fusion
  73.1 0.7 slice_bitcast_fusion.3
  73.8 0.7 slice_bitcast_fusion.2
  74.5 1.4 copy_bitcast_fusion.4.rate_ref.refs_5_
  76.0 1.7 copy_bitcast_fusion.3.dtp_ref.refs_3_
  77.7 1.8 copy_bitcast_fusion.2.xproj_ref
  79.5 0.6 pad_convert_fusion.1.conv_ref
  80.1 0.6 pad_convert_fusion.vec_ref.refs_4_
  80.7 0.6 pad_maximum_fusion.1.gain_ref.refs_6_
  81.3 0.6 pad_add_fusion.order_ref
  81.9 0.6 broadcast_in_dim.18.mix_ref.refs_7_
  82.5 110.4 %shard_map.221 = (bf16[2,1152,1024]{2,1,0:T(8,128)(2,1)}, f32[1152,1]{1,0:T(8,128)}, f32[1152,1024]{1,0:T(8,128)}, bf16[1152,1024]{1,0:T(8,128)(2,1)}, bf16[1152...) custom-call(bf16[2,1152,1024]{2,1,0:T(8,128)(2,1)} %get-tuple-elemen, ...), custom_call_target="tpu_custom_call" | custom-call | flops 60000002048 | bytes 1000000 | tf_op jit(solution)/shard_map/pallas_call | solution.py:836
  193.0 22.4 %shard_map.222 = (bf16[1152,1024]{1,0:T(8,128)(2,1)}, f32[1152,1024]{1,0:T(8,128)}, bf16[1152,1024]{1,0:T(8,128)(2,1)}, f32[1152,1]{1,0:T(8,128)}, f32[1152,1024]{1,0:T(8,128)}, /*index=5*/bf16[1152,1024]{1,0:T(8,128)(2,1)}) custom-call(bf16[2,1152,1024]{2,1,0:T(8,128)(2,1)} %get-tuple-element.63.normed_ref.refs_2_, ...), custom_call_target="tpu_custom_call" | custom-call | flops 22000001024 | bytes 1000000 | tf_op jit(solution)/shard_map/pallas_call | solution.py:282
  215.4 21.3 %shard_map.223 = (bf16[2,2,1024,256]{3,2,1,0:T(8,128)(2,1)}, bf16[2,2,1024,256]{3,2,1,0:T(8,128)(2,1)}, f32[2,2,1024,256]{3,2,1,0:T(8,128)}, f32[2,2,1024,256]{3,2,1,0:T(8,128)}) custom-call(s32[4]{0:T(128)} %pad_add_fusion.order_ref, bf16[2,1152,1024]{2,1,0:T(8,128)(2,1)} %get-tuple-element.63.normed_ref.refs_2_, ...), custom_call_target="tpu_custom_call" | custom-call | flops 14000000000 | bytes 1000000 | tf_op jit(solution)/shard_map/pallas_call | solution.py:1429
  236.7 0.6 broadcast_in_dim.19.refs_8_.into_ref
  237.3 117.3 %shard_map.224 = (f32[9,160,128]{2,1,0:T(8,128)}, f32[1152,1024]{1,0:T(8,128)}, f32[16,1024]{1,0:T(8,128)}, f32[8,1024]{1,0:T(8,128)}, f32[128,1024]{1,0:T(8,128...) custom-call(f32[9,160,128]{2,1,0:T(8,128)} %get-tuple-element.61.refs_0_, ...), custom_call_target="tpu_custom_call" | custom-call | flops 120000004096 | bytes 1000000 | tf_op jit(solution)/shard_map/pallas_call | solution.py:1754
  354.6 0.0 copy-start.7
  354.6 24.5 %shard_map.225 = (bf16[1152,1024]{1,0:T(8,128)(2,1)}, f32[1152,1]{1,0:T(8,128)}, f32[8,1024]{1,0:T(8,128)}, f32[160,1024]{1,0:T(8,128)}) custom-call(f32[1152,1024]{1,0:T(8,128)} %get-tuple-element.80.inner_ref.halo_ref, f32[1152,1024]{1,0:T(8,128)} %get-tuple-element.80.inner_ref.halo_ref, f32[1152,1]{1,0:T(8,128)} %get-tuple-element.68.inv_ref.halo_inv_ref, ...), custom_call_target="tpu_custom_call" | custom-call | flops 20000000000 | bytes 1000000 | tf_op jit(solution)/shard_map/pallas_call | solution.py:1872
  379.2 0.0 copy-start
  379.2 0.0 copy-start.2
  379.2 1.3 add.52
  380.6 2.2 collective-permute-start.2
  382.7 0.0 collective-permute-start.1
  382.7 1.4 collective-permute-start
  384.1 1.5 add_convert_fusion.1
  385.6 6.0 %collective-permute-done = f32[576,1]{1,0:T(8,128)S(1)} collective-permute-done((f32[576,1]{1,0:T(8,128)S(1)}, f32[576,1]{1,0:T(8,128)S(1)}, u32[]{:S(2)}, u32[]{:S(2)}) %collective-permute-start) | collective-permute-done | bytes 2336 | tf_op jit(solution)/shard_map/ppermute | solution.py:1934
  391.6 0.0 collective-permute-done.2
  391.6 0.0 collective-permute-done.1
  391.7 0.8 fusion.refs_7_
  392.5 94.8 %shard_map.226 = (bf16[576,1024]{1,0:T(8,128)(2,1)}, f32[1024,256]{1,0:T(8,128)}, f32[8,256]{1,0:T(8,128)}, f32[4,128]{1,0:T(4,128)}, f32[1,128]{1,0:T(1,128)}, ...) custom-call(bf16[1152,1024]{1,0:T(8,128)(2,1)} %get-tuple-element.84, ...), custom_call_target="tpu_custom_call" | custom-call | flops 60000002048 | bytes 1000000 | tf_op jit(solution)/shard_map/pallas_call | solution.py:1346
  487.3 2.9 add_convert_fusion
  490.2 0.1 pad_maximum_fusion
  490.4 2.9 copy.36
  493.4 0.6 reduce_sum.9
  493.9 0.6 copy.55
  494.5 0.5 copy.56
  495.0 0.6 copy.57
  495.7 0.6 copy.58
  496.3 0.5 copy.59
  496.8 0.6 copy.60
  497.4 0.5 copy.61
  497.9 1.0 copy.62
  (47 shorter events, 0.1 us)
Async XLA Ops:
  0.6 7.4 %copy-start.19 = (bf16[128]{0:T(256)(128)(2,1)S(1)}, bf16[128]{0:T(256)(128)(2,1)}, u32[]{:S(2)}) copy-start(bf16[128]{0:T(256)(128)(2,1)} %param.22) | copy-start | bytes 772
  0.7 7.4 %copy-start.14 = (bf16[16,128]{1,0:T(8,128)(2,1)S(1)}, bf16[16,128]{1,0:T(8,128)(2,1)}, u32[]{:S(2)}) copy-start(bf16[16,128]{1,0:T(8,128)(2,1)} %param.21) | copy-start | bytes 12292
  0.7 7.4 %copy-start.18 = (bf16[128]{0:T(256)(128)(2,1)S(1)}, bf16[128]{0:T(256)(128)(2,1)}, u32[]{:S(2)}) copy-start(bf16[128]{0:T(256)(128)(2,1)} %param.20) | copy-start | bytes 772
  0.7 7.4 %copy-start.11 = (bf16[128,128]{1,0:T(8,128)(2,1)S(1)}, bf16[128,128]{1,0:T(8,128)(2,1)}, u32[]{:S(2)}) copy-start(bf16[128,128]{1,0:T(8,128)(2,1)} %param.19) | copy-start | bytes 98308
  0.7 7.4 %copy-start.10 = (bf16[128,160]{0,1:T(8,128)(2,1)S(1)}, bf16[128,160]{0,1:T(8,128)(2,1)}, u32[]{:S(2)}) copy-start(bf16[128,160]{0,1:T(8,128)(2,1)} %param.18) | copy-start | bytes 122884
  0.7 7.4 %copy-start.17 = (bf16[128]{0:T(256)(128)(2,1)S(1)}, bf16[128]{0:T(256)(128)(2,1)}, u32[]{:S(2)}) copy-start(bf16[128]{0:T(256)(128)(2,1)} %param.17) | copy-start | bytes 772
  0.7 7.4 %copy-start.16 = (bf16[4,128]{1,0:T(4,128)(2,1)S(1)}, bf16[4,128]{1,0:T(4,128)(2,1)}, u32[]{:S(2)}) copy-start(bf16[4,128]{1,0:T(4,128)(2,1)} %param.16) | copy-start | bytes 3076
  0.7 7.4 %copy-start.20 = (bf16[256]{0:T(256)(128)(2,1)S(1)}, bf16[256]{0:T(256)(128)(2,1)}, u32[]{:S(2)}) copy-start(bf16[256]{0:T(256)(128)(2,1)} %param.14) | copy-start | bytes 1540
  354.6 24.6 %copy-start.7 = (f32[1152,1]{1,0:T(8,128)S(1)}, f32[1152,1]{1,0:T(8,128)}, u32[]{:S(2)}) copy-start(f32[1152,1]{1,0:T(8,128)} %get-tuple-element.85) | copy-start | bytes 13828
  379.2 4.9 copy-start
  379.2 4.9 copy-start.2
  380.5 11.1 %copy-start.6 = (f32[1152,1]{1,0:T(8,128)S(1)}, f32[1152,1]{1,0:T(8,128)}, u32[]{:S(2)}) copy-start(f32[1152,1]{1,0:T(8,128)} %get-tuple-element.68.inv_ref.halo_inv_ref) | copy-start | bytes 13828
  380.6 11.1 %collective-permute-start.2 = (f32[576,1]{1,0:T(8,128)S(1)}, f32[576,1]{1,0:T(8,128)S(1)}, u32[]{:S(2)}, u32[]{:S(2)}) collective-permute-start(f32[576,1]{1,0:T(8,128)S(1)} %get-tuple-element.131), channel_id=1, source_target_pairs={{0,5},{1,4},{2,7},{3,6},{4,1},{5,0},{6,3},{7,2},{8,13},{9,12},{10,... | collective-permute-start | bytes 6920 | tf_op jit(solution)/shard_map/ppermute | solution.py:1934
  382.7 8.9 %collective-permute-start.1 = (f32[576,1]{1,0:T(8,128)S(1)}, f32[576,1]{1,0:T(8,128)S(1)}, u32[]{:S(2)}, u32[]{:S(2)}) collective-permute-start(f32[576,1]{1,0:T(8,128)S(1)} %get-tuple-element.131), channel_id=1, source_target_pairs={{0,1},{1,0},{2,3},{3,2},{4,5},{5,4},{6,7},{7,6},{8,9},{9,8},{10,11... | collective-permute-start | bytes 6920 | tf_op jit(solution)/shard_map/ppermute | solution.py:1934
  382.7 8.9 %collective-permute-start = (f32[576,1]{1,0:T(8,128)S(1)}, f32[576,1]{1,0:T(8,128)S(1)}, u32[]{:S(2)}, u32[]{:S(2)}) collective-permute-start(f32[576,1]{1,0:T(8,128)S(1)} %get-tuple-element.130), channel_id=1, source_target_pairs={{0,4},{1,5},{2,6},{3,7},{4,0},{5,1},{6,2},{7,3},{8,12},{9,13},{10,... | collective-permute-start | bytes 6920 | tf_op jit(solution)/shard_map/ppermute | solution.py:1934
  392.5 94.8 %copy-start.1 = (bf16[576,1024]{1,0:T(8,128)(2,1)S(1)}, bf16[576,1024]{1,0:T(8,128)(2,1)}, u32[]{:S(2)}) copy-start(bf16[576,1024]{1,0:T(8,128)(2,1)} %cot_in.1) | copy-start | bytes 3538948
  487.3 2.9 copy-start.4
  487.3 2.9 copy-start.5
  490.3 3.0 copy-start.12
  490.3 3.6 copy-start.15
  490.4 4.2 copy-start.23
  490.4 4.7 copy-start.8
  490.4 5.3 %copy-start.9 = (f32[128,128]{1,0:T(8,128)S(1)}, f32[128,128]{1,0:T(8,128)}, u32[]{:S(2)}) copy-start(f32[128,128]{1,0:T(8,128)} %get-tuple-element.157) | copy-start | bytes 196612
  490.4 5.9 %copy-start.22 = (f32[1,128]{1,0:T(1,128)S(1)}, f32[1,128]{1,0:T(1,128)}, u32[]{:S(2)}) copy-start(f32[1,128]{1,0:T(1,128)} %get-tuple-element.100) | copy-start | bytes 1540
  490.4 6.4 %copy-start.13 = (f32[16,128]{1,0:T(8,128)S(1)}, f32[16,128]{1,0:T(8,128)}, u32[]{:S(2)}) copy-start(f32[16,128]{1,0:T(8,128)} %get-tuple-element.159) | copy-start | bytes 24580
  490.4 7.0 %copy-start.21 = (f32[1,128]{1,0:T(1,128)S(1)}, f32[1,128]{1,0:T(1,128)}, u32[]{:S(2)}) copy-start(f32[1,128]{1,0:T(1,128)} %get-tuple-element.102) | copy-start | bytes 1540
  490.4 7.5 %copy-start.3 = (f32[1024,256]{1,0:T(8,128)S(1)}, f32[1024,256]{1,0:T(8,128)}, u32[]{:S(2)}) copy-start(f32[1024,256]{1,0:T(8,128)} %get-tuple-element.161) | copy-start | bytes 3145732
